TPU v7x, 256 devices: a whole 4x4x8 slice. The times are simulated.
256 devices in a mesh: section: 2 (over z_lo), dp: 2 (over core), expert: 64 (over z_hi, x, y).
Axes of the slice: x: 4, y: 4, z: 8 (z_hi: 4, z_lo: 2; z = z_hi * 2 + z_lo), core: 2. Of those that a mesh axis runs over, the one named last changes fastest.
Arguments:
- grad_out: bfloat16 [2, 8192, 3584], P(None, ('dp', 'expert')), may hold values from -6 to 6
- layer_in: bfloat16 [2, 2, 8192, 3584], P('section', None, ('dp', 'expert')), may hold values from -6 to 6
- routes: int32 [2, 2, 8192, 2], P('section', None, ('dp', 'expert')), may hold values from 0 to 31, all different within a row; in each aligned block of 64 rows (0 to 63, 64 to 127, ..., all dimensions but the last counted through in order) at most 5 rows name the same one
- gates: float32 [2, 2, 8192, 2], P('section', None, ('dp', 'expert')), may hold values from 0.05 to 0.5
- w_up: bfloat16 [2, 64, 3584, 512], P('section', 'expert', 'dp'), may hold values from -0.09375 to 0.09375
- w_down: bfloat16 [2, 64, 512, 3584], P('section', 'expert', None, 'dp'), may hold values from -0.1875 to 0.1875
Outputs:
- grad_in: bfloat16 [2, 2, 8192, 3584], P('section', None, ('dp', 'expert'))
- grad_up: bfloat16 [2, 64, 3584, 512], P('section', 'expert', 'dp')
- grad_down: bfloat16 [2, 64, 512, 3584], P('section', 'expert', None, 'dp')
Inputs may be any that keep to these rules, and one draw needn't show every extreme that they name: `routes`: each token names 2 different experts. In each device's block of 64 tokens of one section and micro-batch no expert is named by more than 5 tokens, a bound that some block reaches.
All inputs are finite; a program needn't handle non-finite values.
Results may differ from a plain program's by a relative error of at most 0.0075.
Values may be sent and summed in bfloat16 or wider, within the bound.
No kernel may reach another device: no remote copies, remote signals or barrier semaphores. Data moves between devices by JAX's collectives and lax.ppermute only.
A program may use at most 128 MiB of HBM per device.

v0:
```python
import jax
import jax.numpy as jnp
from jax import lax
from jax.sharding import PartitionSpec as P


def from_behind(value, axis, steps):
    count = lax.axis_size(axis)
    first, last = (max(0, -steps), min(count, count - steps))
    return lax.ppermute(value, axis, [(source, source + steps) for source in range(first, last)])


def silu_grad(preact):
    sigmoid_value = jax.nn.sigmoid(preact)
    return sigmoid_value * (1.0 + preact * (1.0 - sigmoid_value))


def on_device(grad_out, layer_in, routes, gates, w_up, w_down):
    section_count = lax.axis_size("section")
    section_here = lax.axis_index("section")
    experts = lax.axis_size("expert") // 2
    micro_count = grad_out.shape[0]
    tok_rows = grad_out.shape[1]
    model_width = grad_out.shape[2]
    top_count = routes.shape[3]
    capacity = max(2, 5 * tok_rows * top_count // (4 * experts))
    up_full, down_full = (
        lax.all_gather(w_up, "dp", axis=2, tiled=True),
        lax.all_gather(w_down, "dp", axis=3, tiled=True),
    )
    up_matrix = up_full[0, 0]
    down_matrix = down_full[0, 0]
    expert_ids = jnp.arange(experts, dtype=jnp.int32)
    slot_ids = jnp.arange(capacity, dtype=jnp.int32)
    row_total = 2 * experts * capacity
    kept_inputs = []
    kept_scaled = []
    kept_active = []
    kept_grads = []
    results = jnp.zeros((micro_count, tok_rows, model_width), jnp.bfloat16)
    passed = jnp.zeros((tok_rows, model_width), jnp.bfloat16)
    tick_count = micro_count + section_count - 1
    for tick_index in range(tick_count):
        micro_now = tick_index - (section_count - 1 - section_here)
        active = (micro_now >= 0) & (micro_now < micro_count)
        chosen = jnp.clip(micro_now, 0, micro_count - 1)
        top_grad = lax.dynamic_index_in_dim(grad_out, chosen, 0, keepdims=False)
        incoming = jnp.where(section_here == section_count - 1, top_grad, passed)
        inputs_now = lax.dynamic_index_in_dim(layer_in[0], chosen, 0, keepdims=False)
        routes_now = lax.dynamic_index_in_dim(routes[0], chosen, 0, keepdims=False)
        gates_now = lax.dynamic_index_in_dim(gates[0], chosen, 0, keepdims=False)
        scaled = (gates_now[:, :, None] * incoming[:, None, :].astype(jnp.float32)).astype(
            jnp.bfloat16
        )
        onehot = (routes_now[:, :, None] == expert_ids).astype(jnp.int32)
        flat_hits = onehot.reshape(tok_rows * top_count, experts)
        before = jnp.cumsum(flat_hits, axis=0) - flat_hits
        position = jnp.sum(before * flat_hits, axis=1).reshape(tok_rows, top_count)
        placement = (
            (onehot[:, :, :, None] == 1) & (position[:, :, None, None] == slot_ids)
        ).astype(jnp.bfloat16)
        inputs_slots = jnp.einsum(
            "tjec,td->ecd", placement, inputs_now, preferred_element_type=jnp.float32
        ).astype(jnp.bfloat16)
        scaled_slots = jnp.einsum(
            "tjec,tjd->ecd", placement, scaled, preferred_element_type=jnp.float32
        ).astype(jnp.bfloat16)
        doubled_inputs = jnp.repeat(inputs_slots, 2, axis=0)
        doubled_scaled = jnp.repeat(scaled_slots, 2, axis=0)
        got_inputs, got_scaled = (
            lax.all_to_all(doubled_inputs, "expert", split_axis=0, concat_axis=0, tiled=True),
            lax.all_to_all(doubled_scaled, "expert", split_axis=0, concat_axis=0, tiled=True),
        )
        row_inputs = got_inputs.reshape(row_total, model_width)
        row_scaled = got_scaled.reshape(row_total, model_width)
        pre_act = jnp.dot(row_inputs, up_matrix, preferred_element_type=jnp.float32)
        activated = jax.nn.silu(pre_act).astype(jnp.bfloat16)
        grad_act = jnp.dot(row_scaled, down_matrix.T, preferred_element_type=jnp.float32)
        grad_pre = (grad_act * silu_grad(pre_act)).astype(jnp.bfloat16)
        partial_rows = jnp.dot(grad_pre, up_matrix.T, preferred_element_type=jnp.float32).astype(
            jnp.bfloat16
        )
        partial_rows, activated, grad_pre = (partial_rows, activated, grad_pre)
        returned = lax.all_to_all(
            partial_rows.reshape(2 * experts, capacity, model_width),
            "expert",
            split_axis=0,
            concat_axis=0,
            tiled=True,
        )
        combined = jnp.sum(
            returned.reshape(experts, 2, capacity, model_width).astype(jnp.float32), axis=1
        ).astype(jnp.bfloat16)
        returned_sum = jnp.einsum(
            "tjec,ecd->td", placement, combined, preferred_element_type=jnp.float32
        )
        kept_inputs.append(row_inputs)
        kept_scaled.append(row_scaled)
        kept_active.append(jnp.where(active, activated, jnp.zeros_like(activated)))
        kept_grads.append(jnp.where(active, grad_pre, jnp.zeros_like(grad_pre)))
        produced = (incoming.astype(jnp.float32) + returned_sum).astype(jnp.bfloat16)
        current = lax.dynamic_index_in_dim(results, chosen, 0, keepdims=False)
        results = lax.dynamic_update_index_in_dim(
            results, jnp.where(active, produced, current), chosen, 0
        )
        if tick_index + 1 < tick_count:
            passed = from_behind(produced, "section", -1)
    all_inputs = jnp.concatenate(kept_inputs, axis=0)
    all_scaled = jnp.concatenate(kept_scaled, axis=0)
    all_active = jnp.concatenate(kept_active, axis=0)
    all_grads = jnp.concatenate(kept_grads, axis=0)
    total_up = lax.dot_general(
        all_inputs, all_grads, (((0,), (0,)), ((), ())), preferred_element_type=jnp.float32
    )
    total_down = lax.dot_general(
        all_active, all_scaled, (((0,), (0,)), ((), ())), preferred_element_type=jnp.float32
    )
    upper_sum, lower_sum = (
        lax.psum_scatter(
            total_up.astype(jnp.bfloat16), "dp", scatter_dimension=0, tiled=True
        ).astype(jnp.float32),
        lax.psum_scatter(
            total_down.astype(jnp.bfloat16), "dp", scatter_dimension=1, tiled=True
        ).astype(jnp.float32),
    )
    return (
        results[None],
        upper_sum.astype(jnp.bfloat16)[None, None],
        lower_sum.astype(jnp.bfloat16)[None, None],
    )


def solution(mesh):
    in_specs = (
        P(None, ("dp", "expert"), None),
        P("section", None, ("dp", "expert"), None),
        P("section", None, ("dp", "expert"), None),
        P("section", None, ("dp", "expert"), None),
        P("section", "expert", "dp", None),
        P("section", "expert", None, "dp"),
    )
    out_specs = (
        P("section", None, ("dp", "expert"), None),
        P("section", "expert", "dp", None),
        P("section", "expert", None, "dp"),
    )
    return jax.shard_map(
        on_device, mesh=mesh, in_specs=in_specs, out_specs=out_specs, check_vma=False
    )
```

profile of v0, /device:TPU:1, one launch (start us, length us, event | category | flops | bytes accessed | tf_op | source)
XLA Modules:
  0.0 978.6 jit_solution(356773457502795399)
XLA Ops:
  7.2 0.8 constant_dynamic-slice_fusion.1
  8.9 0.8 fusion.116
  9.7 1.1 bitcast_convert_fusion
  11.3 0.7 copy.35
  12.0 2.1 broadcast_in_dim.65
  14.1 15.3 %all-to-all-start = ((bf16[64,5,3584]{2,1,0:T(8,128)(2,1)}), bf16[64,5,3584]{2,1,0:T(8,128)(2,1)}, u32[]{:S(2)}, u32[]{:S(2)}) async-start(bf16[64,5,3584]{2,1,0:T(8,128)(2,1)} %bitcast.183), calls=%async_computation | async-start | bytes 7340032 | tf_op jit(solution)/shard_map/all_to_all | solution.py:72
  29.5 0.7 all-gather.5.cloned.1.call-update
  30.7 0.7 copy.36
  31.3 79.8 %all-to-all-done = bf16[64,5,3584]{2,1,0:T(8,128)(2,1)} async-done(((bf16[64,5,3584]{2,1,0:T(8,128)(2,1)}), bf16[64,5,3584]{2,1,0:T(8,128)(2,1)}, u32[]{:S(2)}, u32[]{:S(2)}) %all-to-all-start) | async-done | bytes 2293792 | tf_op jit(solution)/shard_map/all_to_all | solution.py:72
  111.2 2.1 broadcast_in_dim.66
  113.3 10.4 %all-to-all-start.1 = ((bf16[64,5,3584]{2,1,0:T(8,128)(2,1)}), bf16[64,5,3584]{2,1,0:T(8,128)(2,1)}, u32[]{:S(2)}, u32[]{:S(2)}) async-start(bf16[64,5,3584]{2,1,0:T(8,128)(2,1)} %bitcast.181), calls=%async_computation.1 | async-start | bytes 7340032 | tf_op jit(solution)/shard_map/all_to_all | solution.py:71
  123.7 0.7 all-gather.3.cloned.1.call-update
  124.4 4.5 reshape.160
  129.0 73.4 %all-to-all-done.1 = bf16[64,5,3584]{2,1,0:T(8,128)(2,1)} async-done(((bf16[64,5,3584]{2,1,0:T(8,128)(2,1)}), bf16[64,5,3584]{2,1,0:T(8,128)(2,1)}, u32[]{:S(2)}, u32[]{:S(2)}) %all-to-all-start.1) | async-done | bytes 2293792 | tf_op jit(solution)/shard_map/all_to_all | solution.py:71
  202.4 3.2 reshape.162
  205.6 5.1 fusion.96
  210.8 5.2 broadcast_select_fusion.2
  216.0 1.4 convolution_convert_fusion.2
  217.4 2.7 reshape.163
  220.1 13.8 %all-to-all-start.2 = ((bf16[64,5,3584]{2,1,0:T(8,128)(2,1)}), bf16[64,5,3584]{2,1,0:T(8,128)(2,1)}, u32[]{:S(2)}, u32[]{:S(2)}) async-start(bf16[64,5,3584]{2,1,0:T(8,128)(2,1)} %reshape.163), calls=%async_computation.2 | async-start | bytes 7340032 | tf_op jit(solution)/shard_map/all_to_all | solution.py:84
  235.3 0.7 copy.41
  236.0 78.1 %all-to-all-done.2 = bf16[64,5,3584]{2,1,0:T(8,128)(2,1)} async-done(((bf16[64,5,3584]{2,1,0:T(8,128)(2,1)}), bf16[64,5,3584]{2,1,0:T(8,128)(2,1)}, u32[]{:S(2)}, u32[]{:S(2)}) %all-to-all-start.2) | async-done | bytes 2293792 | tf_op jit(solution)/shard_map/all_to_all | solution.py:84
  314.1 2.1 broadcast_in_dim.70
  316.2 11.7 %all-to-all-start.4 = ((bf16[64,5,3584]{2,1,0:T(8,128)(2,1)}), bf16[64,5,3584]{2,1,0:T(8,128)(2,1)}, u32[]{:S(2)}, u32[]{:S(2)}) async-start(bf16[64,5,3584]{2,1,0:T(8,128)(2,1)} %bitcast.180), calls=%async_computation.4 | async-start | bytes 7340032 | tf_op jit(solution)/shard_map/all_to_all | solution.py:71
  327.9 2.9 bitcast_reduce_fusion.2
  330.9 0.6 bitcast_dynamic-update-slice_fusion.1
  331.5 1.3 collective-permute-start
  332.8 85.5 %collective-permute-done = bf16[64,3584]{1,0:T(8,128)(2,1)S(1)} collective-permute-done((bf16[64,3584]{1,0:T(8,128)(2,1)S(1)}, bf16[64,3584]{1,0:T(8,128)(2,1)S(1)}, u32[]{:S(2)}, u32[]{:S(2)}) %collective-permute-start) | collective-permute-done | bytes 458784 | tf_op jit(solution)/shard_map/ppermute | solution.py:10
  418.9 1.9 copy.40
  420.8 3.6 broadcast_in_dim.69
  424.4 13.7 %all-to-all-start.3 = ((bf16[64,5,3584]{2,1,0:T(8,128)(2,1)}), bf16[64,5,3584]{2,1,0:T(8,128)(2,1)}, u32[]{:S(2)}, u32[]{:S(2)}) async-start(bf16[64,5,3584]{2,1,0:T(8,128)(2,1)} %bitcast.184), calls=%async_computation.3 | async-start | bytes 7340032 | tf_op jit(solution)/shard_map/all_to_all | solution.py:72
  438.1 4.6 reshape.168
  442.7 5.0 fusion.97
  447.7 74.6 %all-to-all-done.3 = bf16[64,5,3584]{2,1,0:T(8,128)(2,1)} async-done(((bf16[64,5,3584]{2,1,0:T(8,128)(2,1)}), bf16[64,5,3584]{2,1,0:T(8,128)(2,1)}, u32[]{:S(2)}, u32[]{:S(2)}) %all-to-all-start.3) | async-done | bytes 2293792 | tf_op jit(solution)/shard_map/all_to_all | solution.py:72
  522.3 4.6 reshape.166
  526.9 5.2 broadcast_select_fusion.1
  532.2 2.9 convolution_convert_fusion.1
  535.0 4.5 reshape.169
  539.6 11.2 %all-to-all-start.5 = ((bf16[64,5,3584]{2,1,0:T(8,128)(2,1)}), bf16[64,5,3584]{2,1,0:T(8,128)(2,1)}, u32[]{:S(2)}, u32[]{:S(2)}) async-start(bf16[64,5,3584]{2,1,0:T(8,128)(2,1)} %reshape.169), calls=%async_computation.5 | async-start | bytes 7340032 | tf_op jit(solution)/shard_map/all_to_all | solution.py:84
  552.2 1.9 copy.46
  554.1 80.5 %all-to-all-done.5 = bf16[64,5,3584]{2,1,0:T(8,128)(2,1)} async-done(((bf16[64,5,3584]{2,1,0:T(8,128)(2,1)}), bf16[64,5,3584]{2,1,0:T(8,128)(2,1)}, u32[]{:S(2)}, u32[]{:S(2)}) %all-to-all-start.5) | async-done | bytes 2293792 | tf_op jit(solution)/shard_map/all_to_all | solution.py:84
  634.6 3.6 broadcast_in_dim.74
  638.2 10.2 %all-to-all-start.7 = ((bf16[64,5,3584]{2,1,0:T(8,128)(2,1)}), bf16[64,5,3584]{2,1,0:T(8,128)(2,1)}, u32[]{:S(2)}, u32[]{:S(2)}) async-start(bf16[64,5,3584]{2,1,0:T(8,128)(2,1)} %bitcast.179), calls=%async_computation.7 | async-start | bytes 7340032 | tf_op jit(solution)/shard_map/all_to_all | solution.py:71
  648.5 2.8 bitcast_reduce_fusion.1
  651.3 0.6 bitcast_dynamic-update-slice_fusion
  651.9 1.3 collective-permute-start.1
  653.2 82.6 %collective-permute-done.1 = bf16[64,3584]{1,0:T(8,128)(2,1)S(1)} collective-permute-done((bf16[64,3584]{1,0:T(8,128)(2,1)S(1)}, bf16[64,3584]{1,0:T(8,128)(2,1)S(1)}, u32[]{:S(2)}, u32[]{:S(2)}) %collective-permute-start.1) | collective-permute-done | bytes 458784 | tf_op jit(solution)/shard_map/ppermute | solution.py:10
  736.4 1.9 copy.45
  738.3 3.6 broadcast_in_dim.73
  741.9 14.2 %all-to-all-start.6 = ((bf16[64,5,3584]{2,1,0:T(8,128)(2,1)}), bf16[64,5,3584]{2,1,0:T(8,128)(2,1)}, u32[]{:S(2)}, u32[]{:S(2)}) async-start(bf16[64,5,3584]{2,1,0:T(8,128)(2,1)} %bitcast.182), calls=%async_computation.6 | async-start | bytes 7340032 | tf_op jit(solution)/shard_map/all_to_all | solution.py:72
  756.2 4.6 reshape.174
  760.7 4.9 fusion.98
  765.6 74.1 %all-to-all-done.6 = bf16[64,5,3584]{2,1,0:T(8,128)(2,1)} async-done(((bf16[64,5,3584]{2,1,0:T(8,128)(2,1)}), bf16[64,5,3584]{2,1,0:T(8,128)(2,1)}, u32[]{:S(2)}, u32[]{:S(2)}) %all-to-all-start.6) | async-done | bytes 2293792 | tf_op jit(solution)/shard_map/all_to_all | solution.py:72
  839.7 4.5 reshape.172
  844.3 7.5 fusion.12
  852.1 4.4 broadcast_select_fusion
  856.9 5.6 fusion.15
  862.5 5.5 convolution_convert_fusion
  868.0 4.5 reshape.175
  872.5 11.7 %all-to-all-start.8 = ((bf16[64,5,3584]{2,1,0:T(8,128)(2,1)}), bf16[64,5,3584]{2,1,0:T(8,128)(2,1)}, u32[]{:S(2)}, u32[]{:S(2)}) async-start(bf16[64,5,3584]{2,1,0:T(8,128)(2,1)} %reshape.175), calls=%async_computation.8 | async-start | bytes 7340032 | tf_op jit(solution)/shard_map/all_to_all | solution.py:84
  884.2 0.9 copy.63
  885.1 82.5 %all-to-all-done.8 = bf16[64,5,3584]{2,1,0:T(8,128)(2,1)} async-done(((bf16[64,5,3584]{2,1,0:T(8,128)(2,1)}), bf16[64,5,3584]{2,1,0:T(8,128)(2,1)}, u32[]{:S(2)}, u32[]{:S(2)}) %all-to-all-start.8) | async-done | bytes 2293792 | tf_op jit(solution)/shard_map/all_to_all | solution.py:84
  967.6 2.9 bitcast_reduce_fusion
  970.5 1.4 fusion.29
  (80 shorter events, 6.9 us)
Async XLA Ops:
  7.2 23.1 %copy-start = (bf16[1,2,64,3584]{3,2,1,0:T(8,128)(2,1)S(1)}, bf16[1,2,64,3584]{3,2,1,0:T(8,128)(2,1)}, u32[]{:S(2)}) copy-start(bf16[1,2,64,3584]{3,2,1,0:T(8,128)(2,1)} %param.7) | copy-start | bytes 2752516
  14.1 97.0 %all-to-all-start = ((bf16[64,5,3584]{2,1,0:T(8,128)(2,1)}), bf16[64,5,3584]{2,1,0:T(8,128)(2,1)}, u32[]{:S(2)}, u32[]{:S(2)}) async-start(bf16[64,5,3584]{2,1,0:T(8,128)(2,1)} %bitcast.183), calls=%async_computation | async-start | bytes 7340032 | tf_op jit(solution)/shard_map/all_to_all | solution.py:72
  29.5 176.2 %all-gather.5.cloned.1.call-start = ((), (), s32[]{:S(2)}) async-start(), calls=%async_computation.12 | async-start | bytes 5505024 | tf_op jit(solution)/shard_map/all_gather | solution.py:28
  113.3 89.1 %all-to-all-start.1 = ((bf16[64,5,3584]{2,1,0:T(8,128)(2,1)}), bf16[64,5,3584]{2,1,0:T(8,128)(2,1)}, u32[]{:S(2)}, u32[]{:S(2)}) async-start(bf16[64,5,3584]{2,1,0:T(8,128)(2,1)} %bitcast.181), calls=%async_computation.1 | async-start | bytes 7340032 | tf_op jit(solution)/shard_map/all_to_all | solution.py:71
  123.7 87.1 %all-gather.3.cloned.1.call-start = ((), (), s32[]{:S(2)}) async-start(), calls=%async_computation.11 | async-start | bytes 5505024 | tf_op jit(solution)/shard_map/all_gather | solution.py:29
  205.6 5.2 copy-start.2
  210.8 5.2 copy-start.8
  220.1 94.0 %all-to-all-start.2 = ((bf16[64,5,3584]{2,1,0:T(8,128)(2,1)}), bf16[64,5,3584]{2,1,0:T(8,128)(2,1)}, u32[]{:S(2)}, u32[]{:S(2)}) async-start(bf16[64,5,3584]{2,1,0:T(8,128)(2,1)} %reshape.163), calls=%async_computation.2 | async-start | bytes 7340032 | tf_op jit(solution)/shard_map/all_to_all | solution.py:84
  316.2 104.6 %all-to-all-start.4 = ((bf16[64,5,3584]{2,1,0:T(8,128)(2,1)}), bf16[64,5,3584]{2,1,0:T(8,128)(2,1)}, u32[]{:S(2)}, u32[]{:S(2)}) async-start(bf16[64,5,3584]{2,1,0:T(8,128)(2,1)} %bitcast.180), calls=%async_computation.4 | async-start | bytes 7340032 | tf_op jit(solution)/shard_map/all_to_all | solution.py:71
  327.9 3.0 copy-start.6
  331.5 86.8 %collective-permute-start = (bf16[64,3584]{1,0:T(8,128)(2,1)S(1)}, bf16[64,3584]{1,0:T(8,128)(2,1)S(1)}, u32[]{:S(2)}, u32[]{:S(2)}) collective-permute-start(bf16[64,3584]{1,0:T(8,128)(2,1)S(1)} %get-tuple-element.10), channel_id=1, source_target_pairs={{128,0},{129,1},{130,2},{131,3},{132,4},{133,5},{134,6},{135,7},{1... | collective-permute-start | bytes 1376264 | tf_op jit(solution)/shard_map/ppermute | solution.py:10
  424.4 97.9 %all-to-all-start.3 = ((bf16[64,5,3584]{2,1,0:T(8,128)(2,1)}), bf16[64,5,3584]{2,1,0:T(8,128)(2,1)}, u32[]{:S(2)}, u32[]{:S(2)}) async-start(bf16[64,5,3584]{2,1,0:T(8,128)(2,1)} %bitcast.184), calls=%async_computation.3 | async-start | bytes 7340032 | tf_op jit(solution)/shard_map/all_to_all | solution.py:72
  526.9 5.2 copy-start.9
  539.6 95.0 %all-to-all-start.5 = ((bf16[64,5,3584]{2,1,0:T(8,128)(2,1)}), bf16[64,5,3584]{2,1,0:T(8,128)(2,1)}, u32[]{:S(2)}, u32[]{:S(2)}) async-start(bf16[64,5,3584]{2,1,0:T(8,128)(2,1)} %reshape.169), calls=%async_computation.5 | async-start | bytes 7340032 | tf_op jit(solution)/shard_map/all_to_all | solution.py:84
  638.2 100.1 %all-to-all-start.7 = ((bf16[64,5,3584]{2,1,0:T(8,128)(2,1)}), bf16[64,5,3584]{2,1,0:T(8,128)(2,1)}, u32[]{:S(2)}, u32[]{:S(2)}) async-start(bf16[64,5,3584]{2,1,0:T(8,128)(2,1)} %bitcast.179), calls=%async_computation.7 | async-start | bytes 7340032 | tf_op jit(solution)/shard_map/all_to_all | solution.py:71
  651.3 84.5 %copy-start.7 = (bf16[2,64,3584]{2,1,0:T(8,128)(2,1)S(1)}, bf16[2,64,3584]{2,1,0:T(8,128)(2,1)}, u32[]{:S(2)}) copy-start(bf16[2,64,3584]{2,1,0:T(8,128)(2,1)} %param.6) | copy-start | bytes 2752516
  651.9 83.9 %collective-permute-start.1 = (bf16[64,3584]{1,0:T(8,128)(2,1)S(1)}, bf16[64,3584]{1,0:T(8,128)(2,1)S(1)}, u32[]{:S(2)}, u32[]{:S(2)}) collective-permute-start(bf16[64,3584]{1,0:T(8,128)(2,1)S(1)} %get-tuple-element.12), channel_id=1, source_target_pairs={{128,0},{129,1},{130,2},{131,3},{132,4},{133,5},{134,6},{135,7},{1... | collective-permute-start | bytes 1376264 | tf_op jit(solution)/shard_map/ppermute | solution.py:10
  741.9 97.8 %all-to-all-start.6 = ((bf16[64,5,3584]{2,1,0:T(8,128)(2,1)}), bf16[64,5,3584]{2,1,0:T(8,128)(2,1)}, u32[]{:S(2)}, u32[]{:S(2)}) async-start(bf16[64,5,3584]{2,1,0:T(8,128)(2,1)} %bitcast.182), calls=%async_computation.6 | async-start | bytes 7340032 | tf_op jit(solution)/shard_map/all_to_all | solution.py:72
  756.1 215.7 %reduce-scatter.5.cloned.1.call-start = ((), (), s32[]{:S(2)}) async-start(), calls=%async_computation.14 | async-start | bytes 5505024 | tf_op jit(solution)/shard_map/reduce_scatter | solution.py:122
  765.6 78.6 %copy-start.10 = (bf16[320,512]{1,0:T(8,128)(2,1)S(1)}, bf16[320,512]{1,0:T(8,128)(2,1)}, u32[]{:S(2)}) copy-start(bf16[320,512]{1,0:T(8,128)(2,1)} %get-tuple-element.23) | copy-start | bytes 983044
  765.6 78.6 %copy-start.11 = (bf16[320,512]{1,0:T(8,128)(2,1)S(1)}, bf16[320,512]{1,0:T(8,128)(2,1)}, u32[]{:S(2)}) copy-start(bf16[320,512]{1,0:T(8,128)(2,1)} %get-tuple-element.21) | copy-start | bytes 983044
  851.8 120.1 %reduce-scatter.3.cloned.1.call-start = ((), (), s32[]{:S(2)}) async-start(), calls=%async_computation.13 | async-start | bytes 5505024 | tf_op jit(solution)/shard_map/reduce_scatter | solution.py:119
  852.0 4.4 copy-start.3
  852.0 4.4 copy-start.4
  852.0 4.8 copy-start.5
  852.0 4.8 copy-start.12
  852.1 4.8 copy-start.13
  872.5 95.1 %all-to-all-start.8 = ((bf16[64,5,3584]{2,1,0:T(8,128)(2,1)}), bf16[64,5,3584]{2,1,0:T(8,128)(2,1)}, u32[]{:S(2)}, u32[]{:S(2)}) async-start(bf16[64,5,3584]{2,1,0:T(8,128)(2,1)} %reshape.175), calls=%async_computation.8 | async-start | bytes 7340032 | tf_op jit(solution)/shard_map/all_to_all | solution.py:84
  967.6 4.3 copy-start.1
Sparse Core Ops, SparseCore 0:
  32.1 20.3 all-gather.4
  126.3 20.6 all-gather.2
  851.9 17.9 reduce-scatter.4
  872.9 18.1 reduce-scatter.2
where the time goes:
time: 988 us; the launch traced here: 979 us
  waiting for transfers between devices  713 us (72%)
  starting transfers between devices  115 us (12%)
  local copies, waits for them, and re-layouts  66.9 us (7%)
  matrix products  58.2 us (6%)
  between operations  14.5 us (1%)
  other arithmetic  11.3 us (1%)
    all_to_all x3, waiting for transfers between devices, on_device(): lax.all_to_all(partial_rows.reshape(2 * experts, capacity, model_width),...  241 us
    all_to_all x3, waiting for transfers between devices, on_device(): lax.all_to_all(doubled_scaled, 'expert', split_axis=0, concat_axis=0, til...  229 us
    ppermute x2, waiting for transfers between devices, from_behind(): lax.ppermute(value, axis, [(source, source + steps) for source in range(f...  168 us
    all_to_all x3, waiting for transfers between devices, on_device(): lax.all_to_all(doubled_inputs, 'expert', split_axis=0, concat_axis=0, til...  73.4 us
    all_to_all x3, starting transfers between devices, on_device(): lax.all_to_all(doubled_scaled, 'expert', split_axis=0, concat_axis=0, til...  43.2 us
    all_to_all x3, starting transfers between devices, on_device(): lax.all_to_all(partial_rows.reshape(2 * experts, capacity, model_width),...  36.7 us
    all_to_all x3, starting transfers between devices, on_device(): lax.all_to_all(doubled_inputs, 'expert', split_axis=0, concat_axis=0, til...  32.3 us
  transfers between devices with their start and end apart: 15, of which 9 were waited for; matrix products, arithmetic and copies ran while one was open for 8% of the time, Pallas kernels for 0%

commit v1 on v0

v1 whole, which is shorter than its diff:
```python
import functools

import jax
import jax.numpy as jnp
from jax import lax
from jax.experimental import pallas as pl
from jax.experimental.pallas import tpu as pltpu
from jax.sharding import Mesh, PartitionSpec as P

BF = jnp.bfloat16
F32 = jnp.float32
LANES = 128
GROUP = 16
VMEM_BYTES = 28 << 20
CAP = 5
PAIRED = ("pair", "half")
ROWS = GROUP * CAP
NT = (((1,), (1,)), ((), ()))


def vmem_call(body, outs, scratch=(), scalars=0):
    spec = pl.BlockSpec(memory_space=pltpu.VMEM)
    smem = pl.BlockSpec(memory_space=pltpu.SMEM)

    def call(*args):
        return pl.pallas_call(
            body,
            out_shape=outs,
            in_specs=[smem] * scalars + [spec] * (len(args) - scalars),
            out_specs=jax.tree.map(lambda _: spec, outs),
            scratch_shapes=list(scratch),
            cost_estimate=pl.CostEstimate(flops=1, bytes_accessed=1, transcendentals=0),
            compiler_params=pltpu.CompilerParams(vmem_limit_bytes=VMEM_BYTES),
        )(*args)

    return call


def dot(a, b, dims=(((1,), (0,)), ((), ()))):
    return lax.dot_general(a, b, dims, preferred_element_type=F32)


def pack(source, starts, pack_ref, mixed, store):
    blocks = mixed.shape[0] // ROWS
    for side, (row, col) in enumerate(starts):
        for block in range(blocks):
            mixed[block * ROWS : (block + 1) * ROWS, side * LANES : (side + 1) * LANES] = source[
                row : row + ROWS, col + block * LANES : col + (block + 1) * LANES
            ]
    chunks = dot(pack_ref[...], mixed[...])
    high = chunks.shape[0] // GROUP
    for side in range(2):
        for item in range(GROUP):
            store(
                side,
                item,
                chunks[item * high : (item + 1) * high, side * LANES : (side + 1) * LANES].astype(BF),
            )


def unpack(load, unpack_ref, stage, target, starts):
    high = stage.shape[0] // GROUP
    for side in range(2):
        for item in range(GROUP):
            stage[item * high : (item + 1) * high, side * LANES : (side + 1) * LANES] = load(side, item).astype(F32)
    mixed = dot(unpack_ref[...], stage[...].astype(BF))
    for side, (row, col) in enumerate(starts):
        for block in range(mixed.shape[0] // ROWS):
            target[row : row + ROWS, col + block * LANES : col + (block + 1) * LANES] = mixed[
                block * ROWS : (block + 1) * ROWS, side * LANES : (side + 1) * LANES
            ].astype(BF)


def dispatch_body(count, *refs):
    values, places, weights = refs[:count], refs[count : 2 * count], refs[2 * count : 3 * count]
    pack_ref, out, slots, mixed = refs[3 * count :]
    half = slots.shape[1] // 2
    for index in range(count):
        slots[...] = (dot(places[index][...], values[index][...]) * weights[index][...]).astype(BF)
        for group in range(slots.shape[0] // ROWS):

            def store(side, item, chunk, index=index, group=group):
                out[(group * GROUP + item) * 2 + side, index] = chunk

            pack(slots, [(group * ROWS, 0), (group * ROWS, half)], pack_ref, mixed, store)


def dispatch(values, places, weights, packer, chunk_rows):
    count = len(values)
    slot_count, width = places[0].shape[0], values[0].shape[1]
    experts = slot_count // CAP
    return vmem_call(
        functools.partial(dispatch_body, count),
        jax.ShapeDtypeStruct((2 * experts, count, chunk_rows, LANES), BF),
        [pltpu.VMEM((slot_count, width), BF), pltpu.VMEM((packer.shape[1], 2 * LANES), BF)],
    )(*values, *places, *weights, packer)


def unpack_all(got, index, unpack_ref, stage, rows):
    for pair in range(got.shape[0] // (2 * GROUP)):

        def load(side, item, pair=pair):
            return got[(2 * pair + side) * GROUP + item, index]

        unpack(load, unpack_ref, stage, rows, [(2 * pair * ROWS, 0), ((2 * pair + 1) * ROWS, 0)])


def by_parts(rows, parts, dims, own, sent):
    start = 0
    for part in parts:
        product = dot(rows[...], part[...], dims)
        width = product.shape[1]
        own[:, start : start + width] = product
        sent[:, start : start + width] = product.astype(BF)
        start += width


def arrive_body(index, got, unpack_ref, part0, part1, rows, own, sent, stage):
    unpack_all(got, index, unpack_ref, stage, rows)
    dims = NT if part0.shape[1] == rows.shape[1] else (((1,), (0,)), ((), ()))
    by_parts(rows, (part0, part1), dims, own, sent)


def arrive_either_body(index, flag, got, unpack_ref, up0, up1, down0, down1, rows, own, sent, stage):
    unpack_all(got, index, unpack_ref, stage, rows)

    @pl.when(flag[0] == 1)
    def _():
        by_parts(rows, (down0, down1), NT, own, sent)

    @pl.when(flag[0] == 0)
    def _():
        by_parts(rows, (up0, up1), (((1,), (0,)), ((), ())), own, sent)


def shapes_of(got, hidden, width):
    total = got.shape[0] * CAP
    return (
        jax.ShapeDtypeStruct((total, width), BF),
        jax.ShapeDtypeStruct((total, hidden), F32),
        jax.ShapeDtypeStruct((total, hidden), BF),
    )


def arrive(got, index, unpacker, parts):
    stage = pltpu.VMEM((unpacker.shape[1], 2 * LANES), F32)
    hidden = 2 * min(parts[0].shape)
    return vmem_call(functools.partial(arrive_body, index), shapes_of(got, hidden, max(parts[0].shape)), [stage])(
        got, unpacker, *parts
    )


def arrive_either(flag, got, index, unpacker, ups, downs):
    stage = pltpu.VMEM((unpacker.shape[1], 2 * LANES), F32)
    return vmem_call(
        functools.partial(arrive_either_body, index),
        shapes_of(got, 2 * ups[0].shape[1], ups[0].shape[0]),
        [stage],
        1,
    )(flag, got, unpacker, *ups, *downs)


def turn_body(pre_own, pre_got, act_own, act_got, up0, up1, pack_ref, active, grads, out, rows, mixed):
    pre = pre_own[...] + pre_got[...].astype(F32)
    gate = 1.0 / (1.0 + jnp.exp(-pre))
    active[...] = (pre * gate).astype(BF)
    slope = gate * (1.0 + pre * (1.0 - gate))
    grads[...] = ((act_own[...] + act_got[...].astype(F32)) * slope).astype(BF)
    hidden = up0.shape[1]
    rows[...] = (dot(grads[:, :hidden], up0[...], NT) + dot(grads[:, hidden:], up1[...], NT)).astype(BF)
    for pair in range(out.shape[0] // (2 * GROUP)):

        def store(side, item, chunk, pair=pair):
            out[(2 * pair + side) * GROUP + item, 0] = chunk

        pack(rows, [(2 * pair * ROWS, 0), ((2 * pair + 1) * ROWS, 0)], pack_ref, mixed, store)


def turn(pre_own, pre_got, act_own, act_got, ups, packer, chunk_rows):
    total, hidden = pre_own.shape
    width = ups[0].shape[0]
    kept = jax.ShapeDtypeStruct((total, hidden), BF)
    return vmem_call(
        turn_body,
        (kept, kept, jax.ShapeDtypeStruct((total // CAP, 1, chunk_rows, LANES), BF)),
        [pltpu.VMEM((total, width), BF), pltpu.VMEM((packer.shape[1], 2 * LANES), BF)],
    )(pre_own, pre_got, act_own, act_got, *ups, packer)


def combine_body(got, unpack_ref, place_t, incoming, out, slots, stage):
    half = slots.shape[1] // 2
    for group in range(slots.shape[0] // ROWS):

        def load(side, item, group=group):
            return got[(group * GROUP + item) * 2 + side, 0]

        unpack(load, unpack_ref, stage, slots, [(group * ROWS, 0), (group * ROWS, half)])
    out[...] = (dot(place_t[...], slots[...]) + incoming[...].astype(F32)).astype(BF)


def combine(got, unpacker, place_t, incoming):
    return vmem_call(
        combine_body,
        jax.ShapeDtypeStruct(incoming.shape, BF),
        [
            pltpu.VMEM((place_t.shape[1], incoming.shape[1]), BF),
            pltpu.VMEM((unpacker.shape[1], 2 * LANES), F32),
        ],
    )(got, unpacker, place_t, incoming)


def slots_of(routes, gates, experts):
    tokens, top = routes.shape
    flat = routes.reshape(-1)
    order = jnp.arange(tokens * top, dtype=jnp.int32)
    earlier = (flat[:, None] == flat[None, :]) & (order[None, :] < order[:, None])
    slot = flat * CAP + jnp.sum(earlier.astype(jnp.int32), axis=1)
    hits = slot.reshape(tokens, top)[None] == jnp.arange(experts * CAP, dtype=jnp.int32)[:, None, None]
    place = jnp.any(hits, axis=2)
    weight = jnp.sum(jnp.where(hits, gates[None], 0.0), axis=(1, 2))
    return place.astype(BF), weight[:, None]


def packing(blocks, chunk_rows):
    total = GROUP * chunk_rows
    row = jnp.arange(total, dtype=jnp.int32)
    col = jnp.arange(blocks * ROWS, dtype=jnp.int32)
    item, place = row // chunk_rows, row % chunk_rows
    block, inner = place // CAP, place % CAP
    wanted = jnp.where(block < blocks, block * ROWS + item * CAP + inner, -1)
    return (wanted[:, None] == col[None, :]).astype(BF), (wanted[None, :] == col[:, None]).astype(BF)


def swap(value, axis):
    return lax.ppermute(value, axis, [(0, 1), (1, 0)])


def cross(value):
    moved = lax.ppermute(value, ("dp", "half"), [(1, 2), (2, 1)])
    return jnp.where(lax.axis_index("dp") == lax.axis_index("half"), value, moved)


def send(chunks):
    return lax.all_to_all(chunks, PAIRED, split_axis=0, concat_axis=0, tiled=True)


def on_device(grad_out, layer_in, routes, gates, w_up, w_down):
    section = lax.axis_index("section")
    top_section = section == lax.axis_size("section") - 1
    flag = top_section.astype(jnp.int32)[None]
    experts = lax.axis_size("pair")
    width = grad_out.shape[2]
    blocks = width // (2 * LANES)
    chunk_rows = -(-blocks * CAP // 8) * 8
    packer, unpacker = packing(blocks, chunk_rows)

    place, weight = zip(*[slots_of(routes[0, micro], gates[0, micro], experts) for micro in range(2)])
    place_t = [p.T for p in place]
    ones = jnp.ones_like(weight[0])
    inputs = [layer_in[0, 0], layer_in[0, 1]]

    up_here, down_here = cross(w_up[0, 0]), cross(w_down[0, 0])
    ups = (up_here, swap(up_here, "dp"))
    downs = (down_here, swap(down_here, "dp"))

    def pick(here, there):
        return jnp.where(top_section, here, there)

    def prepare(values, places, weights):
        return dispatch(values, places, weights, packer, chunk_rows)

    def top_start():
        first = send(prepare([inputs[0], grad_out[0]], [place[0]] * 2, [ones, weight[0]]))
        return first, prepare([inputs[1], grad_out[1]], [place[1]] * 2, [ones, weight[1]])

    def low_start():
        chunks = prepare(inputs, place, [ones, ones])
        return jnp.zeros_like(chunks), chunks

    first, second_chunks = lax.cond(top_section, top_start, low_start)
    first, second_chunks, unpacker = lax.optimization_barrier((first, second_chunks, unpacker))
    second = send(second_chunks)

    rows_a0, own_a0, sent_a0 = arrive(first, 0, unpacker, ups)
    got_a0 = swap(sent_a0, "half")
    rows_a1, own_a1, sent_a1 = arrive(first, 1, unpacker, downs)
    got_a1 = swap(sent_a1, "half")
    top_active0, top_grads0, back0 = turn(own_a0, got_a0, own_a1, got_a1, ups, packer, chunk_rows)
    second, back0 = lax.optimization_barrier((second, back0))
    third = send(back0)

    rows_b0, own_b0, sent_b0 = arrive(second, 0, unpacker, ups)
    got_b0 = swap(sent_b0, "half")
    rows_b1, own_b1, sent_b1 = arrive_either(flag, second, 1, unpacker, ups, downs)
    got_b1 = swap(sent_b1, "half")
    top_active1, top_grads1, back1 = turn(own_b0, got_b0, own_b1, got_b1, ups, packer, chunk_rows)

    top_out0 = combine(third, unpacker, place_t[0], grad_out[0])
    low_in0 = lax.ppermute(top_out0, "section", [(1, 0)])
    fourth_chunks = pick(back1, dispatch([low_in0], [place[0]], [weight[0]], packer, chunk_rows))
    rows_in0, rows_in1 = pick(rows_a0, rows_b0), pick(rows_b0, rows_b1)
    fourth = send(fourth_chunks)
    top_out1 = combine(fourth, unpacker, place_t[1], grad_out[1])
    low_in1 = lax.ppermute(top_out1, "section", [(1, 0)])
    rows_d, own_d, sent_d = arrive(fourth, 0, unpacker, downs)
    low_in1, sent_d = lax.optimization_barrier((low_in1, sent_d))
    got_d = swap(sent_d, "half")

    fifth = send(dispatch([low_in1], [place[1]], [weight[1]], packer, chunk_rows))
    low_active0, low_grads0, back2 = turn(own_b0, got_b0, own_d, got_d, ups, packer, chunk_rows)
    fifth, back2 = lax.optimization_barrier((fifth, back2))
    sixth = send(back2)
    rows_e, own_e, sent_e = arrive(fifth, 0, unpacker, downs)
    got_e = swap(sent_e, "half")
    low_active1, low_grads1, back3 = turn(own_b1, got_b1, own_e, got_e, ups, packer, chunk_rows)
    seventh = send(back3)

    def both(top0, top1, low0, low1):
        return jnp.concatenate([pick(top0, low0), pick(top1, low1)])

    hidden = own_a0.shape[1] // 2
    over = (((0,), (0,)), ((), ()))
    rows = jnp.concatenate([rows_in0, rows_in1])
    scaled = both(rows_a1, rows_b1, rows_d, rows_e)
    sixth, low_active1, low_grads1, scaled, rows = lax.optimization_barrier(
        (sixth, low_active1, low_grads1, scaled, rows)
    )
    active = both(top_active0, top_active1, low_active0, low_active1)
    grads = both(top_grads0, top_grads1, low_grads0, low_grads1)
    other_up = swap(dot(rows, grads[:, hidden:], over).astype(BF), "dp")
    other_down = swap(dot(active[:, hidden:], scaled, over).astype(BF), "dp")
    grad_up = (dot(rows, grads[:, :hidden], over) + other_up.astype(F32)).astype(BF)
    grad_down = (dot(active[:, :hidden], scaled, over) + other_down.astype(F32)).astype(BF)
    grad_up, grad_down = cross(grad_up), cross(grad_down)
    seventh, grad_up, grad_down = lax.optimization_barrier((seventh, grad_up, grad_down))
    low_out0 = combine(sixth, unpacker, place_t[0], low_in0)
    low_out1 = combine(seventh, unpacker, place_t[1], low_in1)
    results = jnp.stack([pick(top_out0, low_out0), pick(top_out1, low_out1)])
    return results[None], grad_up[None, None], grad_down[None, None]


def solution(mesh):
    sizes = dict(zip(mesh.axis_names, mesh.devices.shape))
    fine = Mesh(
        mesh.devices.reshape(sizes["section"], sizes["dp"], sizes["expert"] // 2, 2),
        ("section", "dp", "pair", "half"),
    )
    tokens = P("section", None, ("dp", "pair", "half"), None)
    up, down = P("section", PAIRED, "dp", None), P("section", PAIRED, None, "dp")
    return jax.shard_map(
        on_device,
        mesh=fine,
        in_specs=(P(None, ("dp", "pair", "half"), None), tokens, tokens, tokens, up, down),
        out_specs=(tokens, up, down),
        check_vma=False,
    )
```

time: 988 us -> 470 us (0.48)
  the two profiles are of different devices: /device:TPU:1 before, /device:TPU:35 now
where the time goes in v1:
time: 470 us; the launch traced here: 461 us
  waiting for transfers between devices  148 us (31%)
  starting transfers between devices  115 us (24%)
  Pallas kernels  79.2 us (17%)
  local copies, waits for them, and re-layouts  49.8 us (11%)
  blocking collectives  33.3 us (7%)
  other arithmetic  23.7 us (5%)
  matrix products  8.96 us (2%)
    ppermute x10, waiting for transfers between devices, swap(): return lax.ppermute(value, axis, [(0, 1), (1, 0)])  84.8 us
    all_to_all x6, starting transfers between devices, send(): lax.all_to_all(chunks, PAIRED, split_axis=0, concat_axis=0, tiled=True)  81.8 us
    pallas_call x18, Pallas kernels, call(): pl.pallas_call(body, out_shape=outs, in_specs=[smem] * scalars + [spec] *...  79.2 us
    unnamed x130, local copies, waits for them, and re-layouts  41.7 us
    all_to_all x6, waiting for transfers between devices, send(): lax.all_to_all(chunks, PAIRED, split_axis=0, concat_axis=0, tiled=True)  34 us
    all_to_all x1, blocking collectives, send(): lax.all_to_all(chunks, PAIRED, split_axis=0, concat_axis=0, tiled=True)  33.3 us
    ppermute x4, waiting for transfers between devices, cross(): moved = lax.ppermute(value, ('dp', 'half'), [(1, 2), (2, 1)])  29.3 us
    ppermute x10, starting transfers between devices, swap(): return lax.ppermute(value, axis, [(0, 1), (1, 0)])  18.1 us
  transfers between devices with their start and end apart: 22, of which 11 were waited for; matrix products, arithmetic and copies ran while one was open for 7% of the time, Pallas kernels for 14%

profile of v1, /device:TPU:35, one launch (start us, length us, event | category | flops | bytes accessed | tf_op | source)
XLA Modules:
  0.0 460.6 jit_solution(12843886238080127840)
XLA Ops:
  0.6 3.8 collective-permute-start.3
  4.4 1.9 collective-permute-start
  7.4 2.0 fusion.pack_ref.refs_3_
  10.9 2.0 slice_bitcast_fusion.4
  13.2 65.3 %conditional.1 = (bf16[64,2,72,128]{3,2,1,0:T(8,128)(2,1)}, bf16[64,2,72,128]{3,2,1,0:T(8,128)(2,1)}) conditional(s32[]{:T(128)} %convert_element_type.64, (bf16[64,3584]{1,0:T(8,128)(2,1)}, bf16[64,3584]{1,0:T(8,128)(2,1)S(1)}, bf16[160,64]{0,1:T(8,128)(2,1)S(1)}, bf16[160,64]{0,1:T(8,128)(2,1)S(1)}, bf16[1152,1120]{1,0:T(8,128)(2,1)}) %tuple.22, ...), branch_computations={%region_6.7_spmd, %region_7.8_spmd} | conditional | flops 2 | bytes 22105352 | solution.py:280
  15.3 5.9 %branch_1_fun.2 = bf16[64,2,72,128]{3,2,1,0:T(8,128)(2,1)S(1)} custom-call(bf16[64,3584]{1,0:T(8,128)(2,1)S(1)} %copy-done.61, bf16[64,3584]{1,0:T(8,128)(2,1)S(1)} %get-tuple-element.185.refs_1_, bf16[160,64]{1,0:T(8,128)(2,1)S(1)} %copy.47.refs_2_.refs_3_, bf16[160,64]{1,0:T(8,128)(2,1)S(1)} %copy.47.refs_2_.refs_3_, ...), custom_call_target="tpu_custom_call" | custom-call | flops 1 | bytes 1 | tf_op jit(solution)/shard_map/cond/branch_1_fun/pallas_call | solution.py:26
  22.6 13.7 %all-to-all-start = ((bf16[64,2,72,128]{3,2,1,0:T(8,128)(2,1)}), bf16[64,2,72,128]{3,2,1,0:T(8,128)(2,1)}, u32[]{:S(2)}, u32[]{:S(2)}) async-start(bf16[64,2,72,128]{3,2,1,0:T(8,128)(2,1)} %copy-done.20), calls=%async_computation | async-start | bytes 4718592 | tf_op jit(solution)/shard_map/cond/branch_1_fun/all_to_all | solution.py:244
  36.5 7.5 %branch_1_fun.3 = bf16[64,2,72,128]{3,2,1,0:T(8,128)(2,1)} custom-call(bf16[64,3584]{1,0:T(8,128)(2,1)} %copy-done.60, bf16[64,3584]{1,0:T(8,128)(2,1)S(1)} %get-tuple-element.184.refs_1_, bf16[160,64]{1,0:T(8,128)(2,1)S(1)} %copy.49.refs_2_.refs_3_, bf16[160,64]{1,0:T(8,128)(2,1)S(1)} %copy.49.refs_2_.refs_3_, f32[160,1]{1,0:T(8,128)S(1)} %broadcast_in_dim.46.refs_4_, ...), custom_call_target="tpu_custom_call" | custom-call | flops 1 | bytes 1 | tf_op jit(solution)/shard_map/cond/branch_1_fun/pallas_call | solution.py:26
  44.0 33.9 %all-to-all-done = bf16[64,2,72,128]{3,2,1,0:T(8,128)(2,1)} async-done(((bf16[64,2,72,128]{3,2,1,0:T(8,128)(2,1)}), bf16[64,2,72,128]{3,2,1,0:T(8,128)(2,1)}, u32[]{:S(2)}, u32[]{:S(2)}) %all-to-all-start) | async-done | bytes 2359328 | tf_op jit(solution)/shard_map/cond/branch_1_fun/all_to_all | solution.py:244
  78.4 17.3 %all-to-all-start.1 = ((bf16[64,2,72,128]{3,2,1,0:T(8,128)(2,1)}), bf16[64,2,72,128]{3,2,1,0:T(8,128)(2,1)}, u32[]{:S(2)}, u32[]{:S(2)}) async-start(bf16[64,2,72,128]{3,2,1,0:T(8,128)(2,1)} %get-tuple-element.95), calls=%async_computation.1 | async-start | bytes 4718592 | tf_op jit(solution)/shard_map/all_to_all | solution.py:244
  95.7 2.4 broadcast_select_fusion.1.part0.down0
  98.1 6.3 %collective-permute-start.4 = (bf16[512,1792]{1,0:T(8,128)(2,1)S(1)}, bf16[512,1792]{1,0:T(8,128)(2,1)S(1)}, u32[]{:S(2)}, u32[]{:S(2)}) collective-permute-start(bf16[512,1792]{1,0:T(8,128)(2,1)S(1)} %broadcast_select_fusion.1.part0.down0), channel_id=1, source_target_pairs={{0,64},{64,0},{1,65},{65,1},{2,66},{66,2},{3,67},{67,3},{4,68},{68... | collective-permute-start | bytes 5505032 | tf_op jit(solution)/shard_map/ppermute | solution.py:235
  104.4 1.8 broadcast_select_fusion.3.part0.up0
  107.8 5.2 %shard_map.86 = (bf16[320,1792]{1,0:T(8,128)(2,1)S(1)}, f32[320,1024]{1,0:T(8,128)S(1)}, bf16[320,1024]{1,0:T(8,128)(2,1)S(1)}) custom-call(bf16[64,2,72,128]{3,2,1,0:T(8,128)(2,1)} %get-tuple-element.96.got, bf16[1120,1152]{1,0:T(8,128)(2,1)S(1)} %fusion.1.unpack_ref, bf16[512,1792]{1,0:T(8,128)(2,1)S(1)} %broadcast_select_fusion.1.part0.down0, ...), custom_call_target="tpu_custom_call" | custom-call | flops 1 | bytes 1 | tf_op jit(solution)/shard_map/pallas_call | solution.py:26
  113.0 1.8 collective-permute-start.5
  114.9 5.2 %shard_map.85 = (bf16[320,1792]{1,0:T(8,128)(2,1)S(1)}, f32[320,1024]{1,0:T(8,128)S(1)}, bf16[320,1024]{1,0:T(8,128)(2,1)S(1)}) custom-call(bf16[64,2,72,128]{3,2,1,0:T(8,128)(2,1)} %get-tuple-element.96.got, bf16[1120,1152]{1,0:T(8,128)(2,1)S(1)} %fusion.1.unpack_ref, bf16[1792,512]{1,0:T(8,128)(2,1)S(1)} %broadcast_select_fusion.3.part0.up0, ...), custom_call_target="tpu_custom_call" | custom-call | flops 1 | bytes 1 | tf_op jit(solution)/shard_map/pallas_call | solution.py:26
  121.6 16.4 %collective-permute-done.5.act_got = bf16[320,1024]{1,0:T(8,128)(2,1)S(1)} collective-permute-done((bf16[320,1024]{1,0:T(8,128)(2,1)S(1)}, bf16[320,1024]{1,0:T(8,128)(2,1)S(1)}, u32[]{:S(2)}, u32[]{:S(2)}) %collective-permute-start.5) | collective-permute-done | bytes 655392 | tf_op jit(solution)/shard_map/ppermute | solution.py:235
  138.0 14.7 %collective-permute-done.2.pre_got = bf16[320,1024]{1,0:T(8,128)(2,1)S(1)} collective-permute-done((bf16[320,1024]{1,0:T(8,128)(2,1)S(1)}, bf16[320,1024]{1,0:T(8,128)(2,1)S(1)}, u32[]{:S(2)}, u32[]{:S(2)}) %collective-permute-start.2) | collective-permute-done | bytes 655392 | tf_op jit(solution)/shard_map/ppermute | solution.py:235
  152.7 3.3 shard_map.87
  158.8 11.3 %all-to-all-start.2 = ((bf16[64,1,72,128]{3,2,1,0:T(8,128)(2,1)}), bf16[64,1,72,128]{3,2,1,0:T(8,128)(2,1)}, u32[]{:S(2)}, u32[]{:S(2)}) async-start(bf16[64,1,72,128]{3,2,1,0:T(8,128)(2,1)} %copy-done.34), calls=%async_computation.2 | async-start | bytes 2359296 | tf_op jit(solution)/shard_map/all_to_all | solution.py:244
  171.7 1.5 copy-done.6
  173.2 1.5 copy-done.11
  174.7 1.5 copy-done.15
  176.2 5.6 %shard_map.90 = (bf16[320,1792]{1,0:T(8,128)(2,1)S(1)}, f32[320,1024]{1,0:T(8,128)S(1)}, bf16[320,1024]{1,0:T(8,128)(2,1)}) custom-call(s32[1]{0:T(128)} %bitcast.14.flag, bf16[64,2,72,128]{3,2,1,0:T(8,128)(2,1)} %all-to-all-done.1.got, bf16[1120,1152]{1,0:T(8,128)(2,1)S(1)} %fusion.1.unpack_ref, bf16[1792,512]{1,0:T(8,128)(2,1)S(1)} %copy-done.1, ...), custom_call_target="tpu_custom_call" | custom-call | flops 1 | bytes 1 | tf_op jit(solution)/shard_map/pallas_call | solution.py:26
  182.9 5.3 %shard_map.89 = (bf16[320,1792]{1,0:T(8,128)(2,1)S(1)}, f32[320,1024]{1,0:T(8,128)S(1)}, bf16[320,1024]{1,0:T(8,128)(2,1)}) custom-call(bf16[64,2,72,128]{3,2,1,0:T(8,128)(2,1)} %all-to-all-done.1.got, bf16[1120,1152]{1,0:T(8,128)(2,1)S(1)} %fusion.1.unpack_ref, bf16[1792,512]{1,0:T(8,128)(2,1)S(1)} %copy-done.1, bf16[1792,512]{1,0:T(8,128)(2,1)S(1)} %copy-done.6), custom_call_target="tpu_custom_call" | custom-call | flops 1 | bytes 1 | tf_op jit(solution)/shard_map/pallas_call | solution.py:26
  193.6 4.0 shard_map.88
  197.6 2.1 collective-permute-start.8
  200.8 14.1 %collective-permute-done.6.pre_got = bf16[320,1024]{1,0:T(8,128)(2,1)} collective-permute-done((bf16[320,1024]{1,0:T(8,128)(2,1)}, bf16[320,1024]{1,0:T(8,128)(2,1)}, u32[]{:S(2)}, u32[]{:S(2)}) %collective-permute-start.6) | collective-permute-done | bytes 655392 | tf_op jit(solution)/shard_map/ppermute | solution.py:235
  214.9 1.5 copy-done.2
  220.5 5.5 %shard_map.91 = (bf16[320,1024]{1,0:T(8,128)(2,1)S(1)}, bf16[320,1024]{1,0:T(8,128)(2,1)S(1)}, bf16[64,1,72,128]{3,2,1,0:T(8,128)(2,1)S(1)}) custom-call(f32[320,1024]{1,0:T(8,128)S(1)} %copy-done.25, bf16[320,1024]{1,0:T(8,128)(2,1)} %collective-permute-done.6.pre_got, f32[320,1024]{1,0:T(8,128)S(1)} %copy-done.22, ...), custom_call_target="tpu_custom_call" | custom-call | flops 1 | bytes 1 | tf_op jit(solution)/shard_map/pallas_call | solution.py:26
  226.1 3.5 shard_map.92
  229.8 33.3 %all_to_all.34.got = bf16[64,1,72,128]{3,2,1,0:T(8,128)(2,1)S(1)} all-to-all(bf16[64,1,72,128]{3,2,1,0:T(8,128)(2,1)S(1)} %broadcast_select_fusion.4), channel_id=1, replica_groups=mesh['section'=2,'dp'=2,'pair'=32,'half'=2] {'pair','half'}, dimensions={0} | all-to-all | bytes 2359296 | tf_op jit(solution)/shard_map/all_to_all | solution.py:244
  263.1 2.7 shard_map.93
  265.8 2.1 collective-permute-start.9
  272.4 2.8 shard_map.94
  278.3 3.2 shard_map.95
  282.5 9.2 %all-to-all-start.4 = ((bf16[64,1,72,128]{3,2,1,0:T(8,128)(2,1)}), bf16[64,1,72,128]{3,2,1,0:T(8,128)(2,1)}, u32[]{:S(2)}, u32[]{:S(2)}) async-start(bf16[64,1,72,128]{3,2,1,0:T(8,128)(2,1)} %copy-done.27), calls=%async_computation.4 | async-start | bytes 2359296 | tf_op jit(solution)/shard_map/all_to_all | solution.py:244
  293.0 20.4 %collective-permute-done.10.act_got = bf16[320,1024]{1,0:T(8,128)(2,1)S(1)} collective-permute-done((bf16[320,1024]{1,0:T(8,128)(2,1)}, bf16[320,1024]{1,0:T(8,128)(2,1)S(1)}, u32[]{:S(2)}, u32[]{:S(2)}) %collective-permute-start.10) | collective-permute-done | bytes 655392 | tf_op jit(solution)/shard_map/ppermute | solution.py:235
  313.4 1.5 copy-done.3
  319.0 5.4 %shard_map.96 = (bf16[320,1024]{1,0:T(8,128)(2,1)S(1)}, bf16[320,1024]{1,0:T(8,128)(2,1)S(1)}, bf16[64,1,72,128]{3,2,1,0:T(8,128)(2,1)S(1)}) custom-call(f32[320,1024]{1,0:T(8,128)S(1)} %copy-done.26, bf16[320,1024]{1,0:T(8,128)(2,1)} %collective-permute-done.6.pre_got, f32[320,1024]{1,0:T(8,128)S(1)} %copy-done.31, ...), custom_call_target="tpu_custom_call" | custom-call | flops 1 | bytes 1 | tf_op jit(solution)/shard_map/pallas_call | solution.py:26
  327.2 18.7 %all-to-all-start.5 = ((bf16[64,1,72,128]{3,2,1,0:T(8,128)(2,1)}), bf16[64,1,72,128]{3,2,1,0:T(8,128)(2,1)}, u32[]{:S(2)}, u32[]{:S(2)}) async-start(bf16[64,1,72,128]{3,2,1,0:T(8,128)(2,1)} %copy-done.33), calls=%async_computation.5 | async-start | bytes 2359296 | tf_op jit(solution)/shard_map/all_to_all | solution.py:244
  345.9 1.5 broadcast_select_fusion.8
  347.7 1.5 copy-done.17
  349.2 4.3 shard_map.97
  355.1 1.5 pad_maximum_fusion.1
  356.6 1.6 pad_maximum_fusion
  358.2 16.7 %collective-permute-done.11.act_got = bf16[320,1024]{1,0:T(8,128)(2,1)S(1)} collective-permute-done((bf16[320,1024]{1,0:T(8,128)(2,1)S(1)}, bf16[320,1024]{1,0:T(8,128)(2,1)S(1)}, u32[]{:S(2)}, u32[]{:S(2)}) %collective-permute-start.11) | collective-permute-done | bytes 655392 | tf_op jit(solution)/shard_map/ppermute | solution.py:235
  374.9 3.3 shard_map.98
  381.0 1.6 broadcast_select_fusion.9
  383.1 1.6 convolution_convert_fusion
  384.7 4.4 collective-permute-start.14
  389.3 1.5 copy-done.63
  390.8 1.6 convolution_convert_fusion.1
  392.5 2.9 add_convert_fusion
  395.4 2.8 collective-permute-start.15
  398.2 2.9 add_convert_fusion.1
  401.1 2.9 collective-permute-start.13
  404.0 11.6 %all-to-all-start.6 = ((bf16[64,1,72,128]{3,2,1,0:T(8,128)(2,1)}), bf16[64,1,72,128]{3,2,1,0:T(8,128)(2,1)}, u32[]{:S(2)}, u32[]{:S(2)}) async-start(bf16[64,1,72,128]{3,2,1,0:T(8,128)(2,1)} %copy-done.32), calls=%async_computation.6 | async-start | bytes 2359296 | tf_op jit(solution)/shard_map/all_to_all | solution.py:244
  415.5 3.3 shard_map.99
  419.9 3.4 collective-permute-done.15
  423.4 2.9 broadcast_select_fusion
  426.3 25.8 %collective-permute-done.13 = bf16[1792,512]{1,0:T(8,128)(2,1)} collective-permute-done((bf16[1792,512]{1,0:T(8,128)(2,1)}, bf16[1792,512]{1,0:T(8,128)(2,1)}, u32[]{:S(2)}, u32[]{:S(2)}) %collective-permute-start.13) | collective-permute-done | bytes 1835040 | tf_op jit(solution)/shard_map/ppermute | solution.py:239
  452.1 2.9 broadcast_select_fusion.2
  455.0 3.3 shard_map.100
  (188 shorter events, 51.0 us)
Async XLA Ops:
  0.6 95.1 %collective-permute-start.3 = (bf16[512,1792]{1,0:T(8,128)(2,1)}, bf16[512,1792]{1,0:T(8,128)(2,1)}, u32[]{:S(2)}, u32[]{:S(2)}) collective-permute-start(bf16[512,1792]{1,0:T(8,128)(2,1)} %bitcast.47), channel_id=1, source_target_pairs={{1,64},{64,1},{3,66},{66,3},{5,68},{68,5},{7,70},{70,7},{9,72},{72... | collective-permute-start | bytes 5505032 | tf_op jit(solution)/shard_map/ppermute | solution.py:239
  4.4 100.0 %collective-permute-start = (bf16[1792,512]{1,0:T(8,128)(2,1)}, bf16[1792,512]{1,0:T(8,128)(2,1)}, u32[]{:S(2)}, u32[]{:S(2)}) collective-permute-start(bf16[1792,512]{1,0:T(8,128)(2,1)} %bitcast.48), channel_id=1, source_target_pairs={{1,64},{64,1},{3,66},{66,3},{5,68},{68,5},{7,70},{70,7},{9,72},{72... | collective-permute-start | bytes 5505032 | tf_op jit(solution)/shard_map/ppermute | solution.py:239
  7.4 2.0 copy-start.66
  7.4 5.5 %copy-start.67 = (f32[1,2,64,2]{2,3,1,0:T(2,128)S(1)}, f32[1,2,64,2]{2,3,1,0:T(2,128)}, u32[]{:S(2)}) copy-start(f32[1,2,64,2]{2,3,1,0:T(2,128)} %param.11) | copy-start | bytes 3076
  22.6 55.3 %all-to-all-start = ((bf16[64,2,72,128]{3,2,1,0:T(8,128)(2,1)}), bf16[64,2,72,128]{3,2,1,0:T(8,128)(2,1)}, u32[]{:S(2)}, u32[]{:S(2)}) async-start(bf16[64,2,72,128]{3,2,1,0:T(8,128)(2,1)} %copy-done.20), calls=%async_computation | async-start | bytes 4718592 | tf_op jit(solution)/shard_map/cond/branch_1_fun/all_to_all | solution.py:244
  78.4 80.4 %all-to-all-start.1 = ((bf16[64,2,72,128]{3,2,1,0:T(8,128)(2,1)}), bf16[64,2,72,128]{3,2,1,0:T(8,128)(2,1)}, u32[]{:S(2)}, u32[]{:S(2)}) async-start(bf16[64,2,72,128]{3,2,1,0:T(8,128)(2,1)} %get-tuple-element.95), calls=%async_computation.1 | async-start | bytes 4718592 | tf_op jit(solution)/shard_map/all_to_all | solution.py:244
  95.7 8.7 %copy-start.65 = (bf16[1,1,1792,512]{3,2,1,0:T(8,128)(2,1)S(1)}, bf16[1,1,1792,512]{3,2,1,0:T(8,128)(2,1)}, u32[]{:S(2)}) copy-start(bf16[1,1,1792,512]{3,2,1,0:T(8,128)(2,1)} %param.12) | copy-start | bytes 5505028
  98.1 9.7 %copy-start.10 = (bf16[512,1792]{1,0:T(8,128)(2,1)}, bf16[512,1792]{1,0:T(8,128)(2,1)S(1)}, u32[]{:S(2)}) copy-start(bf16[512,1792]{1,0:T(8,128)(2,1)S(1)} %broadcast_select_fusion.1.part0.down0) | copy-start | bytes 5505028
  98.1 9.7 %collective-permute-start.4 = (bf16[512,1792]{1,0:T(8,128)(2,1)S(1)}, bf16[512,1792]{1,0:T(8,128)(2,1)S(1)}, u32[]{:S(2)}, u32[]{:S(2)}) collective-permute-start(bf16[512,1792]{1,0:T(8,128)(2,1)S(1)} %broadcast_select_fusion.1.part0.down0), channel_id=1, source_target_pairs={{0,64},{64,0},{1,65},{65,1},{2,66},{66,2},{3,67},{67,3},{4,68},{68... | collective-permute-start | bytes 5505032 | tf_op jit(solution)/shard_map/ppermute | solution.py:235
  106.2 46.5 %copy-start = (bf16[1792,512]{1,0:T(8,128)(2,1)}, bf16[1792,512]{1,0:T(8,128)(2,1)S(1)}, u32[]{:S(2)}) copy-start(bf16[1792,512]{1,0:T(8,128)(2,1)S(1)} %broadcast_select_fusion.3.part0.up0) | copy-start | bytes 5505028
  106.2 8.6 %collective-permute-start.1 = (bf16[1792,512]{1,0:T(8,128)(2,1)S(1)}, bf16[1792,512]{1,0:T(8,128)(2,1)S(1)}, u32[]{:S(2)}, u32[]{:S(2)}) collective-permute-start(bf16[1792,512]{1,0:T(8,128)(2,1)S(1)} %broadcast_select_fusion.3.part0.up0), channel_id=1, source_target_pairs={{0,64},{64,0},{1,65},{65,1},{2,66},{66,2},{3,67},{67,3},{4,68},{68... | collective-permute-start | bytes 5505032 | tf_op jit(solution)/shard_map/ppermute | solution.py:235
  107.8 5.2 %copy-start.14 = (bf16[512,1792]{1,0:T(8,128)(2,1)}, bf16[512,1792]{1,0:T(8,128)(2,1)S(1)}, u32[]{:S(2)}) copy-start(bf16[512,1792]{1,0:T(8,128)(2,1)S(1)} %collective-permute-done.4.part1.down1) | copy-start | bytes 5505028
  113.0 7.0 %copy-start.35 = (bf16[320,1792]{1,0:T(8,128)(2,1)}, bf16[320,1792]{1,0:T(8,128)(2,1)S(1)}, u32[]{:S(2)}) copy-start(bf16[320,1792]{1,0:T(8,128)(2,1)S(1)} %get-tuple-element.121) | copy-start | bytes 3440644
  113.0 39.7 %copy-start.56 = (bf16[1152,1120]{1,0:T(8,128)(2,1)S(1)}, bf16[1152,1120]{1,0:T(8,128)(2,1)}, u32[]{:S(2)}) copy-start(bf16[1152,1120]{1,0:T(8,128)(2,1)} %fusion.pack_ref.refs_3_) | copy-start | bytes 7741444
  113.0 24.9 %collective-permute-start.5 = (bf16[320,1024]{1,0:T(8,128)(2,1)S(1)}, bf16[320,1024]{1,0:T(8,128)(2,1)S(1)}, u32[]{:S(2)}, u32[]{:S(2)}) collective-permute-start(bf16[320,1024]{1,0:T(8,128)(2,1)S(1)} %get-tuple-element.101), channel_id=1, source_target_pairs={{0,1},{1,0},{2,3},{3,2},{4,5},{5,4},{6,7},{7,6},{8,9},{9,8},{10,11... | collective-permute-start | bytes 1966088 | tf_op jit(solution)/shard_map/ppermute | solution.py:235
  114.9 37.8 %copy-start.5 = (bf16[1792,512]{1,0:T(8,128)(2,1)}, bf16[1792,512]{1,0:T(8,128)(2,1)S(1)}, u32[]{:S(2)}) copy-start(bf16[1792,512]{1,0:T(8,128)(2,1)S(1)} %collective-permute-done.1.part1.up1) | copy-start | bytes 5505028
  121.0 31.7 %collective-permute-start.2 = (bf16[320,1024]{1,0:T(8,128)(2,1)S(1)}, bf16[320,1024]{1,0:T(8,128)(2,1)S(1)}, u32[]{:S(2)}, u32[]{:S(2)}) collective-permute-start(bf16[320,1024]{1,0:T(8,128)(2,1)S(1)} %get-tuple-element.99), channel_id=1, source_target_pairs={{0,1},{1,0},{2,3},{3,2},{4,5},{5,4},{6,7},{7,6},{8,9},{9,8},{10,11... | collective-permute-start | bytes 1966088 | tf_op jit(solution)/shard_map/ppermute | solution.py:235
  158.8 33.8 %all-to-all-start.2 = ((bf16[64,1,72,128]{3,2,1,0:T(8,128)(2,1)}), bf16[64,1,72,128]{3,2,1,0:T(8,128)(2,1)}, u32[]{:S(2)}, u32[]{:S(2)}) async-start(bf16[64,1,72,128]{3,2,1,0:T(8,128)(2,1)} %copy-done.34), calls=%async_computation.2 | async-start | bytes 2359296 | tf_op jit(solution)/shard_map/all_to_all | solution.py:244
  170.1 1.5 copy-start.1
  171.7 1.5 copy-start.6
  173.2 1.5 copy-start.11
  174.7 1.5 copy-start.15
  181.7 6.5 %copy-start.21 = (f32[320,1024]{1,0:T(8,128)}, f32[320,1024]{1,0:T(8,128)S(1)}, u32[]{:S(2)}) copy-start(f32[320,1024]{1,0:T(8,128)S(1)} %get-tuple-element.107.act_own.pre_own) | copy-start | bytes 3932164
  181.7 6.5 %copy-start.39 = (bf16[320,1792]{1,0:T(8,128)(2,1)}, bf16[320,1792]{1,0:T(8,128)(2,1)S(1)}, u32[]{:S(2)}) copy-start(bf16[320,1792]{1,0:T(8,128)(2,1)S(1)} %get-tuple-element.123) | copy-start | bytes 3440644
  181.7 9.8 %copy-start.62 = (bf16[2,64,3584]{2,1,0:T(8,128)(2,1)S(1)}, bf16[2,64,3584]{2,1,0:T(8,128)(2,1)}, u32[]{:S(2)}) copy-start(bf16[2,64,3584]{2,1,0:T(8,128)(2,1)} %param.8) | copy-start | bytes 2752516
  181.7 19.0 %collective-permute-start.7 = (bf16[320,1024]{1,0:T(8,128)(2,1)}, bf16[320,1024]{1,0:T(8,128)(2,1)S(1)}, u32[]{:S(2)}, u32[]{:S(2)}) collective-permute-start(bf16[320,1024]{1,0:T(8,128)(2,1)} %get-tuple-element.108), channel_id=1, source_target_pairs={{0,1},{1,0},{2,3},{3,2},{4,5},{5,4},{6,7},{7,6},{8,9},{9,8},{10,11... | collective-permute-start | bytes 1966088 | tf_op jit(solution)/shard_map/ppermute | solution.py:235
  190.4 24.5 %collective-permute-start.6 = (bf16[320,1024]{1,0:T(8,128)(2,1)}, bf16[320,1024]{1,0:T(8,128)(2,1)}, u32[]{:S(2)}, u32[]{:S(2)}) collective-permute-start(bf16[320,1024]{1,0:T(8,128)(2,1)} %get-tuple-element.106), channel_id=1, source_target_pairs={{0,1},{1,0},{2,3},{3,2},{4,5},{5,4},{6,7},{7,6},{8,9},{9,8},{10,11... | collective-permute-start | bytes 1966088 | tf_op jit(solution)/shard_map/ppermute | solution.py:235
  197.6 28.5 %collective-permute-start.8 = (bf16[64,3584]{1,0:T(8,128)(2,1)}, bf16[64,3584]{1,0:T(8,128)(2,1)}, u32[]{:S(2)}, u32[]{:S(2)}) collective-permute-start(bf16[64,3584]{1,0:T(8,128)(2,1)} %shard_map.88), channel_id=1, source_target_pairs={{128,0},{129,1},{130,2},{131,3},{132,4},{133,5},{134,6},{135,7},{1... | collective-permute-start | bytes 1376264 | tf_op jit(solution)/shard_map/ppermute | solution.py:299
  214.9 1.5 copy-start.2
  220.5 5.6 %copy-start.57 = (bf16[1152,1120]{1,0:T(8,128)(2,1)S(1)}, bf16[1152,1120]{1,0:T(8,128)(2,1)}, u32[]{:S(2)}) copy-start(bf16[1152,1120]{1,0:T(8,128)(2,1)} %fusion.pack_ref.refs_3_) | copy-start | bytes 7741444
  226.1 3.6 copy-start.46
  226.1 3.6 copy-start.48
  229.8 33.3 %copy-start.28 = (bf16[64,3584]{1,0:T(8,128)(2,1)S(1)}, bf16[64,3584]{1,0:T(8,128)(2,1)}, u32[]{:S(2)}) copy-start(bf16[64,3584]{1,0:T(8,128)(2,1)} %get-tuple-element.189.incoming) | copy-start | bytes 1376260
  263.1 2.7 copy-start.18
  265.8 12.4 %collective-permute-start.9 = (bf16[64,3584]{1,0:T(8,128)(2,1)}, bf16[64,3584]{1,0:T(8,128)(2,1)}, u32[]{:S(2)}, u32[]{:S(2)}) collective-permute-start(bf16[64,3584]{1,0:T(8,128)(2,1)} %shard_map.93), channel_id=1, source_target_pairs={{128,0},{129,1},{130,2},{131,3},{132,4},{133,5},{134,6},{135,7},{1... | collective-permute-start | bytes 1376264 | tf_op jit(solution)/shard_map/ppermute | solution.py:304
  268.1 1.5 copy-start.12
  269.7 1.5 copy-start.16
  272.4 5.8 %copy-start.58 = (bf16[1152,1120]{1,0:T(8,128)(2,1)S(1)}, bf16[1152,1120]{1,0:T(8,128)(2,1)}, u32[]{:S(2)}) copy-start(bf16[1152,1120]{1,0:T(8,128)(2,1)} %fusion.pack_ref.refs_3_) | copy-start | bytes 7741444
  282.5 44.6 %all-to-all-start.4 = ((bf16[64,1,72,128]{3,2,1,0:T(8,128)(2,1)}), bf16[64,1,72,128]{3,2,1,0:T(8,128)(2,1)}, u32[]{:S(2)}, u32[]{:S(2)}) async-start(bf16[64,1,72,128]{3,2,1,0:T(8,128)(2,1)} %copy-done.27), calls=%async_computation.4 | async-start | bytes 2359296 | tf_op jit(solution)/shard_map/all_to_all | solution.py:244
  291.7 21.7 %collective-permute-start.10 = (bf16[320,1024]{1,0:T(8,128)(2,1)}, bf16[320,1024]{1,0:T(8,128)(2,1)S(1)}, u32[]{:S(2)}, u32[]{:S(2)}) collective-permute-start(bf16[320,1024]{1,0:T(8,128)(2,1)} %copy-done.55), channel_id=1, source_target_pairs={{0,1},{1,0},{2,3},{3,2},{4,5},{5,4},{6,7},{7,6},{8,9},{9,8},{10,11... | collective-permute-start | bytes 1966088 | tf_op jit(solution)/shard_map/ppermute | solution.py:235
  313.4 1.5 copy-start.3
  314.9 1.5 copy-start.8
  327.2 53.9 %all-to-all-start.5 = ((bf16[64,1,72,128]{3,2,1,0:T(8,128)(2,1)}), bf16[64,1,72,128]{3,2,1,0:T(8,128)(2,1)}, u32[]{:S(2)}, u32[]{:S(2)}) async-start(bf16[64,1,72,128]{3,2,1,0:T(8,128)(2,1)} %copy-done.33), calls=%async_computation.5 | async-start | bytes 2359296 | tf_op jit(solution)/shard_map/all_to_all | solution.py:244
  345.9 1.8 copy-start.13
  347.7 1.5 copy-start.17
  349.2 5.5 %copy-start.38 = (bf16[320,1792]{1,0:T(8,128)(2,1)S(1)}, bf16[320,1792]{1,0:T(8,128)(2,1)}, u32[]{:S(2)}) copy-start(bf16[320,1792]{1,0:T(8,128)(2,1)} %copy-done.37) | copy-start | bytes 3440644
  349.2 5.5 %copy-start.40 = (bf16[320,1792]{1,0:T(8,128)(2,1)S(1)}, bf16[320,1792]{1,0:T(8,128)(2,1)}, u32[]{:S(2)}) copy-start(bf16[320,1792]{1,0:T(8,128)(2,1)} %copy-done.39) | copy-start | bytes 3440644
  349.2 5.5 %copy-start.42 = (bf16[320,1792]{1,0:T(8,128)(2,1)S(1)}, bf16[320,1792]{1,0:T(8,128)(2,1)}, u32[]{:S(2)}) copy-start(bf16[320,1792]{1,0:T(8,128)(2,1)} %copy-done.41) | copy-start | bytes 3440644
  353.5 21.4 %collective-permute-start.11 = (bf16[320,1024]{1,0:T(8,128)(2,1)S(1)}, bf16[320,1024]{1,0:T(8,128)(2,1)S(1)}, u32[]{:S(2)}, u32[]{:S(2)}) collective-permute-start(bf16[320,1024]{1,0:T(8,128)(2,1)S(1)} %get-tuple-element.118), channel_id=1, source_target_pairs={{0,1},{1,0},{2,3},{3,2},{4,5},{5,4},{6,7},{7,6},{8,9},{9,8},{10,11... | collective-permute-start | bytes 1966088 | tf_op jit(solution)/shard_map/ppermute | solution.py:235
  355.0 19.9 %copy-start.23 = (f32[320,1024]{1,0:T(8,128)S(1)}, f32[320,1024]{1,0:T(8,128)}, u32[]{:S(2)}) copy-start(f32[320,1024]{1,0:T(8,128)} %copy-done.21) | copy-start | bytes 3932164
  355.0 19.9 %copy-start.59 = (bf16[1152,1120]{1,0:T(8,128)(2,1)S(1)}, bf16[1152,1120]{1,0:T(8,128)(2,1)}, u32[]{:S(2)}) copy-start(bf16[1152,1120]{1,0:T(8,128)(2,1)} %fusion.pack_ref.refs_3_) | copy-start | bytes 7741444
  356.6 18.3 %copy-start.4 = (bf16[1792,512]{1,0:T(8,128)(2,1)S(1)}, bf16[1792,512]{1,0:T(8,128)(2,1)}, u32[]{:S(2)}) copy-start(bf16[1792,512]{1,0:T(8,128)(2,1)} %copy-done) | copy-start | bytes 5505028
  356.6 18.3 %copy-start.9 = (bf16[1792,512]{1,0:T(8,128)(2,1)S(1)}, bf16[1792,512]{1,0:T(8,128)(2,1)}, u32[]{:S(2)}) copy-start(bf16[1792,512]{1,0:T(8,128)(2,1)} %copy-done.5) | copy-start | bytes 5505028
  381.0 2.0 copy-start.64
  383.1 6.0 %copy-start.44 = (bf16[320,1024]{1,0:T(8,128)(2,1)S(1)}, bf16[320,1024]{1,0:T(8,128)(2,1)}, u32[]{:S(2)}) copy-start(bf16[320,1024]{1,0:T(8,128)(2,1)} %copy-done.43) | copy-start | bytes 1966084
  383.1 6.0 %copy-start.47 = (bf16[320,1024]{1,0:T(8,128)(2,1)S(1)}, bf16[320,1024]{1,0:T(8,128)(2,1)}, u32[]{:S(2)}) copy-start(bf16[320,1024]{1,0:T(8,128)(2,1)} %copy-done.46) | copy-start | bytes 1966084
  383.1 6.0 %copy-start.50 = (bf16[320,1024]{1,0:T(8,128)(2,1)S(1)}, bf16[320,1024]{1,0:T(8,128)(2,1)}, u32[]{:S(2)}) copy-start(bf16[320,1024]{1,0:T(8,128)(2,1)} %copy-done.49) | copy-start | bytes 1966084
  383.1 6.0 %copy-start.53 = (bf16[320,1024]{1,0:T(8,128)(2,1)S(1)}, bf16[320,1024]{1,0:T(8,128)(2,1)}, u32[]{:S(2)}) copy-start(bf16[320,1024]{1,0:T(8,128)(2,1)} %copy-done.52) | copy-start | bytes 1966084
  384.7 7.8 %collective-permute-start.14 = (bf16[512,1792]{1,0:T(8,128)(2,1)S(1)}, bf16[512,1792]{1,0:T(8,128)(2,1)S(1)}, u32[]{:S(2)}, u32[]{:S(2)}) collective-permute-start(bf16[512,1792]{1,0:T(8,128)(2,1)S(1)} %convolution_convert_fusion), channel_id=1, source_target_pairs={{0,64},{64,0},{1,65},{65,1},{2,66},{66,2},{3,67},{67,3},{4,68},{68... | collective-permute-start | bytes 5505032 | tf_op jit(solution)/shard_map/ppermute | solution.py:235
  389.1 1.6 copy-start.63
  392.4 5.8 %collective-permute-start.12 = (bf16[1792,512]{1,0:T(8,128)(2,1)S(1)}, bf16[1792,512]{1,0:T(8,128)(2,1)S(1)}, u32[]{:S(2)}, u32[]{:S(2)}) collective-permute-start(bf16[1792,512]{1,0:T(8,128)(2,1)S(1)} %convolution_convert_fusion.1), channel_id=1, source_target_pairs={{0,64},{64,0},{1,65},{65,1},{2,66},{66,2},{3,67},{67,3},{4,68},{68... | collective-permute-start | bytes 5505032 | tf_op jit(solution)/shard_map/ppermute | solution.py:235
  395.4 28.0 %collective-permute-start.15 = (bf16[512,1792]{1,0:T(8,128)(2,1)}, bf16[512,1792]{1,0:T(8,128)(2,1)}, u32[]{:S(2)}, u32[]{:S(2)}) collective-permute-start(bf16[512,1792]{1,0:T(8,128)(2,1)} %add_convert_fusion), channel_id=1, source_target_pairs={{1,64},{64,1},{3,66},{66,3},{5,68},{68,5},{7,70},{70,7},{9,72},{72... | collective-permute-start | bytes 5505032 | tf_op jit(solution)/shard_map/ppermute | solution.py:239
  401.1 51.0 %collective-permute-start.13 = (bf16[1792,512]{1,0:T(8,128)(2,1)}, bf16[1792,512]{1,0:T(8,128)(2,1)}, u32[]{:S(2)}, u32[]{:S(2)}) collective-permute-start(bf16[1792,512]{1,0:T(8,128)(2,1)} %add_convert_fusion.1), channel_id=1, source_target_pairs={{1,64},{64,1},{3,66},{66,3},{5,68},{68,5},{7,70},{70,7},{9,72},{72... | collective-permute-start | bytes 5505032 | tf_op jit(solution)/shard_map/ppermute | solution.py:239
  404.0 51.1 %all-to-all-start.6 = ((bf16[64,1,72,128]{3,2,1,0:T(8,128)(2,1)}), bf16[64,1,72,128]{3,2,1,0:T(8,128)(2,1)}, u32[]{:S(2)}, u32[]{:S(2)}) async-start(bf16[64,1,72,128]{3,2,1,0:T(8,128)(2,1)} %copy-done.32), calls=%async_computation.6 | async-start | bytes 2359296 | tf_op jit(solution)/shard_map/all_to_all | solution.py:244
  (26 other events, 27.9 us)

commit v2 on v1

v2 whole, which is shorter than its diff:
```python
import functools

import jax
import jax.numpy as jnp
from jax import lax
from jax.experimental import pallas as pl
from jax.experimental.pallas import tpu as pltpu
from jax.sharding import Mesh, PartitionSpec as P

BF = jnp.bfloat16
F32 = jnp.float32
LANES = 128
GROUP = 16
VMEM_BYTES = 56 << 20
CAP = 5
PAIRED = ("pair", "half")
ROWS = GROUP * CAP
NT = (((1,), (1,)), ((), ()))


def staged_call(body, inputs, small, outs, scratch=()):
    outs_flat = [outs] if isinstance(outs, jax.ShapeDtypeStruct) else list(outs)
    n_in, n_small, n_out = len(inputs), len(small), len(outs_flat)
    held = []
    for array, index in inputs:
        shape = tuple(size for size, at in zip(array.shape, index) if isinstance(at, slice)) + array.shape[len(index) :]
        held.append(pltpu.VMEM(shape, array.dtype))

    def kernel(*refs):
        sources, refs = refs[:n_in], refs[n_in:]
        little, refs = refs[:n_small], refs[n_small:]
        targets, refs = refs[:n_out], refs[n_out:]
        taken, refs = refs[:n_in], refs[n_in:]
        made, refs = refs[:n_out], refs[n_out:]
        in_sems, out_sems, rest = refs[0], refs[1], refs[2:]
        loads = [
            pltpu.make_async_copy(ref.at[index] if index else ref, here, in_sems.at[i])
            for i, (ref, (_, index), here) in enumerate(zip(sources, inputs, taken))
        ]
        stores = [pltpu.make_async_copy(here, ref, out_sems.at[i]) for i, (here, ref) in enumerate(zip(made, targets))]
        for load in loads:
            load.start()
        body(taken, lambda i: loads[i].wait(), little, made, lambda i: stores[i].start(), rest)
        for store in stores:
            store.wait()

    anywhere, vmem = pl.BlockSpec(memory_space=pl.ANY), pl.BlockSpec(memory_space=pltpu.VMEM)
    result = pl.pallas_call(
        kernel,
        out_shape=outs_flat,
        in_specs=[anywhere] * n_in + [vmem] * n_small,
        out_specs=[anywhere] * n_out,
        scratch_shapes=held
        + [pltpu.VMEM(out.shape, out.dtype) for out in outs_flat]
        + [pltpu.SemaphoreType.DMA((n_in,)), pltpu.SemaphoreType.DMA((n_out,))]
        + list(scratch),
        cost_estimate=pl.CostEstimate(flops=1, bytes_accessed=1, transcendentals=0),
        compiler_params=pltpu.CompilerParams(vmem_limit_bytes=VMEM_BYTES),
    )(*[array for array, _ in inputs], *small)
    return result[0] if isinstance(outs, jax.ShapeDtypeStruct) else tuple(result)


def dot(a, b, dims=(((1,), (0,)), ((), ()))):
    return lax.dot_general(a, b, dims, preferred_element_type=F32)


def pack(source, starts, pack_ref, mixed, store):
    blocks = mixed.shape[0] // ROWS
    for side, (row, col) in enumerate(starts):
        for block in range(blocks):
            mixed[block * ROWS : (block + 1) * ROWS, side * LANES : (side + 1) * LANES] = source[
                row : row + ROWS, col + block * LANES : col + (block + 1) * LANES
            ]
    chunks = dot(pack_ref[...], mixed[...])
    high = chunks.shape[0] // GROUP
    for side in range(2):
        for item in range(GROUP):
            store(
                side,
                item,
                chunks[item * high : (item + 1) * high, side * LANES : (side + 1) * LANES].astype(BF),
            )


def unpack(load, unpack_ref, stage, target, starts):
    high = stage.shape[0] // GROUP
    for side in range(2):
        for item in range(GROUP):
            stage[item * high : (item + 1) * high, side * LANES : (side + 1) * LANES] = load(side, item).astype(F32)
    mixed = dot(unpack_ref[...], stage[...].astype(BF))
    for side, (row, col) in enumerate(starts):
        for block in range(mixed.shape[0] // ROWS):
            target[row : row + ROWS, col + block * LANES : col + (block + 1) * LANES] = mixed[
                block * ROWS : (block + 1) * ROWS, side * LANES : (side + 1) * LANES
            ].astype(BF)


def dispatch(values, places, weights, packer, chunk_rows):
    count, width = len(values), values[0][0].shape[-1]
    slot_count = places[0].shape[0]

    def body(taken, wait, little, made, put, scratch):
        slots, mixed = scratch
        pack_ref, out = taken[count], made[0]
        for index in range(count):
            wait(index)
            place, weight = little[index], little[count + index]
            slots[...] = (dot(place[...], taken[index][...]) * weight[...]).astype(BF)
            if index == 0:
                wait(count)
            for group in range(slot_count // ROWS):

                def store(side, item, chunk, index=index, group=group):
                    out[(group * GROUP + item) * 2 + side, index] = chunk

                pack(slots, [(group * ROWS, 0), (group * ROWS, width // 2)], pack_ref, mixed, store)
        put(0)

    return staged_call(
        body,
        [*values, (packer, ())],
        [*places, *weights],
        jax.ShapeDtypeStruct((2 * slot_count // CAP, count, chunk_rows, LANES), BF),
        [pltpu.VMEM((slot_count, width), BF), pltpu.VMEM((packer.shape[1], 2 * LANES), BF)],
    )


def arrive(got, index, unpacker, parts):
    hidden, width, total = 2 * min(parts[0].shape), max(parts[0].shape), got.shape[0] * CAP
    dims = NT if parts[0].shape[1] == width else (((1,), (0,)), ((), ()))

    def body(taken, wait, little, made, put, scratch):
        chunks, unpack_ref, *weights = taken
        rows, own, sent = made
        wait(0)
        wait(1)
        for pair in range(chunks.shape[0] // (2 * GROUP)):

            def load(side, item, pair=pair):
                return chunks[(2 * pair + side) * GROUP + item]

            unpack(load, unpack_ref, scratch[0], rows, [(2 * pair * ROWS, 0), ((2 * pair + 1) * ROWS, 0)])
        put(0)
        for number, part in enumerate(weights):
            wait(2 + number)
            product = dot(rows[...], part[...], dims)
            columns = slice(number * hidden // 2, (number + 1) * hidden // 2)
            own[:, columns] = product
            sent[:, columns] = product.astype(BF)
        put(2)
        put(1)

    return staged_call(
        body,
        [(got, (slice(None), index)), (unpacker, ()), (parts[0], ()), (parts[1], ())],
        [],
        (
            jax.ShapeDtypeStruct((total, width), BF),
            jax.ShapeDtypeStruct((total, hidden), F32),
            jax.ShapeDtypeStruct((total, hidden), BF),
        ),
        [pltpu.VMEM((unpacker.shape[1], 2 * LANES), F32)],
    )


def turn(pre_own, pre_got, act_own, act_got, ups, packer, chunk_rows):
    total, hidden = pre_own.shape
    width = ups[0].shape[0]

    def body(taken, wait, little, made, put, scratch):
        pre_here, pre_there, act_here, act_there, up0, up1, pack_ref = taken
        active, grads, out = made
        rows, mixed = scratch
        wait(0)
        wait(1)
        pre = pre_here[...] + pre_there[...].astype(F32)
        gate = 1.0 / (1.0 + jnp.exp(-pre))
        active[...] = (pre * gate).astype(BF)
        put(0)
        slope = gate * (1.0 + pre * (1.0 - gate))
        wait(2)
        wait(3)
        grads[...] = ((act_here[...] + act_there[...].astype(F32)) * slope).astype(BF)
        put(1)
        wait(4)
        wait(5)
        rows[...] = (dot(grads[:, : hidden // 2], up0[...], NT) + dot(grads[:, hidden // 2 :], up1[...], NT)).astype(BF)
        wait(6)
        for pair in range(out.shape[0] // (2 * GROUP)):

            def store(side, item, chunk, pair=pair):
                out[(2 * pair + side) * GROUP + item, 0] = chunk

            pack(rows, [(2 * pair * ROWS, 0), ((2 * pair + 1) * ROWS, 0)], pack_ref, mixed, store)
        put(2)

    kept = jax.ShapeDtypeStruct((total, hidden), BF)
    return staged_call(
        body,
        [(array, ()) for array in (pre_own, pre_got, act_own, act_got, *ups, packer)],
        [],
        (kept, kept, jax.ShapeDtypeStruct((total // CAP, 1, chunk_rows, LANES), BF)),
        [pltpu.VMEM((total, width), BF), pltpu.VMEM((packer.shape[1], 2 * LANES), BF)],
    )


def combine(got, unpacker, place_t, incoming):
    array, index = incoming
    tokens, width = array.shape[-2:]

    def body(taken, wait, little, made, put, scratch):
        chunks, unpack_ref, base = taken
        slots, stage = scratch
        wait(0)
        wait(1)
        for group in range(slots.shape[0] // ROWS):

            def load(side, item, group=group):
                return chunks[(group * GROUP + item) * 2 + side]

            unpack(load, unpack_ref, stage, slots, [(group * ROWS, 0), (group * ROWS, width // 2)])
        wait(2)
        made[0][...] = (dot(little[0][...], slots[...]) + base[...].astype(F32)).astype(BF)
        put(0)

    return staged_call(
        body,
        [(got, (slice(None), 0)), (unpacker, ()), incoming],
        [place_t],
        jax.ShapeDtypeStruct((tokens, width), BF),
        [pltpu.VMEM((place_t.shape[1], width), BF), pltpu.VMEM((unpacker.shape[1], 2 * LANES), F32)],
    )


def slots_of(routes, gates, experts):
    tokens, top = routes.shape
    flat = routes.reshape(-1)
    order = jnp.arange(tokens * top, dtype=jnp.int32)
    earlier = (flat[:, None] == flat[None, :]) & (order[None, :] < order[:, None])
    slot = flat * CAP + jnp.sum(earlier.astype(jnp.int32), axis=1)
    hits = slot.reshape(tokens, top)[None] == jnp.arange(experts * CAP, dtype=jnp.int32)[:, None, None]
    place = jnp.any(hits, axis=2)
    weight = jnp.sum(jnp.where(hits, gates[None], 0.0), axis=(1, 2))
    return place.astype(BF), weight[:, None]


def packing(blocks, chunk_rows):
    total = GROUP * chunk_rows
    row = jnp.arange(total, dtype=jnp.int32)
    col = jnp.arange(blocks * ROWS, dtype=jnp.int32)
    item, place = row // chunk_rows, row % chunk_rows
    block, inner = place // CAP, place % CAP
    wanted = jnp.where(block < blocks, block * ROWS + item * CAP + inner, -1)
    return (wanted[:, None] == col[None, :]).astype(BF), (wanted[None, :] == col[:, None]).astype(BF)


def swap(value, axis):
    return lax.ppermute(value, axis, [(0, 1), (1, 0)])


def cross(value):
    moved = lax.ppermute(value, ("dp", "half"), [(1, 2), (2, 1)])
    return jnp.where(lax.axis_index("dp") == lax.axis_index("half"), value, moved)


def send(chunks):
    return lax.all_to_all(chunks, PAIRED, split_axis=0, concat_axis=0, tiled=True)


def on_device(grad_out, layer_in, routes, gates, w_up, w_down):
    section = lax.axis_index("section")
    top_section = section == lax.axis_size("section") - 1
    experts = lax.axis_size("pair")
    width = grad_out.shape[2]
    blocks = width // (2 * LANES)
    chunk_rows = -(-blocks * CAP // 8) * 8
    packer, unpacker = packing(blocks, chunk_rows)

    place, weight = zip(*[slots_of(routes[0, micro], gates[0, micro], experts) for micro in range(2)])
    place_t = [p.T for p in place]
    ones = jnp.ones_like(weight[0])
    inputs = [(layer_in, (0, 0)), (layer_in, (0, 1))]
    outer = [(grad_out, (0,)), (grad_out, (1,))]

    up_here, down_here = cross(w_up[0, 0]), cross(w_down[0, 0])
    ups = (up_here, swap(up_here, "dp"))
    downs = (down_here, swap(down_here, "dp"))

    def pick(here, there):
        return jnp.where(top_section, here, there)

    def prepare(values, places, weights):
        return dispatch(values, places, weights, packer, chunk_rows)

    def top_start():
        first = send(prepare([inputs[0], outer[0]], [place[0]] * 2, [ones, weight[0]]))
        return first, prepare([inputs[1], outer[1]], [place[1]] * 2, [ones, weight[1]])

    def low_start():
        chunks = prepare(inputs, place, [ones, ones])
        return jnp.zeros_like(chunks), chunks

    first, second_chunks = lax.cond(top_section, top_start, low_start)
    first, second_chunks, unpacker = lax.optimization_barrier((first, second_chunks, unpacker))
    second = send(second_chunks)

    rows_a0, own_a0, sent_a0 = arrive(first, 0, unpacker, ups)
    got_a0 = swap(sent_a0, "half")
    rows_a1, own_a1, sent_a1 = arrive(first, 1, unpacker, downs)
    got_a1 = swap(sent_a1, "half")
    top_active0, top_grads0, back0 = turn(own_a0, got_a0, own_a1, got_a1, ups, packer, chunk_rows)
    second, back0 = lax.optimization_barrier((second, back0))
    third = send(back0)

    rows_b0, own_b0, sent_b0 = arrive(second, 0, unpacker, ups)
    got_b0 = swap(sent_b0, "half")
    rows_b1, own_b1, sent_b1 = lax.cond(
        top_section, lambda: arrive(second, 1, unpacker, downs), lambda: arrive(second, 1, unpacker, ups)
    )
    got_b1 = swap(sent_b1, "half")
    top_active1, top_grads1, back1 = turn(own_b0, got_b0, own_b1, got_b1, ups, packer, chunk_rows)

    top_out0 = combine(third, unpacker, place_t[0], outer[0])
    low_in0 = lax.ppermute(top_out0, "section", [(1, 0)])
    fourth_chunks = pick(back1, dispatch([(low_in0, ())], [place[0]], [weight[0]], packer, chunk_rows))
    rows_in0, rows_in1 = pick(rows_a0, rows_b0), pick(rows_b0, rows_b1)
    fourth = send(fourth_chunks)
    top_out1 = combine(fourth, unpacker, place_t[1], outer[1])
    low_in1 = lax.ppermute(top_out1, "section", [(1, 0)])
    rows_d, own_d, sent_d = arrive(fourth, 0, unpacker, downs)
    low_in1, sent_d = lax.optimization_barrier((low_in1, sent_d))
    got_d = swap(sent_d, "half")

    fifth = send(dispatch([(low_in1, ())], [place[1]], [weight[1]], packer, chunk_rows))
    low_active0, low_grads0, back2 = turn(own_b0, got_b0, own_d, got_d, ups, packer, chunk_rows)
    fifth, back2 = lax.optimization_barrier((fifth, back2))
    sixth = send(back2)
    rows_e, own_e, sent_e = arrive(fifth, 0, unpacker, downs)
    got_e = swap(sent_e, "half")
    low_active1, low_grads1, back3 = turn(own_b1, got_b1, own_e, got_e, ups, packer, chunk_rows)
    seventh = send(back3)

    def both(top0, top1, low0, low1):
        return jnp.concatenate([pick(top0, low0), pick(top1, low1)])

    hidden = own_a0.shape[1] // 2
    over = (((0,), (0,)), ((), ()))
    rows = jnp.concatenate([rows_in0, rows_in1])
    scaled = both(rows_a1, rows_b1, rows_d, rows_e)
    sixth, low_active1, low_grads1, scaled, rows = lax.optimization_barrier(
        (sixth, low_active1, low_grads1, scaled, rows)
    )
    active = both(top_active0, top_active1, low_active0, low_active1)
    grads = both(top_grads0, top_grads1, low_grads0, low_grads1)
    other_up = swap(dot(rows, grads[:, hidden:], over).astype(BF), "dp")
    other_down = swap(dot(active[:, hidden:], scaled, over).astype(BF), "dp")
    grad_up = (dot(rows, grads[:, :hidden], over) + other_up.astype(F32)).astype(BF)
    grad_down = (dot(active[:, :hidden], scaled, over) + other_down.astype(F32)).astype(BF)
    grad_up, grad_down = cross(grad_up), cross(grad_down)
    seventh, grad_up, grad_down = lax.optimization_barrier((seventh, grad_up, grad_down))
    low_out0 = combine(sixth, unpacker, place_t[0], (low_in0, ()))
    low_out1 = combine(seventh, unpacker, place_t[1], (low_in1, ()))
    results = jnp.stack([pick(top_out0, low_out0), pick(top_out1, low_out1)])
    return results[None], grad_up[None, None], grad_down[None, None]


def solution(mesh):
    sizes = dict(zip(mesh.axis_names, mesh.devices.shape))
    fine = Mesh(
        mesh.devices.reshape(sizes["section"], sizes["dp"], sizes["expert"] // 2, 2),
        ("section", "dp", "pair", "half"),
    )
    tokens = P("section", None, ("dp", "pair", "half"), None)
    up, down = P("section", PAIRED, "dp", None), P("section", PAIRED, None, "dp")
    return jax.shard_map(
        on_device,
        mesh=fine,
        in_specs=(P(None, ("dp", "pair", "half"), None), tokens, tokens, tokens, up, down),
        out_specs=(tokens, up, down),
        check_vma=False,
    )
```

time: 470 us -> 475 us (1.011)
  the two profiles are of different devices: /device:TPU:35 before, /device:TPU:1 now
where the time goes in v2:
time: 475 us; the launch traced here: 466 us
  waiting for transfers between devices  179 us (38%)
  Pallas kernels  106 us (22%)
  starting transfers between devices  86.4 us (18%)
  blocking collectives  33 us (7%)
  other arithmetic  28.4 us (6%)
  local copies, waits for them, and re-layouts  13.1 us (3%)
  loops' own time  9.06 us (2%)
  matrix products  8.96 us (2%)
    pallas_call x17, Pallas kernels, staged_call(): pl.pallas_call(kernel, out_shape=outs_flat, in_specs=[anywhere] * n_in +...  106 us
    ppermute x10, waiting for transfers between devices, swap(): return lax.ppermute(value, axis, [(0, 1), (1, 0)])  91.7 us
    all_to_all x5, starting transfers between devices, send(): lax.all_to_all(chunks, PAIRED, split_axis=0, concat_axis=0, tiled=True)  62.2 us
    all_to_all x1, blocking collectives, send(): lax.all_to_all(chunks, PAIRED, split_axis=0, concat_axis=0, tiled=True)  33 us
    ppermute x1, waiting for transfers between devices, on_device(): low_in0 = lax.ppermute(top_out0, 'section', [(1, 0)])  31.3 us
    ppermute x4, waiting for transfers between devices, cross(): moved = lax.ppermute(value, ('dp', 'half'), [(1, 2), (2, 1)])  27.7 us
    ppermute x1, waiting for transfers between devices, on_device(): low_in1 = lax.ppermute(top_out1, 'section', [(1, 0)])  15.8 us
    all_to_all x5, waiting for transfers between devices, send(): lax.all_to_all(chunks, PAIRED, split_axis=0, concat_axis=0, tiled=True)  12.5 us
  transfers between devices with their start and end apart: 21, of which 12 were waited for; matrix products, arithmetic and copies ran while one was open for 9% of the time, Pallas kernels for 18%

profile of v2, /device:TPU:1, one launch (start us, length us, event | category | flops | bytes accessed | tf_op | source)
XLA Modules:
  0.0 465.8 jit_solution(2416723590272232023)
XLA Ops:
  0.6 4.6 collective-permute-start.3
  5.2 1.9 collective-permute-start
  8.3 2.0 fusion.refs_6_.refs_1_
  13.3 21.9 %conditional.2 = (bf16[64,2,72,128]{3,2,1,0:T(8,128)(2,1)}, bf16[64,2,72,128]{3,2,1,0:T(8,128)(2,1)}) conditional(s32[]{:T(128)} %convert_element_type.64, (bf16[1,2,64,3584]{3,2,1,0:T(8,128)(2,1)S(1)}, bf16[1152,1120]{1,0:T(8,128)(2,1)}, bf16[160,64]{0,1:T(8,128)(2,1)}, bf16[160,64]{0,1:T(8,128)(2,1)S(1)}) %tuple.63, ...), branch_computations={%region_6.7_spmd, %region_7.8_spmd} | conditional | flops 2 | bytes 7163062 | solution.py:303
  14.0 1.5 copy.45.refs_3_
  16.1 8.8 %branch_0_fun.2 = bf16[64,2,72,128]{3,2,1,0:T(8,128)(2,1)} custom-call(bf16[1,2,64,3584]{3,2,1,0:T(8,128)(2,1)S(1)} %get-tuple-element.33.refs_0_.refs_1_, bf16[1,2,64,3584]{3,2,1,0:T(8,128)(2,1)S(1)} %get-tuple-element.33.refs_0_.refs_1_, bf16[1152,1120]{1,0:T(8,128)(2,1)} %get-tuple-element.40.refs_2_, bf16[160,64]{1,0:T(8,128)(2,1)} %copy.45.refs_3_, ...), custom_call_target="tpu_custom_call" | custom-call | flops 1 | bytes 1 | tf_op jit(solution)/shard_map/cond/branch_0_fun/pallas_call | solution.py:48
  24.9 1.7 broadcast.173
  35.2 14.4 %all-to-all-start.1 = ((bf16[64,2,72,128]{3,2,1,0:T(8,128)(2,1)}), bf16[64,2,72,128]{3,2,1,0:T(8,128)(2,1)}, u32[]{:S(2)}, u32[]{:S(2)}) async-start(bf16[64,2,72,128]{3,2,1,0:T(8,128)(2,1)} %get-tuple-element.113), calls=%async_computation.1 | async-start | bytes 4718592 | tf_op jit(solution)/shard_map/all_to_all | solution.py:267
  49.6 2.4 broadcast_select_fusion.1.refs_2_
  52.3 2.0 broadcast_select_fusion.3.refs_2_.refs_4_
  54.4 1.4 collective-permute-done.4.refs_3_
  55.9 6.5 %shard_map.86 = (bf16[320,1792]{1,0:T(8,128)(2,1)}, f32[320,1024]{1,0:T(8,128)}, bf16[320,1024]{1,0:T(8,128)(2,1)}) custom-call(bf16[64,2,72,128]{3,2,1,0:T(8,128)(2,1)} %get-tuple-element.114.refs_0_, bf16[1120,1152]{1,0:T(8,128)(2,1)S(1)} %fusion.1.refs_1_, bf16[512,1792]{1,0:T(8,128)(2,1)S(1)} %broadcast_select_fusion.1.refs_2_, ...), custom_call_target="tpu_custom_call" | custom-call | flops 1 | bytes 1 | tf_op jit(solution)/shard_map/pallas_call | solution.py:48
  62.4 1.7 collective-permute-start.5
  64.1 5.8 %shard_map.85 = (bf16[320,1792]{1,0:T(8,128)(2,1)}, f32[320,1024]{1,0:T(8,128)}, bf16[320,1024]{1,0:T(8,128)(2,1)}) custom-call(bf16[64,2,72,128]{3,2,1,0:T(8,128)(2,1)} %get-tuple-element.114.refs_0_, bf16[1120,1152]{1,0:T(8,128)(2,1)S(1)} %fusion.1.refs_1_, bf16[1792,512]{1,0:T(8,128)(2,1)S(1)} %broadcast_select_fusion.3.refs_2_.refs_4_, ...), custom_call_target="tpu_custom_call" | custom-call | flops 1 | bytes 1 | tf_op jit(solution)/shard_map/pallas_call | solution.py:48
  70.2 26.3 %collective-permute-done.5.refs_3_ = bf16[320,1024]{1,0:T(8,128)(2,1)S(1)} collective-permute-done((bf16[320,1024]{1,0:T(8,128)(2,1)}, bf16[320,1024]{1,0:T(8,128)(2,1)S(1)}, u32[]{:S(2)}, u32[]{:S(2)}) %collective-permute-start.5) | collective-permute-done | bytes 655392 | tf_op jit(solution)/shard_map/ppermute | solution.py:258
  96.4 15.2 %collective-permute-done.2.refs_1_ = bf16[320,1024]{1,0:T(8,128)(2,1)} collective-permute-done((bf16[320,1024]{1,0:T(8,128)(2,1)}, bf16[320,1024]{1,0:T(8,128)(2,1)}, u32[]{:S(2)}, u32[]{:S(2)}) %collective-permute-start.2) | collective-permute-done | bytes 655392 | tf_op jit(solution)/shard_map/ppermute | solution.py:258
  111.6 7.4 %shard_map.87 = (bf16[320,1024]{1,0:T(8,128)(2,1)}, bf16[320,1024]{1,0:T(8,128)(2,1)}, bf16[64,1,72,128]{3,2,1,0:T(8,128)(2,1)}) custom-call(f32[320,1024]{1,0:T(8,128)} %get-tuple-element.116.refs_0_, bf16[320,1024]{1,0:T(8,128)(2,1)} %collective-permute-done.2.refs_1_, f32[320,1024]{1,0:T(8,128)} %get-tuple-element.118.refs_2_, ...), custom_call_target="tpu_custom_call" | custom-call | flops 1 | bytes 1 | tf_op jit(solution)/shard_map/pallas_call | solution.py:48
  119.0 10.3 %all-to-all-start.2 = ((bf16[64,1,72,128]{3,2,1,0:T(8,128)(2,1)}), bf16[64,1,72,128]{3,2,1,0:T(8,128)(2,1)}, u32[]{:S(2)}, u32[]{:S(2)}) async-start(bf16[64,1,72,128]{3,2,1,0:T(8,128)(2,1)} %get-tuple-element.121), calls=%async_computation.2 | async-start | bytes 2359296 | tf_op jit(solution)/shard_map/all_to_all | solution.py:267
  129.3 6.4 %conditional.3 = ((bf16[320,1792]{1,0:T(8,128)(2,1)}, f32[320,1024]{1,0:T(8,128)}, bf16[320,1024]{1,0:T(8,128)(2,1)})) conditional(s32[]{:T(128)} %convert_element_type.64, (bf16[64,2,72,128]{3,2,1,0:T(8,128)(2,1)}, bf16[1120,1152]{1,0:T(8,128)(2,1)S(1)}, bf16[1792,512]{1,0:T(8,128)(2,1)}, bf16[1792,512]{1,0:T(8,128)(2,1)}) %tuple.60, ...), branch_computations={%region_8.9_spmd, %region_9.10_spmd} | conditional | flops 1 | bytes 9 | solution.py:317
  129.8 5.9 %branch_0_fun.3 = (bf16[320,1792]{1,0:T(8,128)(2,1)}, f32[320,1024]{1,0:T(8,128)}, bf16[320,1024]{1,0:T(8,128)(2,1)}) custom-call(bf16[64,2,72,128]{3,2,1,0:T(8,128)(2,1)} %get-tuple-element.51.refs_0_, bf16[1120,1152]{1,0:T(8,128)(2,1)S(1)} %get-tuple-element.52.refs_1_, bf16[1792,512]{1,0:T(8,128)(2,1)} %get-tuple-element.53.refs_2_, ...), custom_call_target="tpu_custom_call" | custom-call | flops 1 | bytes 1 | tf_op jit(solution)/shard_map/cond/branch_0_fun/pallas_call | solution.py:48
  136.8 5.8 %shard_map.89 = (bf16[320,1792]{1,0:T(8,128)(2,1)}, f32[320,1024]{1,0:T(8,128)}, bf16[320,1024]{1,0:T(8,128)(2,1)}) custom-call(bf16[64,2,72,128]{3,2,1,0:T(8,128)(2,1)} %all-to-all-done.1.refs_0_, bf16[1120,1152]{1,0:T(8,128)(2,1)S(1)} %fusion.1.refs_1_, bf16[1792,512]{1,0:T(8,128)(2,1)} %copy-done.4, bf16[1792,512]{1,0:T(8,128)(2,1)} %collective-permute-done.1.refs_3_.refs_5_), custom_call_target="tpu_custom_call" | custom-call | flops 1 | bytes 1 | tf_op jit(solution)/shard_map/pallas_call | solution.py:48
  143.2 10.9 %all-to-all-done.2.refs_0_ = bf16[64,1,72,128]{3,2,1,0:T(8,128)(2,1)} async-done(((bf16[64,1,72,128]{3,2,1,0:T(8,128)(2,1)}), bf16[64,1,72,128]{3,2,1,0:T(8,128)(2,1)}, u32[]{:S(2)}, u32[]{:S(2)}) %all-to-all-start.2) | async-done | bytes 1179680 | tf_op jit(solution)/shard_map/all_to_all | solution.py:267
  154.1 4.8 %shard_map.88 = bf16[64,3584]{1,0:T(8,128)(2,1)} custom-call(bf16[64,1,72,128]{3,2,1,0:T(8,128)(2,1)} %all-to-all-done.2.refs_0_, bf16[1120,1152]{1,0:T(8,128)(2,1)S(1)} %fusion.1.refs_1_, bf16[2,64,3584]{2,1,0:T(8,128)(2,1)S(1)} %copy-done.10, bf16[64,160]{1,0:T(8,128)(2,1)} %get-tuple-element.201.refs_3_), custom_call_target="tpu_custom_call" | custom-call | flops 1 | bytes 1 | tf_op jit(solution)/shard_map/pallas_call | solution.py:48
  158.9 1.5 collective-permute-start.8
  160.4 1.5 copy.51.refs_2_
  162.7 12.1 %collective-permute-done.6.refs_1_ = bf16[320,1024]{1,0:T(8,128)(2,1)} collective-permute-done((bf16[320,1024]{1,0:T(8,128)(2,1)}, bf16[320,1024]{1,0:T(8,128)(2,1)}, u32[]{:S(2)}, u32[]{:S(2)}) %collective-permute-start.6) | collective-permute-done | bytes 655392 | tf_op jit(solution)/shard_map/ppermute | solution.py:258
  174.7 8.5 %shard_map.90 = (bf16[320,1024]{1,0:T(8,128)(2,1)}, bf16[320,1024]{1,0:T(8,128)(2,1)}, bf16[64,1,72,128]{3,2,1,0:T(8,128)(2,1)}) custom-call(f32[320,1024]{1,0:T(8,128)} %get-tuple-element.123.refs_0_, bf16[320,1024]{1,0:T(8,128)(2,1)} %collective-permute-done.6.refs_1_, f32[320,1024]{1,0:T(8,128)} %get-tuple-element.125.refs_2_.refs_0_, ...), custom_call_target="tpu_custom_call" | custom-call | flops 1 | bytes 1 | tf_op jit(solution)/shard_map/pallas_call | solution.py:48
  183.2 31.3 %collective-permute-done.8.refs_0_.refs_2_ = bf16[64,3584]{1,0:T(8,128)(2,1)} collective-permute-done((bf16[64,3584]{1,0:T(8,128)(2,1)}, bf16[64,3584]{1,0:T(8,128)(2,1)}, u32[]{:S(2)}, u32[]{:S(2)}) %collective-permute-start.8) | collective-permute-done | bytes 458784 | tf_op jit(solution)/shard_map/ppermute | solution.py:324
  214.5 5.3 %shard_map.91 = bf16[64,1,72,128]{3,2,1,0:T(8,128)(2,1)} custom-call(bf16[64,3584]{1,0:T(8,128)(2,1)} %collective-permute-done.8.refs_0_.refs_2_, bf16[1152,1120]{1,0:T(8,128)(2,1)S(1)} %copy-done.1, bf16[160,64]{1,0:T(8,128)(2,1)} %copy.51.refs_2_, f32[160,1]{1,0:T(8,128)} %copy.52.refs_3_), custom_call_target="tpu_custom_call" | custom-call | flops 1 | bytes 1 | tf_op jit(solution)/shard_map/pallas_call | solution.py:48
  219.8 1.5 broadcast_select_fusion.4
  221.2 33.0 %all_to_all.34.refs_0_ = bf16[64,1,72,128]{3,2,1,0:T(8,128)(2,1)} all-to-all(bf16[64,1,72,128]{3,2,1,0:T(8,128)(2,1)S(1)} %broadcast_select_fusion.4), channel_id=1, replica_groups=mesh['section'=2,'dp'=2,'pair'=32,'half'=2] {'pair','half'}, dimensions={0} | all-to-all | bytes 2359296 | tf_op jit(solution)/shard_map/all_to_all | solution.py:267
  254.2 4.8 %shard_map.92 = bf16[64,3584]{1,0:T(8,128)(2,1)} custom-call(bf16[64,1,72,128]{3,2,1,0:T(8,128)(2,1)} %all_to_all.34.refs_0_, bf16[1120,1152]{1,0:T(8,128)(2,1)S(1)} %fusion.1.refs_1_, bf16[2,64,3584]{2,1,0:T(8,128)(2,1)S(1)} %copy-done.10, bf16[64,160]{1,0:T(8,128)(2,1)} %get-tuple-element.199.refs_3_), custom_call_target="tpu_custom_call" | custom-call | flops 1 | bytes 1 | tf_op jit(solution)/shard_map/pallas_call | solution.py:48
  259.0 1.3 collective-permute-start.9
  261.8 6.0 %shard_map.93 = (bf16[320,1792]{1,0:T(8,128)(2,1)}, f32[320,1024]{1,0:T(8,128)}, bf16[320,1024]{1,0:T(8,128)(2,1)}) custom-call(bf16[64,1,72,128]{3,2,1,0:T(8,128)(2,1)} %all_to_all.34.refs_0_, bf16[1120,1152]{1,0:T(8,128)(2,1)S(1)} %fusion.1.refs_1_, bf16[512,1792]{1,0:T(8,128)(2,1)} %copy-done.6, bf16[512,1792]{1,0:T(8,128)(2,1)} %copy-done.8), custom_call_target="tpu_custom_call" | custom-call | flops 1 | bytes 1 | tf_op jit(solution)/shard_map/pallas_call | solution.py:48
  267.8 15.8 %collective-permute-done.9.refs_0_.refs_2_ = bf16[64,3584]{1,0:T(8,128)(2,1)S(1)} collective-permute-done((bf16[64,3584]{1,0:T(8,128)(2,1)}, bf16[64,3584]{1,0:T(8,128)(2,1)S(1)}, u32[]{:S(2)}, u32[]{:S(2)}) %collective-permute-start.9) | collective-permute-done | bytes 458784 | tf_op jit(solution)/shard_map/ppermute | solution.py:329
  284.4 5.3 %shard_map.94 = bf16[64,1,72,128]{3,2,1,0:T(8,128)(2,1)} custom-call(bf16[64,3584]{1,0:T(8,128)(2,1)} %copy-done.13, bf16[1152,1120]{1,0:T(8,128)(2,1)S(1)} %copy-done.2, bf16[160,64]{1,0:T(8,128)(2,1)} %copy.53.refs_2_, f32[160,1]{1,0:T(8,128)} %copy.54.refs_3_), custom_call_target="tpu_custom_call" | custom-call | flops 1 | bytes 1 | tf_op jit(solution)/shard_map/pallas_call | solution.py:48
  289.7 8.3 %all-to-all-start.4 = ((bf16[64,1,72,128]{3,2,1,0:T(8,128)(2,1)}), bf16[64,1,72,128]{3,2,1,0:T(8,128)(2,1)}, u32[]{:S(2)}, u32[]{:S(2)}) async-start(bf16[64,1,72,128]{3,2,1,0:T(8,128)(2,1)} %shard_map.94), calls=%async_computation.4 | async-start | bytes 2359296 | tf_op jit(solution)/shard_map/all_to_all | solution.py:267
  299.3 19.4 %collective-permute-done.10.refs_3_ = bf16[320,1024]{1,0:T(8,128)(2,1)S(1)} collective-permute-done((bf16[320,1024]{1,0:T(8,128)(2,1)S(1)}, bf16[320,1024]{1,0:T(8,128)(2,1)S(1)}, u32[]{:S(2)}, u32[]{:S(2)}) %collective-permute-start.10) | collective-permute-done | bytes 655392 | tf_op jit(solution)/shard_map/ppermute | solution.py:258
  319.5 8.3 %shard_map.95 = (bf16[320,1024]{1,0:T(8,128)(2,1)}, bf16[320,1024]{1,0:T(8,128)(2,1)}, bf16[64,1,72,128]{3,2,1,0:T(8,128)(2,1)}) custom-call(f32[320,1024]{1,0:T(8,128)} %get-tuple-element.123.refs_0_, bf16[320,1024]{1,0:T(8,128)(2,1)} %collective-permute-done.6.refs_1_, f32[320,1024]{1,0:T(8,128)} %get-tuple-element.130.refs_2_, ...), custom_call_target="tpu_custom_call" | custom-call | flops 1 | bytes 1 | tf_op jit(solution)/shard_map/pallas_call | solution.py:48
  327.8 1.6 all-to-all-done.4.refs_0_
  329.4 17.5 %all-to-all-start.5 = ((bf16[64,1,72,128]{3,2,1,0:T(8,128)(2,1)}), bf16[64,1,72,128]{3,2,1,0:T(8,128)(2,1)}, u32[]{:S(2)}, u32[]{:S(2)}) async-start(bf16[64,1,72,128]{3,2,1,0:T(8,128)(2,1)} %get-tuple-element.133), calls=%async_computation.5 | async-start | bytes 2359296 | tf_op jit(solution)/shard_map/all_to_all | solution.py:267
  346.9 1.5 broadcast_select_fusion.8
  348.7 6.0 %shard_map.96 = (bf16[320,1792]{1,0:T(8,128)(2,1)}, f32[320,1024]{1,0:T(8,128)}, bf16[320,1024]{1,0:T(8,128)(2,1)}) custom-call(bf16[64,1,72,128]{3,2,1,0:T(8,128)(2,1)} %all-to-all-done.4.refs_0_, bf16[1120,1152]{1,0:T(8,128)(2,1)S(1)} %fusion.1.refs_1_, bf16[512,1792]{1,0:T(8,128)(2,1)S(1)} %copy-done.7, bf16[512,1792]{1,0:T(8,128)(2,1)} %copy-done.8), custom_call_target="tpu_custom_call" | custom-call | flops 1 | bytes 1 | tf_op jit(solution)/shard_map/pallas_call | solution.py:48
  356.0 2.0 broadcast_select_fusion.6
  358.0 1.6 pad_maximum_fusion.1
  359.6 1.5 pad_maximum_fusion
  361.1 17.4 %collective-permute-done.11.refs_3_ = bf16[320,1024]{1,0:T(8,128)(2,1)} collective-permute-done((bf16[320,1024]{1,0:T(8,128)(2,1)}, bf16[320,1024]{1,0:T(8,128)(2,1)}, u32[]{:S(2)}, u32[]{:S(2)}) %collective-permute-start.11) | collective-permute-done | bytes 655392 | tf_op jit(solution)/shard_map/ppermute | solution.py:258
  378.5 7.5 %shard_map.97 = (bf16[320,1024]{1,0:T(8,128)(2,1)}, bf16[320,1024]{1,0:T(8,128)(2,1)}, bf16[64,1,72,128]{3,2,1,0:T(8,128)(2,1)}) custom-call(f32[320,1024]{1,0:T(8,128)} %get-tuple-element.125.refs_2_.refs_0_, bf16[320,1024]{1,0:T(8,128)(2,1)} %collective-permute-done.7.refs_3_.refs_1_, f32[320,1024]{1,0:T(8,128)} %get-tuple-element.135.refs_2_, ...), custom_call_target="tpu_custom_call" | custom-call | flops 1 | bytes 1 | tf_op jit(solution)/shard_map/pallas_call | solution.py:48
  386.0 1.7 broadcast_select_fusion.9
  388.1 1.6 convolution_convert_fusion
  389.7 2.7 collective-permute-start.14
  392.5 1.5 copy-done.11
  394.0 1.6 convolution_convert_fusion.1
  395.8 2.9 add_convert_fusion
  398.6 2.7 collective-permute-start.15
  401.4 2.9 add_convert_fusion.1
  404.3 2.8 collective-permute-start.13
  407.1 11.8 %all-to-all-start.6 = ((bf16[64,1,72,128]{3,2,1,0:T(8,128)(2,1)}), bf16[64,1,72,128]{3,2,1,0:T(8,128)(2,1)}, u32[]{:S(2)}, u32[]{:S(2)}) async-start(bf16[64,1,72,128]{3,2,1,0:T(8,128)(2,1)} %get-tuple-element.146), calls=%async_computation.6 | async-start | bytes 2359296 | tf_op jit(solution)/shard_map/all_to_all | solution.py:267
  418.8 4.8 %shard_map.98 = bf16[64,3584]{1,0:T(8,128)(2,1)} custom-call(bf16[64,1,72,128]{3,2,1,0:T(8,128)(2,1)} %all-to-all-done.5.refs_0_, bf16[1120,1152]{1,0:T(8,128)(2,1)S(1)} %fusion.1.refs_1_, bf16[64,3584]{1,0:T(8,128)(2,1)} %collective-permute-done.8.refs_0_.refs_2_, bf16[64,160]{1,0:T(8,128)(2,1)} %get-tuple-element.201.refs_3_), custom_call_target="tpu_custom_call" | custom-call | flops 1 | bytes 1 | tf_op jit(solution)/shard_map/pallas_call | solution.py:48
  424.8 1.8 collective-permute-done.15
  426.6 2.9 broadcast_select_fusion
  429.5 25.9 %collective-permute-done.13 = bf16[1792,512]{1,0:T(8,128)(2,1)} collective-permute-done((bf16[1792,512]{1,0:T(8,128)(2,1)}, bf16[1792,512]{1,0:T(8,128)(2,1)}, u32[]{:S(2)}, u32[]{:S(2)}) %collective-permute-start.13) | collective-permute-done | bytes 1835040 | tf_op jit(solution)/shard_map/ppermute | solution.py:262
  455.4 2.9 broadcast_select_fusion.2
  458.3 4.9 %shard_map.99 = bf16[64,3584]{1,0:T(8,128)(2,1)} custom-call(bf16[64,1,72,128]{3,2,1,0:T(8,128)(2,1)} %all-to-all-done.6.refs_0_, bf16[1120,1152]{1,0:T(8,128)(2,1)S(1)} %fusion.1.refs_1_, bf16[64,3584]{1,0:T(8,128)(2,1)} %copy-done.13, bf16[64,160]{1,0:T(8,128)(2,1)} %get-tuple-element.199.refs_3_), custom_call_target="tpu_custom_call" | custom-call | flops 1 | bytes 1 | tf_op jit(solution)/shard_map/pallas_call | solution.py:48
  (106 shorter events, 18.3 us)
Async XLA Ops:
  0.6 49.0 %collective-permute-start.3 = (bf16[512,1792]{1,0:T(8,128)(2,1)}, bf16[512,1792]{1,0:T(8,128)(2,1)}, u32[]{:S(2)}, u32[]{:S(2)}) collective-permute-start(bf16[512,1792]{1,0:T(8,128)(2,1)} %bitcast.34), channel_id=1, source_target_pairs={{1,64},{64,1},{3,66},{66,3},{5,68},{68,5},{7,70},{70,7},{9,72},{72... | collective-permute-start | bytes 5505032 | tf_op jit(solution)/shard_map/ppermute | solution.py:262
  5.2 47.1 %collective-permute-start = (bf16[1792,512]{1,0:T(8,128)(2,1)}, bf16[1792,512]{1,0:T(8,128)(2,1)}, u32[]{:S(2)}, u32[]{:S(2)}) collective-permute-start(bf16[1792,512]{1,0:T(8,128)(2,1)} %bitcast.35), channel_id=1, source_target_pairs={{1,64},{64,1},{3,66},{66,3},{5,68},{68,5},{7,70},{70,7},{9,72},{72... | collective-permute-start | bytes 5505032 | tf_op jit(solution)/shard_map/ppermute | solution.py:262
  8.2 2.0 copy-start.27
  8.2 4.8 %copy-start.28 = (f32[1,2,64,2]{2,3,1,0:T(2,128)S(1)}, f32[1,2,64,2]{2,3,1,0:T(2,128)}, u32[]{:S(2)}) copy-start(f32[1,2,64,2]{2,3,1,0:T(2,128)} %param.13) | copy-start | bytes 3076
  8.2 5.0 %copy-start.9 = (bf16[1,2,64,3584]{3,2,1,0:T(8,128)(2,1)S(1)}, bf16[1,2,64,3584]{3,2,1,0:T(8,128)(2,1)}, u32[]{:S(2)}) copy-start(bf16[1,2,64,3584]{3,2,1,0:T(8,128)(2,1)} %param.11) | copy-start | bytes 2752516
  35.2 83.9 %all-to-all-start.1 = ((bf16[64,2,72,128]{3,2,1,0:T(8,128)(2,1)}), bf16[64,2,72,128]{3,2,1,0:T(8,128)(2,1)}, u32[]{:S(2)}, u32[]{:S(2)}) async-start(bf16[64,2,72,128]{3,2,1,0:T(8,128)(2,1)} %get-tuple-element.113), calls=%async_computation.1 | async-start | bytes 4718592 | tf_op jit(solution)/shard_map/all_to_all | solution.py:267
  49.6 2.7 copy-start.16
  52.0 3.9 copy-start.6
  52.0 3.9 collective-permute-start.4
  54.3 57.3 %copy-start.4 = (bf16[1792,512]{1,0:T(8,128)(2,1)}, bf16[1792,512]{1,0:T(8,128)(2,1)S(1)}, u32[]{:S(2)}) copy-start(bf16[1792,512]{1,0:T(8,128)(2,1)S(1)} %broadcast_select_fusion.3.refs_2_.refs_4_) | copy-start | bytes 5505028
  54.3 9.8 %collective-permute-start.1 = (bf16[1792,512]{1,0:T(8,128)(2,1)S(1)}, bf16[1792,512]{1,0:T(8,128)(2,1)}, u32[]{:S(2)}, u32[]{:S(2)}) collective-permute-start(bf16[1792,512]{1,0:T(8,128)(2,1)S(1)} %broadcast_select_fusion.3.refs_2_.refs_4_), channel_id=1, source_target_pairs={{0,64},{64,0},{1,65},{65,1},{2,66},{66,2},{3,67},{67,3},{4,68},{68... | collective-permute-start | bytes 5505032 | tf_op jit(solution)/shard_map/ppermute | solution.py:258
  55.9 6.5 %copy-start.8 = (bf16[512,1792]{1,0:T(8,128)(2,1)}, bf16[512,1792]{1,0:T(8,128)(2,1)S(1)}, u32[]{:S(2)}) copy-start(bf16[512,1792]{1,0:T(8,128)(2,1)S(1)} %collective-permute-done.4.refs_3_) | copy-start | bytes 5505028
  62.4 49.2 %copy-start = (bf16[1152,1120]{1,0:T(8,128)(2,1)S(1)}, bf16[1152,1120]{1,0:T(8,128)(2,1)}, u32[]{:S(2)}) copy-start(bf16[1152,1120]{1,0:T(8,128)(2,1)} %fusion.refs_6_.refs_1_) | copy-start | bytes 7741444
  62.4 34.0 %collective-permute-start.5 = (bf16[320,1024]{1,0:T(8,128)(2,1)}, bf16[320,1024]{1,0:T(8,128)(2,1)S(1)}, u32[]{:S(2)}, u32[]{:S(2)}) collective-permute-start(bf16[320,1024]{1,0:T(8,128)(2,1)} %get-tuple-element.119), channel_id=1, source_target_pairs={{0,1},{1,0},{2,3},{3,2},{4,5},{5,4},{6,7},{7,6},{8,9},{9,8},{10,11... | collective-permute-start | bytes 1966088 | tf_op jit(solution)/shard_map/ppermute | solution.py:258
  69.9 41.7 %collective-permute-start.2 = (bf16[320,1024]{1,0:T(8,128)(2,1)}, bf16[320,1024]{1,0:T(8,128)(2,1)}, u32[]{:S(2)}, u32[]{:S(2)}) collective-permute-start(bf16[320,1024]{1,0:T(8,128)(2,1)} %get-tuple-element.117), channel_id=1, source_target_pairs={{0,1},{1,0},{2,3},{3,2},{4,5},{5,4},{6,7},{7,6},{8,9},{9,8},{10,11... | collective-permute-start | bytes 1966088 | tf_op jit(solution)/shard_map/ppermute | solution.py:258
  96.4 15.2 %copy-start.20 = (bf16[320,1024]{1,0:T(8,128)(2,1)}, bf16[320,1024]{1,0:T(8,128)(2,1)S(1)}, u32[]{:S(2)}) copy-start(bf16[320,1024]{1,0:T(8,128)(2,1)S(1)} %collective-permute-done.5.refs_3_) | copy-start | bytes 1966084
  119.0 35.1 %all-to-all-start.2 = ((bf16[64,1,72,128]{3,2,1,0:T(8,128)(2,1)}), bf16[64,1,72,128]{3,2,1,0:T(8,128)(2,1)}, u32[]{:S(2)}, u32[]{:S(2)}) async-start(bf16[64,1,72,128]{3,2,1,0:T(8,128)(2,1)} %get-tuple-element.121), calls=%async_computation.2 | async-start | bytes 2359296 | tf_op jit(solution)/shard_map/all_to_all | solution.py:267
  135.7 18.4 %copy-start.10 = (bf16[2,64,3584]{2,1,0:T(8,128)(2,1)S(1)}, bf16[2,64,3584]{2,1,0:T(8,128)(2,1)}, u32[]{:S(2)}) copy-start(bf16[2,64,3584]{2,1,0:T(8,128)(2,1)} %refs_2_.3) | copy-start | bytes 2752516
  135.7 26.9 %collective-permute-start.7 = (bf16[320,1024]{1,0:T(8,128)(2,1)}, bf16[320,1024]{1,0:T(8,128)(2,1)}, u32[]{:S(2)}, u32[]{:S(2)}) collective-permute-start(bf16[320,1024]{1,0:T(8,128)(2,1)} %get-tuple-element.126), channel_id=1, source_target_pairs={{0,1},{1,0},{2,3},{3,2},{4,5},{5,4},{6,7},{7,6},{8,9},{9,8},{10,11... | collective-permute-start | bytes 1966088 | tf_op jit(solution)/shard_map/ppermute | solution.py:258
  142.6 32.1 %collective-permute-start.6 = (bf16[320,1024]{1,0:T(8,128)(2,1)}, bf16[320,1024]{1,0:T(8,128)(2,1)}, u32[]{:S(2)}, u32[]{:S(2)}) collective-permute-start(bf16[320,1024]{1,0:T(8,128)(2,1)} %get-tuple-element.124), channel_id=1, source_target_pairs={{0,1},{1,0},{2,3},{3,2},{4,5},{5,4},{6,7},{7,6},{8,9},{9,8},{10,11... | collective-permute-start | bytes 1966088 | tf_op jit(solution)/shard_map/ppermute | solution.py:258
  158.9 55.5 %collective-permute-start.8 = (bf16[64,3584]{1,0:T(8,128)(2,1)}, bf16[64,3584]{1,0:T(8,128)(2,1)}, u32[]{:S(2)}, u32[]{:S(2)}) collective-permute-start(bf16[64,3584]{1,0:T(8,128)(2,1)} %shard_map.88), channel_id=1, source_target_pairs={{128,0},{129,1},{130,2},{131,3},{132,4},{133,5},{134,6},{135,7},{1... | collective-permute-start | bytes 1376264 | tf_op jit(solution)/shard_map/ppermute | solution.py:324
  174.7 39.8 %copy-start.1 = (bf16[1152,1120]{1,0:T(8,128)(2,1)S(1)}, bf16[1152,1120]{1,0:T(8,128)(2,1)}, u32[]{:S(2)}) copy-start(bf16[1152,1120]{1,0:T(8,128)(2,1)} %fusion.refs_6_.refs_1_) | copy-start | bytes 7741444
  183.2 36.6 %copy-start.17 = (bf16[64,1,72,128]{3,2,1,0:T(8,128)(2,1)S(1)}, bf16[64,1,72,128]{3,2,1,0:T(8,128)(2,1)}, u32[]{:S(2)}) copy-start(bf16[64,1,72,128]{3,2,1,0:T(8,128)(2,1)} %get-tuple-element.127) | copy-start | bytes 3538948
  259.0 24.7 %collective-permute-start.9 = (bf16[64,3584]{1,0:T(8,128)(2,1)}, bf16[64,3584]{1,0:T(8,128)(2,1)S(1)}, u32[]{:S(2)}, u32[]{:S(2)}) collective-permute-start(bf16[64,3584]{1,0:T(8,128)(2,1)} %shard_map.92), channel_id=1, source_target_pairs={{128,0},{129,1},{130,2},{131,3},{132,4},{133,5},{134,6},{135,7},{1... | collective-permute-start | bytes 1376264 | tf_op jit(solution)/shard_map/ppermute | solution.py:329
  261.8 22.6 %copy-start.2 = (bf16[1152,1120]{1,0:T(8,128)(2,1)S(1)}, bf16[1152,1120]{1,0:T(8,128)(2,1)}, u32[]{:S(2)}) copy-start(bf16[1152,1120]{1,0:T(8,128)(2,1)} %fusion.refs_6_.refs_1_) | copy-start | bytes 7741444
  283.7 0.8 copy-start.13
  289.7 8.3 %copy-start.29 = (bf16[320,1024]{1,0:T(8,128)(2,1)S(1)}, bf16[320,1024]{1,0:T(8,128)(2,1)}, u32[]{:S(2)}) copy-start(bf16[320,1024]{1,0:T(8,128)(2,1)} %get-tuple-element.131) | copy-start | bytes 1966084
  289.7 39.7 %all-to-all-start.4 = ((bf16[64,1,72,128]{3,2,1,0:T(8,128)(2,1)}), bf16[64,1,72,128]{3,2,1,0:T(8,128)(2,1)}, u32[]{:S(2)}, u32[]{:S(2)}) async-start(bf16[64,1,72,128]{3,2,1,0:T(8,128)(2,1)} %shard_map.94), calls=%async_computation.4 | async-start | bytes 2359296 | tf_op jit(solution)/shard_map/all_to_all | solution.py:267
  298.0 20.6 %collective-permute-start.10 = (bf16[320,1024]{1,0:T(8,128)(2,1)S(1)}, bf16[320,1024]{1,0:T(8,128)(2,1)S(1)}, u32[]{:S(2)}, u32[]{:S(2)}) collective-permute-start(bf16[320,1024]{1,0:T(8,128)(2,1)S(1)} %copy-done.29), channel_id=1, source_target_pairs={{0,1},{1,0},{2,3},{3,2},{4,5},{5,4},{6,7},{7,6},{8,9},{9,8},{10,11... | collective-permute-start | bytes 1966088 | tf_op jit(solution)/shard_map/ppermute | solution.py:258
  318.6 0.9 copy-start.21
  329.4 56.6 %all-to-all-start.5 = ((bf16[64,1,72,128]{3,2,1,0:T(8,128)(2,1)}), bf16[64,1,72,128]{3,2,1,0:T(8,128)(2,1)}, u32[]{:S(2)}, u32[]{:S(2)}) async-start(bf16[64,1,72,128]{3,2,1,0:T(8,128)(2,1)} %get-tuple-element.133), calls=%async_computation.5 | async-start | bytes 2359296 | tf_op jit(solution)/shard_map/all_to_all | solution.py:267
  346.8 1.8 copy-start.7
  348.7 7.3 %copy-start.18 = (bf16[320,1792]{1,0:T(8,128)(2,1)S(1)}, bf16[320,1792]{1,0:T(8,128)(2,1)}, u32[]{:S(2)}) copy-start(bf16[320,1792]{1,0:T(8,128)(2,1)} %get-tuple-element.143) | copy-start | bytes 3440644
  348.7 7.3 %copy-start.19 = (bf16[320,1792]{1,0:T(8,128)(2,1)S(1)}, bf16[320,1792]{1,0:T(8,128)(2,1)}, u32[]{:S(2)}) copy-start(bf16[320,1792]{1,0:T(8,128)(2,1)} %get-tuple-element.144) | copy-start | bytes 3440644
  354.7 23.8 %collective-permute-start.11 = (bf16[320,1024]{1,0:T(8,128)(2,1)}, bf16[320,1024]{1,0:T(8,128)(2,1)}, u32[]{:S(2)}, u32[]{:S(2)}) collective-permute-start(bf16[320,1024]{1,0:T(8,128)(2,1)} %get-tuple-element.136), channel_id=1, source_target_pairs={{0,1},{1,0},{2,3},{3,2},{4,5},{5,4},{6,7},{7,6},{8,9},{9,8},{10,11... | collective-permute-start | bytes 1966088 | tf_op jit(solution)/shard_map/ppermute | solution.py:258
  359.6 19.0 %copy-start.3 = (bf16[1152,1120]{1,0:T(8,128)(2,1)S(1)}, bf16[1152,1120]{1,0:T(8,128)(2,1)}, u32[]{:S(2)}) copy-start(bf16[1152,1120]{1,0:T(8,128)(2,1)} %fusion.refs_6_.refs_1_) | copy-start | bytes 7741444
  359.6 19.0 %copy-start.5 = (bf16[1792,512]{1,0:T(8,128)(2,1)S(1)}, bf16[1792,512]{1,0:T(8,128)(2,1)}, u32[]{:S(2)}) copy-start(bf16[1792,512]{1,0:T(8,128)(2,1)} %copy-done.4) | copy-start | bytes 5505028
  378.5 7.5 %copy-start.23 = (bf16[320,1024]{1,0:T(8,128)(2,1)S(1)}, bf16[320,1024]{1,0:T(8,128)(2,1)}, u32[]{:S(2)}) copy-start(bf16[320,1024]{1,0:T(8,128)(2,1)} %get-tuple-element.152) | copy-start | bytes 1966084
  386.0 2.0 copy-start.12
  388.1 4.3 copy-start.22
  388.1 4.3 copy-start.24
  388.1 4.3 copy-start.25
  388.1 4.3 copy-start.26
  389.7 6.1 %collective-permute-start.14 = (bf16[512,1792]{1,0:T(8,128)(2,1)S(1)}, bf16[512,1792]{1,0:T(8,128)(2,1)S(1)}, u32[]{:S(2)}, u32[]{:S(2)}) collective-permute-start(bf16[512,1792]{1,0:T(8,128)(2,1)S(1)} %convolution_convert_fusion), channel_id=1, source_target_pairs={{0,64},{64,0},{1,65},{65,1},{2,66},{66,2},{3,67},{67,3},{4,68},{68... | collective-permute-start | bytes 5505032 | tf_op jit(solution)/shard_map/ppermute | solution.py:258
  392.4 1.6 copy-start.11
  395.7 5.7 %collective-permute-start.12 = (bf16[1792,512]{1,0:T(8,128)(2,1)S(1)}, bf16[1792,512]{1,0:T(8,128)(2,1)S(1)}, u32[]{:S(2)}, u32[]{:S(2)}) collective-permute-start(bf16[1792,512]{1,0:T(8,128)(2,1)S(1)} %convolution_convert_fusion.1), channel_id=1, source_target_pairs={{0,64},{64,0},{1,65},{65,1},{2,66},{66,2},{3,67},{67,3},{4,68},{68... | collective-permute-start | bytes 5505032 | tf_op jit(solution)/shard_map/ppermute | solution.py:258
  398.6 27.9 %collective-permute-start.15 = (bf16[512,1792]{1,0:T(8,128)(2,1)}, bf16[512,1792]{1,0:T(8,128)(2,1)}, u32[]{:S(2)}, u32[]{:S(2)}) collective-permute-start(bf16[512,1792]{1,0:T(8,128)(2,1)} %add_convert_fusion), channel_id=1, source_target_pairs={{1,64},{64,1},{3,66},{66,3},{5,68},{68,5},{7,70},{70,7},{9,72},{72... | collective-permute-start | bytes 5505032 | tf_op jit(solution)/shard_map/ppermute | solution.py:262
  404.3 51.1 %collective-permute-start.13 = (bf16[1792,512]{1,0:T(8,128)(2,1)}, bf16[1792,512]{1,0:T(8,128)(2,1)}, u32[]{:S(2)}, u32[]{:S(2)}) collective-permute-start(bf16[1792,512]{1,0:T(8,128)(2,1)} %add_convert_fusion.1), channel_id=1, source_target_pairs={{1,64},{64,1},{3,66},{66,3},{5,68},{68,5},{7,70},{70,7},{9,72},{72... | collective-permute-start | bytes 5505032 | tf_op jit(solution)/shard_map/ppermute | solution.py:262
  407.1 51.3 %all-to-all-start.6 = ((bf16[64,1,72,128]{3,2,1,0:T(8,128)(2,1)}), bf16[64,1,72,128]{3,2,1,0:T(8,128)(2,1)}, u32[]{:S(2)}, u32[]{:S(2)}) async-start(bf16[64,1,72,128]{3,2,1,0:T(8,128)(2,1)} %get-tuple-element.146), calls=%async_computation.6 | async-start | bytes 2359296 | tf_op jit(solution)/shard_map/all_to_all | solution.py:267
  418.8 4.9 %copy-start.14 = (bf16[64,3584]{1,0:T(8,128)(2,1)S(1)}, bf16[64,3584]{1,0:T(8,128)(2,1)}, u32[]{:S(2)}) copy-start(bf16[64,3584]{1,0:T(8,128)(2,1)} %shard_map.88) | copy-start | bytes 1376260
  458.3 4.9 %copy-start.15 = (bf16[64,3584]{1,0:T(8,128)(2,1)S(1)}, bf16[64,3584]{1,0:T(8,128)(2,1)}, u32[]{:S(2)}) copy-start(bf16[64,3584]{1,0:T(8,128)(2,1)} %shard_map.92) | copy-start | bytes 1376260

commit v3 on v2

--- a/solution.py
+++ b/solution.py
@@ -318,25 +318,37 @@
         top_section, lambda: arrive(second, 1, unpacker, downs), lambda: arrive(second, 1, unpacker, ups)
     )
     got_b1 = swap(sent_b1, "half")
-    top_active1, top_grads1, back1 = turn(own_b0, got_b0, own_b1, got_b1, ups, packer, chunk_rows)
-
     top_out0 = combine(third, unpacker, place_t[0], outer[0])
     low_in0 = lax.ppermute(top_out0, "section", [(1, 0)])
-    fourth_chunks = pick(back1, dispatch([(low_in0, ())], [place[0]], [weight[0]], packer, chunk_rows))
+
+    def top_turn():
+        return turn(own_b0, got_b0, own_b1, got_b1, ups, packer, chunk_rows)
+
+    def low_send():
+        kept = jnp.zeros(own_b0.shape, BF)
+        return kept, kept, dispatch([(low_in0, ())], [place[0]], [weight[0]], packer, chunk_rows)
+
+    top_active1, top_grads1, fourth_chunks = lax.cond(top_section, top_turn, low_send)
     rows_in0, rows_in1 = pick(rows_a0, rows_b0), pick(rows_b0, rows_b1)
     fourth = send(fourth_chunks)
-    top_out1 = combine(fourth, unpacker, place_t[1], outer[1])
+
+    def top_combine():
+        return combine(fourth, unpacker, place_t[1], outer[1]), rows_b1, own_b1, sent_b1
+
+    def low_arrive():
+        return low_in0, *arrive(fourth, 0, unpacker, downs)
+
+    top_out1, rows_d, own_d, sent_d = lax.cond(top_section, top_combine, low_arrive)
     low_in1 = lax.ppermute(top_out1, "section", [(1, 0)])
-    rows_d, own_d, sent_d = arrive(fourth, 0, unpacker, downs)
-    low_in1, sent_d = lax.optimization_barrier((low_in1, sent_d))
     got_d = swap(sent_d, "half")
 
     fifth = send(dispatch([(low_in1, ())], [place[1]], [weight[1]], packer, chunk_rows))
     low_active0, low_grads0, back2 = turn(own_b0, got_b0, own_d, got_d, ups, packer, chunk_rows)
     fifth, back2 = lax.optimization_barrier((fifth, back2))
+    rows_e, own_e, sent_e = arrive(fifth, 0, unpacker, downs)
+    sent_e, back2 = lax.optimization_barrier((sent_e, back2))
+    got_e = swap(sent_e, "half")
     sixth = send(back2)
-    rows_e, own_e, sent_e = arrive(fifth, 0, unpacker, downs)
-    got_e = swap(sent_e, "half")
     low_active1, low_grads1, back3 = turn(own_b1, got_b1, own_e, got_e, ups, packer, chunk_rows)
     seventh = send(back3)
 

time: 475 us -> 479 us (level)
  waiting for transfers between devices: 179 us -> 193 us
  Pallas kernels: 106 us -> 92.3 us
  local copies, waits for them, and re-layouts: 13.1 us -> 18.2 us
    pallas_call x17 -> x15, Pallas kernels: 106 us -> 92.3 us  [staged_call(): pl.pallas_call(kernel, out_shape=outs_flat, in_specs=[anywhere] * n_in +...]
    ppermute x1, waiting for transfers between devices: 31.3 us -> 40.2 us  [on_device(): low_in0 = lax.ppermute(top_out0, 'section', [(1, 0)])]
  transfers between devices with their start and end apart: 21 -> 21, of which waited for: 12 -> 13; matrix products, arithmetic and copies ran while one was open for 9% -> 8% of each run, Pallas kernels for 18% -> 14%
where the time goes in v3:
time: 479 us; the launch traced here: 470 us
  waiting for transfers between devices  193 us (40%)
  Pallas kernels  92.3 us (19%)
  starting transfers between devices  87.4 us (18%)
  blocking collectives  33.2 us (7%)
  other arithmetic  26.6 us (6%)
  local copies, waits for them, and re-layouts  18.2 us (4%)
  loops' own time  9.23 us (2%)
  matrix products  8.96 us (2%)
    ppermute x10, waiting for transfers between devices, swap(): return lax.ppermute(value, axis, [(0, 1), (1, 0)])  94.9 us
    pallas_call x15, Pallas kernels, staged_call(): pl.pallas_call(kernel, out_shape=outs_flat, in_specs=[anywhere] * n_in +...  92.3 us
    all_to_all x5, starting transfers between devices, send(): lax.all_to_all(chunks, PAIRED, split_axis=0, concat_axis=0, tiled=True)  62.8 us
    ppermute x1, waiting for transfers between devices, on_device(): low_in0 = lax.ppermute(top_out0, 'section', [(1, 0)])  40.2 us
    all_to_all x1, blocking collectives, send(): lax.all_to_all(chunks, PAIRED, split_axis=0, concat_axis=0, tiled=True)  33.2 us
    ppermute x4, waiting for transfers between devices, cross(): moved = lax.ppermute(value, ('dp', 'half'), [(1, 2), (2, 1)])  25.3 us
    ppermute x1, waiting for transfers between devices, on_device(): low_in1 = lax.ppermute(top_out1, 'section', [(1, 0)])  20.2 us
    ppermute x4, starting transfers between devices, cross(): moved = lax.ppermute(value, ('dp', 'half'), [(1, 2), (2, 1)])  13.1 us
  transfers between devices with their start and end apart: 21, of which 13 were waited for; matrix products, arithmetic and copies ran while one was open for 8% of the time, Pallas kernels for 14%

profile of v3, /device:TPU:1, one launch (start us, length us, event | category | flops | bytes accessed | tf_op | source)
XLA Modules:
  0.0 470.4 jit_solution(15331255801096103127)
XLA Ops:
  0.6 4.6 collective-permute-start.3
  5.2 1.9 collective-permute-start
  7.2 2.0 fusion.refs_6_.refs_1_
  13.2 21.8 %conditional.4 = (bf16[64,2,72,128]{3,2,1,0:T(8,128)(2,1)}, bf16[64,2,72,128]{3,2,1,0:T(8,128)(2,1)}) conditional(s32[]{:T(128)} %convert_element_type.68, (bf16[1,2,64,3584]{3,2,1,0:T(8,128)(2,1)S(1)}, bf16[1152,1120]{1,0:T(8,128)(2,1)}, bf16[160,64]{0,1:T(8,128)(2,1)}, bf16[160,64]{0,1:T(8,128)(2,1)S(1)}) %tuple.94, ...), branch_computations={%region_6.7_spmd, %region_7.8_spmd} | conditional | flops 2 | bytes 7163062 | solution.py:303
  13.2 1.5 copy.45.refs_3_
  16.1 8.7 %branch_0_fun.4 = bf16[64,2,72,128]{3,2,1,0:T(8,128)(2,1)} custom-call(bf16[1,2,64,3584]{3,2,1,0:T(8,128)(2,1)S(1)} %get-tuple-element.76.refs_0_.refs_1_, bf16[1,2,64,3584]{3,2,1,0:T(8,128)(2,1)S(1)} %get-tuple-element.76.refs_0_.refs_1_, bf16[1152,1120]{1,0:T(8,128)(2,1)} %get-tuple-element.86.refs_2_, bf16[160,64]{1,0:T(8,128)(2,1)} %copy.45.refs_3_, ...), custom_call_target="tpu_custom_call" | custom-call | flops 1 | bytes 1 | tf_op jit(solution)/shard_map/cond/branch_0_fun/pallas_call | solution.py:48
  24.8 1.7 broadcast.175
  35.0 14.4 %all-to-all-start.1 = ((bf16[64,2,72,128]{3,2,1,0:T(8,128)(2,1)}), bf16[64,2,72,128]{3,2,1,0:T(8,128)(2,1)}, u32[]{:S(2)}, u32[]{:S(2)}) async-start(bf16[64,2,72,128]{3,2,1,0:T(8,128)(2,1)} %get-tuple-element.186), calls=%async_computation.1 | async-start | bytes 4718592 | tf_op jit(solution)/shard_map/all_to_all | solution.py:267
  49.5 2.4 broadcast_select_fusion.1.refs_2_
  52.2 2.0 broadcast_select_fusion.3.refs_2_.refs_4_
  54.3 1.4 collective-permute-done.4.refs_3_
  55.7 6.5 %shard_map.86 = (bf16[320,1792]{1,0:T(8,128)(2,1)}, f32[320,1024]{1,0:T(8,128)}, bf16[320,1024]{1,0:T(8,128)(2,1)}) custom-call(bf16[64,2,72,128]{3,2,1,0:T(8,128)(2,1)} %get-tuple-element.187.refs_0_, bf16[1120,1152]{1,0:T(8,128)(2,1)S(1)} %fusion.1.refs_1_, bf16[512,1792]{1,0:T(8,128)(2,1)S(1)} %broadcast_select_fusion.1.refs_2_, ...), custom_call_target="tpu_custom_call" | custom-call | flops 1 | bytes 1 | tf_op jit(solution)/shard_map/pallas_call | solution.py:48
  62.3 1.7 collective-permute-start.5
  64.0 5.8 %shard_map.85 = (bf16[320,1792]{1,0:T(8,128)(2,1)}, f32[320,1024]{1,0:T(8,128)}, bf16[320,1024]{1,0:T(8,128)(2,1)}) custom-call(bf16[64,2,72,128]{3,2,1,0:T(8,128)(2,1)} %get-tuple-element.187.refs_0_, bf16[1120,1152]{1,0:T(8,128)(2,1)S(1)} %fusion.1.refs_1_, bf16[1792,512]{1,0:T(8,128)(2,1)S(1)} %broadcast_select_fusion.3.refs_2_.refs_4_, ...), custom_call_target="tpu_custom_call" | custom-call | flops 1 | bytes 1 | tf_op jit(solution)/shard_map/pallas_call | solution.py:48
  70.1 26.3 %collective-permute-done.5.refs_3_ = bf16[320,1024]{1,0:T(8,128)(2,1)S(1)} collective-permute-done((bf16[320,1024]{1,0:T(8,128)(2,1)}, bf16[320,1024]{1,0:T(8,128)(2,1)S(1)}, u32[]{:S(2)}, u32[]{:S(2)}) %collective-permute-start.5) | collective-permute-done | bytes 655392 | tf_op jit(solution)/shard_map/ppermute | solution.py:258
  96.4 15.1 %collective-permute-done.2.refs_1_ = bf16[320,1024]{1,0:T(8,128)(2,1)} collective-permute-done((bf16[320,1024]{1,0:T(8,128)(2,1)}, bf16[320,1024]{1,0:T(8,128)(2,1)}, u32[]{:S(2)}, u32[]{:S(2)}) %collective-permute-start.2) | collective-permute-done | bytes 655392 | tf_op jit(solution)/shard_map/ppermute | solution.py:258
  111.5 7.4 %shard_map.87 = (bf16[320,1024]{1,0:T(8,128)(2,1)}, bf16[320,1024]{1,0:T(8,128)(2,1)}, bf16[64,1,72,128]{3,2,1,0:T(8,128)(2,1)}) custom-call(f32[320,1024]{1,0:T(8,128)} %get-tuple-element.189.refs_0_, bf16[320,1024]{1,0:T(8,128)(2,1)} %collective-permute-done.2.refs_1_, f32[320,1024]{1,0:T(8,128)} %get-tuple-element.191.refs_2_, ...), custom_call_target="tpu_custom_call" | custom-call | flops 1 | bytes 1 | tf_op jit(solution)/shard_map/pallas_call | solution.py:48
  118.9 10.3 %all-to-all-start.2 = ((bf16[64,1,72,128]{3,2,1,0:T(8,128)(2,1)}), bf16[64,1,72,128]{3,2,1,0:T(8,128)(2,1)}, u32[]{:S(2)}, u32[]{:S(2)}) async-start(bf16[64,1,72,128]{3,2,1,0:T(8,128)(2,1)} %get-tuple-element.194), calls=%async_computation.2 | async-start | bytes 2359296 | tf_op jit(solution)/shard_map/all_to_all | solution.py:267
  129.1 6.3 %conditional.5 = ((bf16[320,1792]{1,0:T(8,128)(2,1)}, f32[320,1024]{1,0:T(8,128)}, bf16[320,1024]{1,0:T(8,128)(2,1)})) conditional(s32[]{:T(128)} %convert_element_type.68, (bf16[64,2,72,128]{3,2,1,0:T(8,128)(2,1)}, bf16[1120,1152]{1,0:T(8,128)(2,1)S(1)}, bf16[1792,512]{1,0:T(8,128)(2,1)}, bf16[1792,512]{1,0:T(8,128)(2,1)}) %tuple.88, ...), branch_computations={%region_8.9_spmd, %region_9.10_spmd} | conditional | flops 1 | bytes 9 | solution.py:317
  129.6 5.8 %branch_0_fun.5 = (bf16[320,1792]{1,0:T(8,128)(2,1)}, f32[320,1024]{1,0:T(8,128)}, bf16[320,1024]{1,0:T(8,128)(2,1)}) custom-call(bf16[64,2,72,128]{3,2,1,0:T(8,128)(2,1)} %get-tuple-element.97.refs_0_, bf16[1120,1152]{1,0:T(8,128)(2,1)S(1)} %get-tuple-element.98.refs_1_, bf16[1792,512]{1,0:T(8,128)(2,1)} %get-tuple-element.99.refs_2_, ...), custom_call_target="tpu_custom_call" | custom-call | flops 1 | bytes 1 | tf_op jit(solution)/shard_map/cond/branch_0_fun/pallas_call | solution.py:48
  136.5 5.8 %shard_map.89 = (bf16[320,1792]{1,0:T(8,128)(2,1)}, f32[320,1024]{1,0:T(8,128)}, bf16[320,1024]{1,0:T(8,128)(2,1)}) custom-call(bf16[64,2,72,128]{3,2,1,0:T(8,128)(2,1)} %all-to-all-done.1.refs_0_, bf16[1120,1152]{1,0:T(8,128)(2,1)S(1)} %fusion.1.refs_1_, bf16[1792,512]{1,0:T(8,128)(2,1)} %copy-done.2, bf16[1792,512]{1,0:T(8,128)(2,1)} %collective-permute-done.1.refs_3_.refs_5_), custom_call_target="tpu_custom_call" | custom-call | flops 1 | bytes 1 | tf_op jit(solution)/shard_map/pallas_call | solution.py:48
  142.9 11.0 %all-to-all-done.2.refs_0_ = bf16[64,1,72,128]{3,2,1,0:T(8,128)(2,1)} async-done(((bf16[64,1,72,128]{3,2,1,0:T(8,128)(2,1)}), bf16[64,1,72,128]{3,2,1,0:T(8,128)(2,1)}, u32[]{:S(2)}, u32[]{:S(2)}) %all-to-all-start.2) | async-done | bytes 1179680 | tf_op jit(solution)/shard_map/all_to_all | solution.py:267
  153.9 4.8 %shard_map.88 = bf16[64,3584]{1,0:T(8,128)(2,1)} custom-call(bf16[64,1,72,128]{3,2,1,0:T(8,128)(2,1)} %all-to-all-done.2.refs_0_, bf16[1120,1152]{1,0:T(8,128)(2,1)S(1)} %fusion.1.refs_1_, bf16[2,64,3584]{2,1,0:T(8,128)(2,1)S(1)} %copy-done.8, bf16[64,160]{1,0:T(8,128)(2,1)} %get-tuple-element.287.refs_3_), custom_call_target="tpu_custom_call" | custom-call | flops 1 | bytes 1 | tf_op jit(solution)/shard_map/pallas_call | solution.py:48
  158.8 1.3 collective-permute-start.6
  160.2 14.0 %collective-permute-done.7.refs_1_ = bf16[320,1024]{1,0:T(8,128)(2,1)} collective-permute-done((bf16[320,1024]{1,0:T(8,128)(2,1)}, bf16[320,1024]{1,0:T(8,128)(2,1)}, u32[]{:S(2)}, u32[]{:S(2)}) %collective-permute-start.7) | collective-permute-done | bytes 655392 | tf_op jit(solution)/shard_map/ppermute | solution.py:258
  174.3 40.2 %collective-permute-done.6.refs_2_ = bf16[64,3584]{1,0:T(8,128)(2,1)} collective-permute-done((bf16[64,3584]{1,0:T(8,128)(2,1)}, bf16[64,3584]{1,0:T(8,128)(2,1)}, u32[]{:S(2)}, u32[]{:S(2)}) %collective-permute-start.6) | collective-permute-done | bytes 458784 | tf_op jit(solution)/shard_map/ppermute | solution.py:322
  214.5 10.0 %conditional.6 = ((bf16[320,1024]{1,0:T(8,128)(2,1)}, bf16[320,1024]{1,0:T(8,128)(2,1)}, bf16[64,1,72,128]{3,2,1,0:T(8,128)(2,1)})) conditional(s32[]{:T(128)} %convert_element_type.68, (bf16[64,3584]{1,0:T(8,128)(2,1)}, bf16[1152,1120]{1,0:T(8,128)(2,1)}, bf16[160,64]{0,1:T(8,128)(2,1)}, f32[160,1]{0,1:T(1,128)S(1)}) %tuple.100, ...), branch_computations={%region_10.11_spmd, %region_11.12_spmd} | conditional | flops 1 | bytes 1352997 | solution.py:331
  215.3 1.5 copy.51.refs_2_
  216.8 5.7 %branch_0_fun.6 = bf16[64,1,72,128]{3,2,1,0:T(8,128)(2,1)} custom-call(bf16[64,3584]{1,0:T(8,128)(2,1)} %get-tuple-element.105.refs_0_, bf16[1152,1120]{1,0:T(8,128)(2,1)} %get-tuple-element.106.refs_1_, bf16[160,64]{1,0:T(8,128)(2,1)} %copy.51.refs_2_, f32[160,1]{1,0:T(8,128)} %copy.52.refs_3_), custom_call_target="tpu_custom_call" | custom-call | flops 1 | bytes 1 | tf_op jit(solution)/shard_map/cond/branch_0_fun/pallas_call | solution.py:48
  224.5 33.2 %all_to_all.34 = bf16[64,1,72,128]{3,2,1,0:T(8,128)(2,1)S(1)} all-to-all(bf16[64,1,72,128]{3,2,1,0:T(8,128)(2,1)} %get-tuple-element.200), channel_id=1, replica_groups=mesh['section'=2,'dp'=2,'pair'=32,'half'=2] {'pair','half'}, dimensions={0} | all-to-all | bytes 2359296 | tf_op jit(solution)/shard_map/all_to_all | solution.py:267
  257.7 7.3 %conditional.7 = (bf16[64,3584]{1,0:T(8,128)(2,1)}, bf16[320,1792]{1,0:T(8,128)(2,1)}, f32[320,1024]{1,0:T(8,128)}, bf16[320,1024]{1,0:T(8,128)(2,1)S(1)}) conditional(s32[]{:T(128)} %convert_element_type.68, (bf16[64,1,72,128]{3,2,1,0:T(8,128)(2,1)S(1)}, bf16[1120,1152]{1,0:T(8,128)(2,1)S(1)}, bf16[512,1792]{1,0:T(8,128)(2,1)S(1)}, ...), branch_computations={%region_12.13_spmd, %region_13.14_spmd} | conditional | flops 1 | bytes 13434969 | solution.py:341
  257.7 5.4 %branch_0_fun.7 = (bf16[320,1792]{1,0:T(8,128)(2,1)}, f32[320,1024]{1,0:T(8,128)}, bf16[320,1024]{1,0:T(8,128)(2,1)S(1)}) custom-call(bf16[64,1,72,128]{3,2,1,0:T(8,128)(2,1)S(1)} %get-tuple-element.117.refs_0_, bf16[1120,1152]{1,0:T(8,128)(2,1)S(1)} %get-tuple-element.118.refs_1_, bf16[512,1792]{1,0:T(8,128)(2,1)S(1)} %get-tuple-element.119.refs_2_, ...), custom_call_target="tpu_custom_call" | custom-call | flops 1 | bytes 1 | tf_op jit(solution)/shard_map/cond/branch_0_fun/pallas_call | solution.py:48
  263.1 1.9 copy.71
  265.8 1.3 collective-permute-start.9
  268.5 20.2 %collective-permute-done.9.refs_0_.refs_2_ = bf16[64,3584]{1,0:T(8,128)(2,1)S(1)} collective-permute-done((bf16[64,3584]{1,0:T(8,128)(2,1)}, bf16[64,3584]{1,0:T(8,128)(2,1)S(1)}, u32[]{:S(2)}, u32[]{:S(2)}) %collective-permute-start.9) | collective-permute-done | bytes 458784 | tf_op jit(solution)/shard_map/ppermute | solution.py:342
  289.5 5.8 %shard_map.90 = bf16[64,1,72,128]{3,2,1,0:T(8,128)(2,1)} custom-call(bf16[64,3584]{1,0:T(8,128)(2,1)} %copy-done.15, bf16[1152,1120]{1,0:T(8,128)(2,1)} %fusion.refs_6_.refs_1_, bf16[160,64]{1,0:T(8,128)(2,1)} %copy.53.refs_2_, f32[160,1]{1,0:T(8,128)} %copy.54.refs_3_), custom_call_target="tpu_custom_call" | custom-call | flops 1 | bytes 1 | tf_op jit(solution)/shard_map/pallas_call | solution.py:48
  295.3 7.3 %all-to-all-start.4 = ((bf16[64,1,72,128]{3,2,1,0:T(8,128)(2,1)}), bf16[64,1,72,128]{3,2,1,0:T(8,128)(2,1)}, u32[]{:S(2)}, u32[]{:S(2)}) async-start(bf16[64,1,72,128]{3,2,1,0:T(8,128)(2,1)} %shard_map.90), calls=%async_computation.4 | async-start | bytes 2359296 | tf_op jit(solution)/shard_map/all_to_all | solution.py:267
  302.7 1.2 collective-permute-start.10
  303.9 21.2 %collective-permute-done.10.refs_3_ = bf16[320,1024]{1,0:T(8,128)(2,1)S(1)} collective-permute-done((bf16[320,1024]{1,0:T(8,128)(2,1)S(1)}, bf16[320,1024]{1,0:T(8,128)(2,1)S(1)}, u32[]{:S(2)}, u32[]{:S(2)}) %collective-permute-start.10) | collective-permute-done | bytes 655392 | tf_op jit(solution)/shard_map/ppermute | solution.py:258
  326.0 8.3 %shard_map.91 = (bf16[320,1024]{1,0:T(8,128)(2,1)}, bf16[320,1024]{1,0:T(8,128)(2,1)}, bf16[64,1,72,128]{3,2,1,0:T(8,128)(2,1)}) custom-call(f32[320,1024]{1,0:T(8,128)} %get-tuple-element.196.refs_0_, bf16[320,1024]{1,0:T(8,128)(2,1)} %collective-permute-done.7.refs_1_, f32[320,1024]{1,0:T(8,128)} %get-tuple-element.203.refs_2_, ...), custom_call_target="tpu_custom_call" | custom-call | flops 1 | bytes 1 | tf_op jit(solution)/shard_map/pallas_call | solution.py:48
  335.3 6.0 %shard_map.92 = (bf16[320,1792]{1,0:T(8,128)(2,1)}, f32[320,1024]{1,0:T(8,128)}, bf16[320,1024]{1,0:T(8,128)(2,1)}) custom-call(bf16[64,1,72,128]{3,2,1,0:T(8,128)(2,1)} %all-to-all-done.4.refs_0_, bf16[1120,1152]{1,0:T(8,128)(2,1)S(1)} %fusion.1.refs_1_, bf16[512,1792]{1,0:T(8,128)(2,1)} %copy-done.4, bf16[512,1792]{1,0:T(8,128)(2,1)} %copy-done.6), custom_call_target="tpu_custom_call" | custom-call | flops 1 | bytes 1 | tf_op jit(solution)/shard_map/pallas_call | solution.py:48
  341.3 16.8 %all-to-all-start.5 = ((bf16[64,1,72,128]{3,2,1,0:T(8,128)(2,1)}), bf16[64,1,72,128]{3,2,1,0:T(8,128)(2,1)}, u32[]{:S(2)}, u32[]{:S(2)}) async-start(bf16[64,1,72,128]{3,2,1,0:T(8,128)(2,1)} %get-tuple-element.209), calls=%async_computation.5 | async-start | bytes 2359296 | tf_op jit(solution)/shard_map/all_to_all | solution.py:267
  358.2 1.5 broadcast_select_fusion.7
  359.7 1.3 collective-permute-start.11
  361.0 1.7 broadcast_select_fusion.5
  362.7 1.6 pad_maximum_fusion.1
  364.2 1.5 pad_maximum_fusion
  365.8 16.6 %collective-permute-done.11.refs_3_ = bf16[320,1024]{1,0:T(8,128)(2,1)S(1)} collective-permute-done((bf16[320,1024]{1,0:T(8,128)(2,1)S(1)}, bf16[320,1024]{1,0:T(8,128)(2,1)S(1)}, u32[]{:S(2)}, u32[]{:S(2)}) %collective-permute-start.11) | collective-permute-done | bytes 655392 | tf_op jit(solution)/shard_map/ppermute | solution.py:258
  383.2 7.4 %shard_map.93 = (bf16[320,1024]{1,0:T(8,128)(2,1)}, bf16[320,1024]{1,0:T(8,128)(2,1)}, bf16[64,1,72,128]{3,2,1,0:T(8,128)(2,1)}) custom-call(f32[320,1024]{1,0:T(8,128)} %get-tuple-element.198.refs_0_, bf16[320,1024]{1,0:T(8,128)(2,1)} %collective-permute-done.8.refs_1_, f32[320,1024]{1,0:T(8,128)} %get-tuple-element.210.refs_2_, ...), custom_call_target="tpu_custom_call" | custom-call | flops 1 | bytes 1 | tf_op jit(solution)/shard_map/pallas_call | solution.py:48
  390.8 1.6 broadcast_select_fusion.8
  392.8 1.6 convolution_convert_fusion
  394.5 2.2 collective-permute-start.14
  396.9 1.5 copy-done.13
  398.4 1.6 convolution_convert_fusion.1
  400.1 2.9 add_convert_fusion
  403.0 4.7 collective-permute-start.15
  407.7 2.9 add_convert_fusion.1
  410.5 1.9 collective-permute-start.13
  412.5 14.1 %all-to-all-start.6 = ((bf16[64,1,72,128]{3,2,1,0:T(8,128)(2,1)}), bf16[64,1,72,128]{3,2,1,0:T(8,128)(2,1)}, u32[]{:S(2)}, u32[]{:S(2)}) async-start(bf16[64,1,72,128]{3,2,1,0:T(8,128)(2,1)} %get-tuple-element.220), calls=%async_computation.6 | async-start | bytes 2359296 | tf_op jit(solution)/shard_map/all_to_all | solution.py:267
  426.5 4.8 %shard_map.94 = bf16[64,3584]{1,0:T(8,128)(2,1)} custom-call(bf16[64,1,72,128]{3,2,1,0:T(8,128)(2,1)} %all-to-all-done.5.refs_0_, bf16[1120,1152]{1,0:T(8,128)(2,1)S(1)} %fusion.1.refs_1_, bf16[64,3584]{1,0:T(8,128)(2,1)} %collective-permute-done.6.refs_2_, bf16[64,160]{1,0:T(8,128)(2,1)} %get-tuple-element.287.refs_3_), custom_call_target="tpu_custom_call" | custom-call | flops 1 | bytes 1 | tf_op jit(solution)/shard_map/pallas_call | solution.py:48
  432.5 2.9 broadcast_select_fusion
  435.5 25.3 %collective-permute-done.13 = bf16[1792,512]{1,0:T(8,128)(2,1)} collective-permute-done((bf16[1792,512]{1,0:T(8,128)(2,1)}, bf16[1792,512]{1,0:T(8,128)(2,1)}, u32[]{:S(2)}, u32[]{:S(2)}) %collective-permute-start.13) | collective-permute-done | bytes 1835040 | tf_op jit(solution)/shard_map/ppermute | solution.py:262
  460.8 2.9 broadcast_select_fusion.2
  463.7 4.0 shard_map.95
  (112 shorter events, 20.4 us)
Async XLA Ops:
  0.6 48.8 %collective-permute-start.3 = (bf16[512,1792]{1,0:T(8,128)(2,1)}, bf16[512,1792]{1,0:T(8,128)(2,1)}, u32[]{:S(2)}, u32[]{:S(2)}) collective-permute-start(bf16[512,1792]{1,0:T(8,128)(2,1)} %bitcast.34), channel_id=1, source_target_pairs={{1,64},{64,1},{3,66},{66,3},{5,68},{68,5},{7,70},{70,7},{9,72},{72... | collective-permute-start | bytes 5505032 | tf_op jit(solution)/shard_map/ppermute | solution.py:262
  5.2 46.9 %collective-permute-start = (bf16[1792,512]{1,0:T(8,128)(2,1)}, bf16[1792,512]{1,0:T(8,128)(2,1)}, u32[]{:S(2)}, u32[]{:S(2)}) collective-permute-start(bf16[1792,512]{1,0:T(8,128)(2,1)} %bitcast.35), channel_id=1, source_target_pairs={{1,64},{64,1},{3,66},{66,3},{5,68},{68,5},{7,70},{70,7},{9,72},{72... | collective-permute-start | bytes 5505032 | tf_op jit(solution)/shard_map/ppermute | solution.py:262
  9.2 1.0 copy-start.29
  9.2 3.8 copy-start.30
  9.2 4.0 copy-start.7
  35.0 83.8 %all-to-all-start.1 = ((bf16[64,2,72,128]{3,2,1,0:T(8,128)(2,1)}), bf16[64,2,72,128]{3,2,1,0:T(8,128)(2,1)}, u32[]{:S(2)}, u32[]{:S(2)}) async-start(bf16[64,2,72,128]{3,2,1,0:T(8,128)(2,1)} %get-tuple-element.186), calls=%async_computation.1 | async-start | bytes 4718592 | tf_op jit(solution)/shard_map/all_to_all | solution.py:267
  49.5 2.7 copy-start.17
  51.9 3.9 copy-start.4
  51.9 3.9 collective-permute-start.4
  54.2 57.3 %copy-start.2 = (bf16[1792,512]{1,0:T(8,128)(2,1)}, bf16[1792,512]{1,0:T(8,128)(2,1)S(1)}, u32[]{:S(2)}) copy-start(bf16[1792,512]{1,0:T(8,128)(2,1)S(1)} %broadcast_select_fusion.3.refs_2_.refs_4_) | copy-start | bytes 5505028
  54.2 9.8 %collective-permute-start.1 = (bf16[1792,512]{1,0:T(8,128)(2,1)S(1)}, bf16[1792,512]{1,0:T(8,128)(2,1)}, u32[]{:S(2)}, u32[]{:S(2)}) collective-permute-start(bf16[1792,512]{1,0:T(8,128)(2,1)S(1)} %broadcast_select_fusion.3.refs_2_.refs_4_), channel_id=1, source_target_pairs={{0,64},{64,0},{1,65},{65,1},{2,66},{66,2},{3,67},{67,3},{4,68},{68... | collective-permute-start | bytes 5505032 | tf_op jit(solution)/shard_map/ppermute | solution.py:258
  55.7 6.5 %copy-start.6 = (bf16[512,1792]{1,0:T(8,128)(2,1)}, bf16[512,1792]{1,0:T(8,128)(2,1)S(1)}, u32[]{:S(2)}) copy-start(bf16[512,1792]{1,0:T(8,128)(2,1)S(1)} %collective-permute-done.4.refs_3_) | copy-start | bytes 5505028
  62.3 49.2 %copy-start = (bf16[1152,1120]{1,0:T(8,128)(2,1)S(1)}, bf16[1152,1120]{1,0:T(8,128)(2,1)}, u32[]{:S(2)}) copy-start(bf16[1152,1120]{1,0:T(8,128)(2,1)} %fusion.refs_6_.refs_1_) | copy-start | bytes 7741444
  62.3 34.1 %collective-permute-start.5 = (bf16[320,1024]{1,0:T(8,128)(2,1)}, bf16[320,1024]{1,0:T(8,128)(2,1)S(1)}, u32[]{:S(2)}, u32[]{:S(2)}) collective-permute-start(bf16[320,1024]{1,0:T(8,128)(2,1)} %get-tuple-element.192), channel_id=1, source_target_pairs={{0,1},{1,0},{2,3},{3,2},{4,5},{5,4},{6,7},{7,6},{8,9},{9,8},{10,11... | collective-permute-start | bytes 1966088 | tf_op jit(solution)/shard_map/ppermute | solution.py:258
  69.8 41.6 %collective-permute-start.2 = (bf16[320,1024]{1,0:T(8,128)(2,1)}, bf16[320,1024]{1,0:T(8,128)(2,1)}, u32[]{:S(2)}, u32[]{:S(2)}) collective-permute-start(bf16[320,1024]{1,0:T(8,128)(2,1)} %get-tuple-element.190), channel_id=1, source_target_pairs={{0,1},{1,0},{2,3},{3,2},{4,5},{5,4},{6,7},{7,6},{8,9},{9,8},{10,11... | collective-permute-start | bytes 1966088 | tf_op jit(solution)/shard_map/ppermute | solution.py:258
  96.4 15.1 %copy-start.21 = (bf16[320,1024]{1,0:T(8,128)(2,1)}, bf16[320,1024]{1,0:T(8,128)(2,1)S(1)}, u32[]{:S(2)}) copy-start(bf16[320,1024]{1,0:T(8,128)(2,1)S(1)} %collective-permute-done.5.refs_3_) | copy-start | bytes 1966084
  118.9 35.0 %all-to-all-start.2 = ((bf16[64,1,72,128]{3,2,1,0:T(8,128)(2,1)}), bf16[64,1,72,128]{3,2,1,0:T(8,128)(2,1)}, u32[]{:S(2)}, u32[]{:S(2)}) async-start(bf16[64,1,72,128]{3,2,1,0:T(8,128)(2,1)} %get-tuple-element.194), calls=%async_computation.2 | async-start | bytes 2359296 | tf_op jit(solution)/shard_map/all_to_all | solution.py:267
  135.4 18.5 %copy-start.8 = (bf16[2,64,3584]{2,1,0:T(8,128)(2,1)S(1)}, bf16[2,64,3584]{2,1,0:T(8,128)(2,1)}, u32[]{:S(2)}) copy-start(bf16[2,64,3584]{2,1,0:T(8,128)(2,1)} %refs_2_.1) | copy-start | bytes 2752516
  135.4 24.8 %collective-permute-start.8 = (bf16[320,1024]{1,0:T(8,128)(2,1)}, bf16[320,1024]{1,0:T(8,128)(2,1)}, u32[]{:S(2)}, u32[]{:S(2)}) collective-permute-start(bf16[320,1024]{1,0:T(8,128)(2,1)} %get-tuple-element.199), channel_id=1, source_target_pairs={{0,1},{1,0},{2,3},{3,2},{4,5},{5,4},{6,7},{7,6},{8,9},{9,8},{10,11... | collective-permute-start | bytes 1966088 | tf_op jit(solution)/shard_map/ppermute | solution.py:258
  142.3 32.0 %collective-permute-start.7 = (bf16[320,1024]{1,0:T(8,128)(2,1)}, bf16[320,1024]{1,0:T(8,128)(2,1)}, u32[]{:S(2)}, u32[]{:S(2)}) collective-permute-start(bf16[320,1024]{1,0:T(8,128)(2,1)} %get-tuple-element.197), channel_id=1, source_target_pairs={{0,1},{1,0},{2,3},{3,2},{4,5},{5,4},{6,7},{7,6},{8,9},{9,8},{10,11... | collective-permute-start | bytes 1966088 | tf_op jit(solution)/shard_map/ppermute | solution.py:258
  158.8 55.7 %collective-permute-start.6 = (bf16[64,3584]{1,0:T(8,128)(2,1)}, bf16[64,3584]{1,0:T(8,128)(2,1)}, u32[]{:S(2)}, u32[]{:S(2)}) collective-permute-start(bf16[64,3584]{1,0:T(8,128)(2,1)} %shard_map.88), channel_id=1, source_target_pairs={{128,0},{129,1},{130,2},{131,3},{132,4},{133,5},{134,6},{135,7},{1... | collective-permute-start | bytes 1376264 | tf_op jit(solution)/shard_map/ppermute | solution.py:322
  224.5 33.2 %copy-start.5 = (bf16[512,1792]{1,0:T(8,128)(2,1)S(1)}, bf16[512,1792]{1,0:T(8,128)(2,1)}, u32[]{:S(2)}) copy-start(bf16[512,1792]{1,0:T(8,128)(2,1)} %copy-done.4) | copy-start | bytes 5505028
  224.5 33.2 %copy-start.27 = (bf16[64,160]{1,0:T(8,128)(2,1)S(1)}, bf16[64,160]{1,0:T(8,128)(2,1)}, u32[]{:S(2)}) copy-start(bf16[64,160]{1,0:T(8,128)(2,1)} %get-tuple-element.285.refs_3_) | copy-start | bytes 61444
  264.9 0.8 copy-start.32
  265.8 23.0 %collective-permute-start.9 = (bf16[64,3584]{1,0:T(8,128)(2,1)}, bf16[64,3584]{1,0:T(8,128)(2,1)S(1)}, u32[]{:S(2)}, u32[]{:S(2)}) collective-permute-start(bf16[64,3584]{1,0:T(8,128)(2,1)} %get-tuple-element.202), channel_id=1, source_target_pairs={{128,0},{129,1},{130,2},{131,3},{132,4},{133,5},{134,6},{135,7},{1... | collective-permute-start | bytes 1376264 | tf_op jit(solution)/shard_map/ppermute | solution.py:342
  288.8 0.8 copy-start.15
  295.3 7.3 %copy-start.33 = (bf16[320,1024]{1,0:T(8,128)(2,1)S(1)}, bf16[320,1024]{1,0:T(8,128)(2,1)}, u32[]{:S(2)}) copy-start(bf16[320,1024]{1,0:T(8,128)(2,1)} %copy-done.32) | copy-start | bytes 1966084
  295.3 40.0 %all-to-all-start.4 = ((bf16[64,1,72,128]{3,2,1,0:T(8,128)(2,1)}), bf16[64,1,72,128]{3,2,1,0:T(8,128)(2,1)}, u32[]{:S(2)}, u32[]{:S(2)}) async-start(bf16[64,1,72,128]{3,2,1,0:T(8,128)(2,1)} %shard_map.90), calls=%async_computation.4 | async-start | bytes 2359296 | tf_op jit(solution)/shard_map/all_to_all | solution.py:267
  302.7 22.5 %collective-permute-start.10 = (bf16[320,1024]{1,0:T(8,128)(2,1)S(1)}, bf16[320,1024]{1,0:T(8,128)(2,1)S(1)}, u32[]{:S(2)}, u32[]{:S(2)}) collective-permute-start(bf16[320,1024]{1,0:T(8,128)(2,1)S(1)} %copy-done.33), channel_id=1, source_target_pairs={{0,1},{1,0},{2,3},{3,2},{4,5},{5,4},{6,7},{7,6},{8,9},{9,8},{10,11... | collective-permute-start | bytes 1966088 | tf_op jit(solution)/shard_map/ppermute | solution.py:258
  325.1 0.9 copy-start.22
  341.3 18.4 %copy-start.31 = (bf16[320,1024]{1,0:T(8,128)(2,1)S(1)}, bf16[320,1024]{1,0:T(8,128)(2,1)}, u32[]{:S(2)}) copy-start(bf16[320,1024]{1,0:T(8,128)(2,1)} %get-tuple-element.211) | copy-start | bytes 1966084
  341.3 49.5 %all-to-all-start.5 = ((bf16[64,1,72,128]{3,2,1,0:T(8,128)(2,1)}), bf16[64,1,72,128]{3,2,1,0:T(8,128)(2,1)}, u32[]{:S(2)}, u32[]{:S(2)}) async-start(bf16[64,1,72,128]{3,2,1,0:T(8,128)(2,1)} %get-tuple-element.209), calls=%async_computation.5 | async-start | bytes 2359296 | tf_op jit(solution)/shard_map/all_to_all | solution.py:267
  358.1 2.9 copy-start.9
  358.1 2.9 copy-start.18
  358.1 2.9 copy-start.19
  359.7 22.7 %collective-permute-start.11 = (bf16[320,1024]{1,0:T(8,128)(2,1)S(1)}, bf16[320,1024]{1,0:T(8,128)(2,1)S(1)}, u32[]{:S(2)}, u32[]{:S(2)}) collective-permute-start(bf16[320,1024]{1,0:T(8,128)(2,1)S(1)} %copy-done.31), channel_id=1, source_target_pairs={{0,1},{1,0},{2,3},{3,2},{4,5},{5,4},{6,7},{7,6},{8,9},{9,8},{10,11... | collective-permute-start | bytes 1966088 | tf_op jit(solution)/shard_map/ppermute | solution.py:258
  364.2 19.0 %copy-start.1 = (bf16[1152,1120]{1,0:T(8,128)(2,1)S(1)}, bf16[1152,1120]{1,0:T(8,128)(2,1)}, u32[]{:S(2)}) copy-start(bf16[1152,1120]{1,0:T(8,128)(2,1)} %fusion.refs_6_.refs_1_) | copy-start | bytes 7741444
  364.2 19.0 %copy-start.3 = (bf16[1792,512]{1,0:T(8,128)(2,1)S(1)}, bf16[1792,512]{1,0:T(8,128)(2,1)}, u32[]{:S(2)}) copy-start(bf16[1792,512]{1,0:T(8,128)(2,1)} %copy-done.2) | copy-start | bytes 5505028
  382.4 0.8 copy-start.20
  383.2 7.6 %copy-start.11 = (bf16[320,1024]{1,0:T(8,128)(2,1)S(1)}, bf16[320,1024]{1,0:T(8,128)(2,1)}, u32[]{:S(2)}) copy-start(bf16[320,1024]{1,0:T(8,128)(2,1)} %get-tuple-element.228) | copy-start | bytes 1966084
  390.8 2.0 copy-start.14
  392.8 3.9 copy-start.12
  392.8 3.9 copy-start.24
  392.8 3.9 copy-start.25
  392.8 3.9 copy-start.26
  394.5 5.7 %collective-permute-start.14 = (bf16[512,1792]{1,0:T(8,128)(2,1)S(1)}, bf16[512,1792]{1,0:T(8,128)(2,1)S(1)}, u32[]{:S(2)}, u32[]{:S(2)}) collective-permute-start(bf16[512,1792]{1,0:T(8,128)(2,1)S(1)} %convolution_convert_fusion), channel_id=1, source_target_pairs={{0,64},{64,0},{1,65},{65,1},{2,66},{66,2},{3,67},{67,3},{4,68},{68... | collective-permute-start | bytes 5505032 | tf_op jit(solution)/shard_map/ppermute | solution.py:258
  396.7 1.6 copy-start.13
  400.0 7.7 %collective-permute-start.12 = (bf16[1792,512]{1,0:T(8,128)(2,1)S(1)}, bf16[1792,512]{1,0:T(8,128)(2,1)S(1)}, u32[]{:S(2)}, u32[]{:S(2)}) collective-permute-start(bf16[1792,512]{1,0:T(8,128)(2,1)S(1)} %convolution_convert_fusion.1), channel_id=1, source_target_pairs={{0,64},{64,0},{1,65},{65,1},{2,66},{66,2},{3,67},{67,3},{4,68},{68... | collective-permute-start | bytes 5505032 | tf_op jit(solution)/shard_map/ppermute | solution.py:258
  403.0 29.5 %collective-permute-start.15 = (bf16[512,1792]{1,0:T(8,128)(2,1)}, bf16[512,1792]{1,0:T(8,128)(2,1)}, u32[]{:S(2)}, u32[]{:S(2)}) collective-permute-start(bf16[512,1792]{1,0:T(8,128)(2,1)} %add_convert_fusion), channel_id=1, source_target_pairs={{1,64},{64,1},{3,66},{66,3},{5,68},{68,5},{7,70},{70,7},{9,72},{72... | collective-permute-start | bytes 5505032 | tf_op jit(solution)/shard_map/ppermute | solution.py:262
  410.5 50.2 %collective-permute-start.13 = (bf16[1792,512]{1,0:T(8,128)(2,1)}, bf16[1792,512]{1,0:T(8,128)(2,1)}, u32[]{:S(2)}, u32[]{:S(2)}) collective-permute-start(bf16[1792,512]{1,0:T(8,128)(2,1)} %add_convert_fusion.1), channel_id=1, source_target_pairs={{1,64},{64,1},{3,66},{66,3},{5,68},{68,5},{7,70},{70,7},{9,72},{72... | collective-permute-start | bytes 5505032 | tf_op jit(solution)/shard_map/ppermute | solution.py:262
  412.5 51.3 %all-to-all-start.6 = ((bf16[64,1,72,128]{3,2,1,0:T(8,128)(2,1)}), bf16[64,1,72,128]{3,2,1,0:T(8,128)(2,1)}, u32[]{:S(2)}, u32[]{:S(2)}) async-start(bf16[64,1,72,128]{3,2,1,0:T(8,128)(2,1)} %get-tuple-element.220), calls=%async_computation.6 | async-start | bytes 2359296 | tf_op jit(solution)/shard_map/all_to_all | solution.py:267
  426.5 4.9 %copy-start.16 = (bf16[64,3584]{1,0:T(8,128)(2,1)S(1)}, bf16[64,3584]{1,0:T(8,128)(2,1)}, u32[]{:S(2)}) copy-start(bf16[64,3584]{1,0:T(8,128)(2,1)} %shard_map.88) | copy-start | bytes 1376260
  435.5 28.3 %copy-start.28 = (bf16[64,160]{1,0:T(8,128)(2,1)S(1)}, bf16[64,160]{1,0:T(8,128)(2,1)}, u32[]{:S(2)}) copy-start(bf16[64,160]{1,0:T(8,128)(2,1)} %get-tuple-element.285.refs_3_) | copy-start | bytes 61444

commit v4 on v1

--- a/solution.py
+++ b/solution.py
@@ -309,9 +309,10 @@
     fifth = send(dispatch([low_in1], [place[1]], [weight[1]], packer, chunk_rows))
     low_active0, low_grads0, back2 = turn(own_b0, got_b0, own_d, got_d, ups, packer, chunk_rows)
     fifth, back2 = lax.optimization_barrier((fifth, back2))
+    rows_e, own_e, sent_e = arrive(fifth, 0, unpacker, downs)
+    sent_e, back2 = lax.optimization_barrier((sent_e, back2))
+    got_e = swap(sent_e, "half")
     sixth = send(back2)
-    rows_e, own_e, sent_e = arrive(fifth, 0, unpacker, downs)
-    got_e = swap(sent_e, "half")
     low_active1, low_grads1, back3 = turn(own_b1, got_b1, own_e, got_e, ups, packer, chunk_rows)
     seventh = send(back3)
 

time: 470 us -> 477 us (1.015)
  the two profiles are of different devices: /device:TPU:35 before, /device:TPU:1 now
where the time goes in v4:
time: 477 us; the launch traced here: 468 us
  waiting for transfers between devices  181 us (38%)
  starting transfers between devices  84.1 us (18%)
  Pallas kernels  72.8 us (15%)
  local copies, waits for them, and re-layouts  52.2 us (11%)
  blocking collectives  35.2 us (7%)
  other arithmetic  23.5 us (5%)
  matrix products  8.96 us (2%)
  loops' own time  8.25 us (2%)
    ppermute x10, waiting for transfers between devices, swap(): return lax.ppermute(value, axis, [(0, 1), (1, 0)])  108 us
    pallas_call x17, Pallas kernels, call(): pl.pallas_call(body, out_shape=outs, in_specs=[smem] * scalars + [spec] *...  72.8 us
    all_to_all x5, starting transfers between devices, send(): lax.all_to_all(chunks, PAIRED, split_axis=0, concat_axis=0, tiled=True)  61.5 us
    unnamed x138, local copies, waits for them, and re-layouts  45.9 us
    all_to_all x1, blocking collectives, send(): lax.all_to_all(chunks, PAIRED, split_axis=0, concat_axis=0, tiled=True)  35.2 us
    ppermute x4, waiting for transfers between devices, cross(): moved = lax.ppermute(value, ('dp', 'half'), [(1, 2), (2, 1)])  31 us
    ppermute x1, waiting for transfers between devices, on_device(): low_in0 = lax.ppermute(top_out0, 'section', [(1, 0)])  24.6 us
    ppermute x1, waiting for transfers between devices, on_device(): low_in1 = lax.ppermute(top_out1, 'section', [(1, 0)])  15 us
  transfers between devices with their start and end apart: 21, of which 12 were waited for; matrix products, arithmetic and copies ran while one was open for 7% of the time, Pallas kernels for 12%

profile of v4, /device:TPU:1, one launch (start us, length us, event | category | flops | bytes accessed | tf_op | source)
XLA Modules:
  0.0 468.0 jit_solution(10559378397855332013)
XLA Ops:
  0.6 4.6 collective-permute-start.3
  5.2 1.9 collective-permute-start
  8.2 2.0 fusion.pack_ref.refs_3_
  11.7 2.0 slice_bitcast_fusion.4
  14.0 17.7 %conditional.1 = (bf16[64,2,72,128]{3,2,1,0:T(8,128)(2,1)}, bf16[64,2,72,128]{3,2,1,0:T(8,128)(2,1)}) conditional(s32[]{:T(128)} %convert_element_type.64, (bf16[64,3584]{1,0:T(8,128)(2,1)}, bf16[64,3584]{1,0:T(8,128)(2,1)S(1)}, bf16[160,64]{0,1:T(8,128)(2,1)S(1)}, bf16[160,64]{0,1:T(8,128)(2,1)S(1)}, bf16[1152,1120]{1,0:T(8,128)(2,1)}) %tuple.23, ...), branch_computations={%region_6.7_spmd, %region_7.8_spmd} | conditional | flops 2 | bytes 22105352 | solution.py:280
  14.3 7.5 %branch_0_fun.1 = bf16[64,2,72,128]{3,2,1,0:T(8,128)(2,1)} custom-call(bf16[64,3584]{1,0:T(8,128)(2,1)} %get-tuple-element.17.refs_0_, bf16[64,3584]{1,0:T(8,128)(2,1)S(1)} %get-tuple-element.28.refs_1_, bf16[160,64]{1,0:T(8,128)(2,1)S(1)} %copy.45.refs_2_, bf16[160,64]{1,0:T(8,128)(2,1)S(1)} %copy.46.refs_3_, ...), custom_call_target="tpu_custom_call" | custom-call | flops 1 | bytes 1 | tf_op jit(solution)/shard_map/cond/branch_0_fun/pallas_call | solution.py:26
  21.8 1.7 broadcast.173
  31.7 14.4 %all-to-all-start.1 = ((bf16[64,2,72,128]{3,2,1,0:T(8,128)(2,1)}), bf16[64,2,72,128]{3,2,1,0:T(8,128)(2,1)}, u32[]{:S(2)}, u32[]{:S(2)}) async-start(bf16[64,2,72,128]{3,2,1,0:T(8,128)(2,1)} %get-tuple-element.97), calls=%async_computation.1 | async-start | bytes 4718592 | tf_op jit(solution)/shard_map/all_to_all | solution.py:244
  46.2 2.4 broadcast_select_fusion.1.part0.down0
  48.9 2.1 broadcast_select_fusion.3.part0.up0
  52.4 5.2 %shard_map.86 = (bf16[320,1792]{1,0:T(8,128)(2,1)S(1)}, f32[320,1024]{1,0:T(8,128)S(1)}, bf16[320,1024]{1,0:T(8,128)(2,1)S(1)}) custom-call(bf16[64,2,72,128]{3,2,1,0:T(8,128)(2,1)} %get-tuple-element.98.got, bf16[1120,1152]{1,0:T(8,128)(2,1)S(1)} %fusion.1.unpack_ref, bf16[512,1792]{1,0:T(8,128)(2,1)S(1)} %broadcast_select_fusion.1.part0.down0, ...), custom_call_target="tpu_custom_call" | custom-call | flops 1 | bytes 1 | tf_op jit(solution)/shard_map/pallas_call | solution.py:26
  57.6 1.7 collective-permute-start.5
  59.4 5.2 %shard_map.85 = (bf16[320,1792]{1,0:T(8,128)(2,1)S(1)}, f32[320,1024]{1,0:T(8,128)S(1)}, bf16[320,1024]{1,0:T(8,128)(2,1)S(1)}) custom-call(bf16[64,2,72,128]{3,2,1,0:T(8,128)(2,1)} %get-tuple-element.98.got, bf16[1120,1152]{1,0:T(8,128)(2,1)S(1)} %fusion.1.unpack_ref, bf16[1792,512]{1,0:T(8,128)(2,1)S(1)} %broadcast_select_fusion.3.part0.up0, ...), custom_call_target="tpu_custom_call" | custom-call | flops 1 | bytes 1 | tf_op jit(solution)/shard_map/pallas_call | solution.py:26
  66.1 17.3 %collective-permute-done.5.act_got = bf16[320,1024]{1,0:T(8,128)(2,1)S(1)} collective-permute-done((bf16[320,1024]{1,0:T(8,128)(2,1)S(1)}, bf16[320,1024]{1,0:T(8,128)(2,1)S(1)}, u32[]{:S(2)}, u32[]{:S(2)}) %collective-permute-start.5) | collective-permute-done | bytes 655392 | tf_op jit(solution)/shard_map/ppermute | solution.py:235
  83.5 22.9 %collective-permute-done.2.pre_got = bf16[320,1024]{1,0:T(8,128)(2,1)S(1)} collective-permute-done((bf16[320,1024]{1,0:T(8,128)(2,1)S(1)}, bf16[320,1024]{1,0:T(8,128)(2,1)S(1)}, u32[]{:S(2)}, u32[]{:S(2)}) %collective-permute-start.2) | collective-permute-done | bytes 655392 | tf_op jit(solution)/shard_map/ppermute | solution.py:235
  106.4 3.3 shard_map.87
  112.5 13.8 %all-to-all-start.2 = ((bf16[64,1,72,128]{3,2,1,0:T(8,128)(2,1)}), bf16[64,1,72,128]{3,2,1,0:T(8,128)(2,1)}, u32[]{:S(2)}, u32[]{:S(2)}) async-start(bf16[64,1,72,128]{3,2,1,0:T(8,128)(2,1)} %copy-done.36), calls=%async_computation.2 | async-start | bytes 2359296 | tf_op jit(solution)/shard_map/all_to_all | solution.py:244
  127.8 1.5 copy-done.6
  129.3 1.5 copy-done.11
  130.8 1.5 copy-done.15
  132.3 5.5 %shard_map.90 = (bf16[320,1792]{1,0:T(8,128)(2,1)S(1)}, f32[320,1024]{1,0:T(8,128)S(1)}, bf16[320,1024]{1,0:T(8,128)(2,1)}) custom-call(s32[1]{0:T(128)} %bitcast.14.flag, bf16[64,2,72,128]{3,2,1,0:T(8,128)(2,1)} %all-to-all-done.1.got, bf16[1120,1152]{1,0:T(8,128)(2,1)S(1)} %fusion.1.unpack_ref, bf16[1792,512]{1,0:T(8,128)(2,1)S(1)} %copy-done.1, ...), custom_call_target="tpu_custom_call" | custom-call | flops 1 | bytes 1 | tf_op jit(solution)/shard_map/pallas_call | solution.py:26
  138.9 5.4 %shard_map.89 = (bf16[320,1792]{1,0:T(8,128)(2,1)S(1)}, f32[320,1024]{1,0:T(8,128)S(1)}, bf16[320,1024]{1,0:T(8,128)(2,1)}) custom-call(bf16[64,2,72,128]{3,2,1,0:T(8,128)(2,1)} %all-to-all-done.1.got, bf16[1120,1152]{1,0:T(8,128)(2,1)S(1)} %fusion.1.unpack_ref, bf16[1792,512]{1,0:T(8,128)(2,1)S(1)} %copy-done.1, bf16[1792,512]{1,0:T(8,128)(2,1)S(1)} %copy-done.6), custom_call_target="tpu_custom_call" | custom-call | flops 1 | bytes 1 | tf_op jit(solution)/shard_map/pallas_call | solution.py:26
  148.5 2.5 all-to-all-done.2.got
  152.0 4.0 shard_map.88
  157.5 3.5 collective-permute-done.7.act_got.pre_got
  161.0 14.1 %collective-permute-done.6.pre_got = bf16[320,1024]{1,0:T(8,128)(2,1)} collective-permute-done((bf16[320,1024]{1,0:T(8,128)(2,1)}, bf16[320,1024]{1,0:T(8,128)(2,1)}, u32[]{:S(2)}, u32[]{:S(2)}) %collective-permute-start.6) | collective-permute-done | bytes 655392 | tf_op jit(solution)/shard_map/ppermute | solution.py:235
  175.2 1.5 copy-done.2
  176.7 1.5 copy-done.7
  180.8 5.5 %shard_map.91 = (bf16[320,1024]{1,0:T(8,128)(2,1)S(1)}, bf16[320,1024]{1,0:T(8,128)(2,1)S(1)}, bf16[64,1,72,128]{3,2,1,0:T(8,128)(2,1)S(1)}) custom-call(f32[320,1024]{1,0:T(8,128)S(1)} %copy-done.25, bf16[320,1024]{1,0:T(8,128)(2,1)} %collective-permute-done.6.pre_got, f32[320,1024]{1,0:T(8,128)S(1)} %copy-done.22, ...), custom_call_target="tpu_custom_call" | custom-call | flops 1 | bytes 1 | tf_op jit(solution)/shard_map/pallas_call | solution.py:26
  186.4 24.6 %collective-permute-done.8.refs_0_.incoming = bf16[64,3584]{1,0:T(8,128)(2,1)} collective-permute-done((bf16[64,3584]{1,0:T(8,128)(2,1)}, bf16[64,3584]{1,0:T(8,128)(2,1)}, u32[]{:S(2)}, u32[]{:S(2)}) %collective-permute-start.8) | collective-permute-done | bytes 458784 | tf_op jit(solution)/shard_map/ppermute | solution.py:299
  211.0 3.2 shard_map.92
  214.3 35.2 %all_to_all.34.got = bf16[64,1,72,128]{3,2,1,0:T(8,128)(2,1)S(1)} all-to-all(bf16[64,1,72,128]{3,2,1,0:T(8,128)(2,1)S(1)} %broadcast_select_fusion.4), channel_id=1, replica_groups=mesh['section'=2,'dp'=2,'pair'=32,'half'=2] {'pair','half'}, dimensions={0} | all-to-all | bytes 2359296 | tf_op jit(solution)/shard_map/all_to_all | solution.py:244
  249.5 2.7 shard_map.93
  258.0 2.8 shard_map.94
  263.9 15.0 %collective-permute-done.9.refs_0_.incoming = bf16[64,3584]{1,0:T(8,128)(2,1)} collective-permute-done((bf16[64,3584]{1,0:T(8,128)(2,1)}, bf16[64,3584]{1,0:T(8,128)(2,1)}, u32[]{:S(2)}, u32[]{:S(2)}) %collective-permute-start.9) | collective-permute-done | bytes 458784 | tf_op jit(solution)/shard_map/ppermute | solution.py:304
  278.9 3.2 shard_map.95
  283.1 9.7 %all-to-all-start.4 = ((bf16[64,1,72,128]{3,2,1,0:T(8,128)(2,1)}), bf16[64,1,72,128]{3,2,1,0:T(8,128)(2,1)}, u32[]{:S(2)}, u32[]{:S(2)}) async-start(bf16[64,1,72,128]{3,2,1,0:T(8,128)(2,1)} %copy-done.27), calls=%async_computation.4 | async-start | bytes 2359296 | tf_op jit(solution)/shard_map/all_to_all | solution.py:244
  293.8 26.7 %collective-permute-done.10.act_got = bf16[320,1024]{1,0:T(8,128)(2,1)S(1)} collective-permute-done((bf16[320,1024]{1,0:T(8,128)(2,1)}, bf16[320,1024]{1,0:T(8,128)(2,1)S(1)}, u32[]{:S(2)}, u32[]{:S(2)}) %collective-permute-start.10) | collective-permute-done | bytes 655392 | tf_op jit(solution)/shard_map/ppermute | solution.py:235
  320.5 1.5 copy-done.3
  326.1 5.4 %shard_map.96 = (bf16[320,1024]{1,0:T(8,128)(2,1)S(1)}, bf16[320,1024]{1,0:T(8,128)(2,1)S(1)}, bf16[64,1,72,128]{3,2,1,0:T(8,128)(2,1)S(1)}) custom-call(f32[320,1024]{1,0:T(8,128)S(1)} %copy-done.26, bf16[320,1024]{1,0:T(8,128)(2,1)} %collective-permute-done.6.pre_got, f32[320,1024]{1,0:T(8,128)S(1)} %copy-done.33, ...), custom_call_target="tpu_custom_call" | custom-call | flops 1 | bytes 1 | tf_op jit(solution)/shard_map/pallas_call | solution.py:26
  334.2 1.5 copy-done.13
  337.2 4.1 shard_map.97
  344.3 12.8 %all-to-all-start.5 = ((bf16[64,1,72,128]{3,2,1,0:T(8,128)(2,1)}), bf16[64,1,72,128]{3,2,1,0:T(8,128)(2,1)}, u32[]{:S(2)}, u32[]{:S(2)}) async-start(bf16[64,1,72,128]{3,2,1,0:T(8,128)(2,1)} %copy-done.35), calls=%async_computation.5 | async-start | bytes 2359296 | tf_op jit(solution)/shard_map/all_to_all | solution.py:244
  357.2 1.5 broadcast_select_fusion.8
  359.8 1.7 broadcast_select_fusion.6
  361.5 1.6 pad_maximum_fusion.1
  363.1 1.5 pad_maximum_fusion
  364.6 22.3 %collective-permute-done.11.act_got = bf16[320,1024]{1,0:T(8,128)(2,1)S(1)} collective-permute-done((bf16[320,1024]{1,0:T(8,128)(2,1)}, bf16[320,1024]{1,0:T(8,128)(2,1)S(1)}, u32[]{:S(2)}, u32[]{:S(2)}) %collective-permute-start.11) | collective-permute-done | bytes 655392 | tf_op jit(solution)/shard_map/ppermute | solution.py:235
  387.0 3.3 shard_map.98
  393.1 1.6 broadcast_select_fusion.9
  395.1 1.6 convolution_convert_fusion
  397.6 1.5 copy-done.67
  399.1 1.6 convolution_convert_fusion.1
  400.9 2.9 add_convert_fusion
  403.7 2.7 collective-permute-start.15
  406.5 2.9 add_convert_fusion.1
  409.3 3.0 collective-permute-start.13
  412.3 10.9 %all-to-all-start.6 = ((bf16[64,1,72,128]{3,2,1,0:T(8,128)(2,1)}), bf16[64,1,72,128]{3,2,1,0:T(8,128)(2,1)}, u32[]{:S(2)}, u32[]{:S(2)}) async-start(bf16[64,1,72,128]{3,2,1,0:T(8,128)(2,1)} %copy-done.34), calls=%async_computation.6 | async-start | bytes 2359296 | tf_op jit(solution)/shard_map/all_to_all | solution.py:244
  423.2 3.3 shard_map.99
  426.6 7.3 %collective-permute-done.15 = bf16[512,1792]{1,0:T(8,128)(2,1)} collective-permute-done((bf16[512,1792]{1,0:T(8,128)(2,1)}, bf16[512,1792]{1,0:T(8,128)(2,1)}, u32[]{:S(2)}, u32[]{:S(2)}) %collective-permute-start.15) | collective-permute-done | bytes 1835040 | tf_op jit(solution)/shard_map/ppermute | solution.py:239
  433.9 2.9 broadcast_select_fusion
  436.8 23.7 %collective-permute-done.13 = bf16[1792,512]{1,0:T(8,128)(2,1)} collective-permute-done((bf16[1792,512]{1,0:T(8,128)(2,1)}, bf16[1792,512]{1,0:T(8,128)(2,1)}, u32[]{:S(2)}, u32[]{:S(2)}) %collective-permute-start.13) | collective-permute-done | bytes 1835040 | tf_op jit(solution)/shard_map/ppermute | solution.py:239
  460.5 2.9 broadcast_select_fusion.2
  463.4 3.3 shard_map.100
  (185 shorter events, 49.7 us)
Async XLA Ops:
  0.6 45.5 %collective-permute-start.3 = (bf16[512,1792]{1,0:T(8,128)(2,1)}, bf16[512,1792]{1,0:T(8,128)(2,1)}, u32[]{:S(2)}, u32[]{:S(2)}) collective-permute-start(bf16[512,1792]{1,0:T(8,128)(2,1)} %bitcast.47), channel_id=1, source_target_pairs={{1,64},{64,1},{3,66},{66,3},{5,68},{68,5},{7,70},{70,7},{9,72},{72... | collective-permute-start | bytes 5505032 | tf_op jit(solution)/shard_map/ppermute | solution.py:239
  5.2 43.6 %collective-permute-start = (bf16[1792,512]{1,0:T(8,128)(2,1)}, bf16[1792,512]{1,0:T(8,128)(2,1)}, u32[]{:S(2)}, u32[]{:S(2)}) collective-permute-start(bf16[1792,512]{1,0:T(8,128)(2,1)} %bitcast.48), channel_id=1, source_target_pairs={{1,64},{64,1},{3,66},{66,3},{5,68},{68,5},{7,70},{70,7},{9,72},{72... | collective-permute-start | bytes 5505032 | tf_op jit(solution)/shard_map/ppermute | solution.py:239
  8.2 2.0 copy-start.70
  8.2 5.5 %copy-start.71 = (f32[1,2,64,2]{2,3,1,0:T(2,128)S(1)}, f32[1,2,64,2]{2,3,1,0:T(2,128)}, u32[]{:S(2)}) copy-start(f32[1,2,64,2]{2,3,1,0:T(2,128)} %param.11) | copy-start | bytes 3076
  31.7 80.8 %all-to-all-start.1 = ((bf16[64,2,72,128]{3,2,1,0:T(8,128)(2,1)}), bf16[64,2,72,128]{3,2,1,0:T(8,128)(2,1)}, u32[]{:S(2)}, u32[]{:S(2)}) async-start(bf16[64,2,72,128]{3,2,1,0:T(8,128)(2,1)} %get-tuple-element.97), calls=%async_computation.1 | async-start | bytes 4718592 | tf_op jit(solution)/shard_map/all_to_all | solution.py:244
  46.1 2.7 copy-start.69
  48.5 3.9 copy-start.10
  48.6 3.9 collective-permute-start.4
  51.0 55.4 %copy-start = (bf16[1792,512]{1,0:T(8,128)(2,1)}, bf16[1792,512]{1,0:T(8,128)(2,1)S(1)}, u32[]{:S(2)}) copy-start(bf16[1792,512]{1,0:T(8,128)(2,1)S(1)} %broadcast_select_fusion.3.part0.up0) | copy-start | bytes 5505028
  51.0 8.3 %collective-permute-start.1 = (bf16[1792,512]{1,0:T(8,128)(2,1)S(1)}, bf16[1792,512]{1,0:T(8,128)(2,1)S(1)}, u32[]{:S(2)}, u32[]{:S(2)}) collective-permute-start(bf16[1792,512]{1,0:T(8,128)(2,1)S(1)} %broadcast_select_fusion.3.part0.up0), channel_id=1, source_target_pairs={{0,64},{64,0},{1,65},{65,1},{2,66},{66,2},{3,67},{67,3},{4,68},{68... | collective-permute-start | bytes 5505032 | tf_op jit(solution)/shard_map/ppermute | solution.py:235
  52.4 5.2 %copy-start.14 = (bf16[512,1792]{1,0:T(8,128)(2,1)}, bf16[512,1792]{1,0:T(8,128)(2,1)S(1)}, u32[]{:S(2)}) copy-start(bf16[512,1792]{1,0:T(8,128)(2,1)S(1)} %collective-permute-done.4.part1.down1) | copy-start | bytes 5505028
  57.6 6.9 %copy-start.37 = (bf16[320,1792]{1,0:T(8,128)(2,1)}, bf16[320,1792]{1,0:T(8,128)(2,1)S(1)}, u32[]{:S(2)}) copy-start(bf16[320,1792]{1,0:T(8,128)(2,1)S(1)} %get-tuple-element.125) | copy-start | bytes 3440644
  57.6 48.7 %copy-start.60 = (bf16[1152,1120]{1,0:T(8,128)(2,1)S(1)}, bf16[1152,1120]{1,0:T(8,128)(2,1)}, u32[]{:S(2)}) copy-start(bf16[1152,1120]{1,0:T(8,128)(2,1)} %fusion.pack_ref.refs_3_) | copy-start | bytes 7741444
  57.6 25.8 %collective-permute-start.5 = (bf16[320,1024]{1,0:T(8,128)(2,1)S(1)}, bf16[320,1024]{1,0:T(8,128)(2,1)S(1)}, u32[]{:S(2)}, u32[]{:S(2)}) collective-permute-start(bf16[320,1024]{1,0:T(8,128)(2,1)S(1)} %get-tuple-element.103), channel_id=1, source_target_pairs={{0,1},{1,0},{2,3},{3,2},{4,5},{5,4},{6,7},{7,6},{8,9},{9,8},{10,11... | collective-permute-start | bytes 1966088 | tf_op jit(solution)/shard_map/ppermute | solution.py:235
  59.4 47.0 %copy-start.5 = (bf16[1792,512]{1,0:T(8,128)(2,1)}, bf16[1792,512]{1,0:T(8,128)(2,1)S(1)}, u32[]{:S(2)}) copy-start(bf16[1792,512]{1,0:T(8,128)(2,1)S(1)} %collective-permute-done.1.part1.up1) | copy-start | bytes 5505028
  65.6 40.8 %collective-permute-start.2 = (bf16[320,1024]{1,0:T(8,128)(2,1)S(1)}, bf16[320,1024]{1,0:T(8,128)(2,1)S(1)}, u32[]{:S(2)}, u32[]{:S(2)}) collective-permute-start(bf16[320,1024]{1,0:T(8,128)(2,1)S(1)} %get-tuple-element.101), channel_id=1, source_target_pairs={{0,1},{1,0},{2,3},{3,2},{4,5},{5,4},{6,7},{7,6},{8,9},{9,8},{10,11... | collective-permute-start | bytes 1966088 | tf_op jit(solution)/shard_map/ppermute | solution.py:235
  112.5 38.5 %all-to-all-start.2 = ((bf16[64,1,72,128]{3,2,1,0:T(8,128)(2,1)}), bf16[64,1,72,128]{3,2,1,0:T(8,128)(2,1)}, u32[]{:S(2)}, u32[]{:S(2)}) async-start(bf16[64,1,72,128]{3,2,1,0:T(8,128)(2,1)} %copy-done.36), calls=%async_computation.2 | async-start | bytes 2359296 | tf_op jit(solution)/shard_map/all_to_all | solution.py:244
  126.3 1.5 copy-start.1
  127.8 1.5 copy-start.6
  129.3 1.5 copy-start.11
  130.8 1.5 copy-start.15
  137.8 6.5 %copy-start.21 = (f32[320,1024]{1,0:T(8,128)}, f32[320,1024]{1,0:T(8,128)S(1)}, u32[]{:S(2)}) copy-start(f32[320,1024]{1,0:T(8,128)S(1)} %get-tuple-element.109.act_own.pre_own) | copy-start | bytes 3932164
  137.8 6.5 %copy-start.41 = (bf16[320,1792]{1,0:T(8,128)(2,1)}, bf16[320,1792]{1,0:T(8,128)(2,1)S(1)}, u32[]{:S(2)}) copy-start(bf16[320,1792]{1,0:T(8,128)(2,1)S(1)} %get-tuple-element.127) | copy-start | bytes 3440644
  137.8 9.7 %copy-start.66 = (bf16[2,64,3584]{2,1,0:T(8,128)(2,1)S(1)}, bf16[2,64,3584]{2,1,0:T(8,128)(2,1)}, u32[]{:S(2)}) copy-start(bf16[2,64,3584]{2,1,0:T(8,128)(2,1)} %param.8) | copy-start | bytes 2752516
  137.8 23.2 %collective-permute-start.7 = (bf16[320,1024]{1,0:T(8,128)(2,1)}, bf16[320,1024]{1,0:T(8,128)(2,1)S(1)}, u32[]{:S(2)}, u32[]{:S(2)}) collective-permute-start(bf16[320,1024]{1,0:T(8,128)(2,1)} %get-tuple-element.110), channel_id=1, source_target_pairs={{0,1},{1,0},{2,3},{3,2},{4,5},{5,4},{6,7},{7,6},{8,9},{9,8},{10,11... | collective-permute-start | bytes 1966088 | tf_op jit(solution)/shard_map/ppermute | solution.py:235
  146.3 28.8 %collective-permute-start.6 = (bf16[320,1024]{1,0:T(8,128)(2,1)}, bf16[320,1024]{1,0:T(8,128)(2,1)}, u32[]{:S(2)}, u32[]{:S(2)}) collective-permute-start(bf16[320,1024]{1,0:T(8,128)(2,1)} %get-tuple-element.108), channel_id=1, source_target_pairs={{0,1},{1,0},{2,3},{3,2},{4,5},{5,4},{6,7},{7,6},{8,9},{9,8},{10,11... | collective-permute-start | bytes 1966088 | tf_op jit(solution)/shard_map/ppermute | solution.py:235
  156.0 55.0 %collective-permute-start.8 = (bf16[64,3584]{1,0:T(8,128)(2,1)}, bf16[64,3584]{1,0:T(8,128)(2,1)}, u32[]{:S(2)}, u32[]{:S(2)}) collective-permute-start(bf16[64,3584]{1,0:T(8,128)(2,1)} %shard_map.88), channel_id=1, source_target_pairs={{128,0},{129,1},{130,2},{131,3},{132,4},{133,5},{134,6},{135,7},{1... | collective-permute-start | bytes 1376264 | tf_op jit(solution)/shard_map/ppermute | solution.py:299
  175.2 1.5 copy-start.2
  176.7 1.5 copy-start.7
  180.8 30.1 %copy-start.61 = (bf16[1152,1120]{1,0:T(8,128)(2,1)S(1)}, bf16[1152,1120]{1,0:T(8,128)(2,1)}, u32[]{:S(2)}) copy-start(bf16[1152,1120]{1,0:T(8,128)(2,1)} %fusion.pack_ref.refs_3_) | copy-start | bytes 7741444
  186.3 27.8 %copy-start.49 = (bf16[320,1024]{1,0:T(8,128)(2,1)}, bf16[320,1024]{1,0:T(8,128)(2,1)S(1)}, u32[]{:S(2)}) copy-start(bf16[320,1024]{1,0:T(8,128)(2,1)S(1)} %get-tuple-element.136) | copy-start | bytes 1966084
  186.3 27.8 %copy-start.51 = (bf16[320,1024]{1,0:T(8,128)(2,1)}, bf16[320,1024]{1,0:T(8,128)(2,1)S(1)}, u32[]{:S(2)}) copy-start(bf16[320,1024]{1,0:T(8,128)(2,1)S(1)} %get-tuple-element.140) | copy-start | bytes 1966084
  214.3 35.2 %copy-start.28 = (bf16[64,3584]{1,0:T(8,128)(2,1)S(1)}, bf16[64,3584]{1,0:T(8,128)(2,1)}, u32[]{:S(2)}) copy-start(bf16[64,3584]{1,0:T(8,128)(2,1)} %get-tuple-element.193.incoming) | copy-start | bytes 1376260
  249.5 2.7 copy-start.18
  252.2 26.7 %collective-permute-start.9 = (bf16[64,3584]{1,0:T(8,128)(2,1)}, bf16[64,3584]{1,0:T(8,128)(2,1)}, u32[]{:S(2)}, u32[]{:S(2)}) collective-permute-start(bf16[64,3584]{1,0:T(8,128)(2,1)} %shard_map.93), channel_id=1, source_target_pairs={{128,0},{129,1},{130,2},{131,3},{132,4},{133,5},{134,6},{135,7},{1... | collective-permute-start | bytes 1376264 | tf_op jit(solution)/shard_map/ppermute | solution.py:304
  253.7 1.5 copy-start.12
  258.0 20.9 %copy-start.62 = (bf16[1152,1120]{1,0:T(8,128)(2,1)S(1)}, bf16[1152,1120]{1,0:T(8,128)(2,1)}, u32[]{:S(2)}) copy-start(bf16[1152,1120]{1,0:T(8,128)(2,1)} %fusion.pack_ref.refs_3_) | copy-start | bytes 7741444
  283.1 51.1 %all-to-all-start.4 = ((bf16[64,1,72,128]{3,2,1,0:T(8,128)(2,1)}), bf16[64,1,72,128]{3,2,1,0:T(8,128)(2,1)}, u32[]{:S(2)}, u32[]{:S(2)}) async-start(bf16[64,1,72,128]{3,2,1,0:T(8,128)(2,1)} %copy-done.27), calls=%async_computation.4 | async-start | bytes 2359296 | tf_op jit(solution)/shard_map/all_to_all | solution.py:244
  292.8 27.7 %collective-permute-start.10 = (bf16[320,1024]{1,0:T(8,128)(2,1)}, bf16[320,1024]{1,0:T(8,128)(2,1)S(1)}, u32[]{:S(2)}, u32[]{:S(2)}) collective-permute-start(bf16[320,1024]{1,0:T(8,128)(2,1)} %copy-done.59), channel_id=1, source_target_pairs={{0,1},{1,0},{2,3},{3,2},{4,5},{5,4},{6,7},{7,6},{8,9},{9,8},{10,11... | collective-permute-start | bytes 1966088 | tf_op jit(solution)/shard_map/ppermute | solution.py:235
  320.5 1.5 copy-start.3
  322.0 1.5 copy-start.8
  334.2 1.5 copy-start.13
  335.7 1.5 copy-start.17
  344.3 48.7 %all-to-all-start.5 = ((bf16[64,1,72,128]{3,2,1,0:T(8,128)(2,1)}), bf16[64,1,72,128]{3,2,1,0:T(8,128)(2,1)}, u32[]{:S(2)}, u32[]{:S(2)}) async-start(bf16[64,1,72,128]{3,2,1,0:T(8,128)(2,1)} %copy-done.35), calls=%async_computation.5 | async-start | bytes 2359296 | tf_op jit(solution)/shard_map/all_to_all | solution.py:244
  357.2 2.6 copy-start.40
  357.2 2.6 copy-start.42
  357.2 2.6 copy-start.44
  358.8 28.2 %collective-permute-start.11 = (bf16[320,1024]{1,0:T(8,128)(2,1)}, bf16[320,1024]{1,0:T(8,128)(2,1)S(1)}, u32[]{:S(2)}, u32[]{:S(2)}) collective-permute-start(bf16[320,1024]{1,0:T(8,128)(2,1)} %copy-done.58), channel_id=1, source_target_pairs={{0,1},{1,0},{2,3},{3,2},{4,5},{5,4},{6,7},{7,6},{8,9},{9,8},{10,11... | collective-permute-start | bytes 1966088 | tf_op jit(solution)/shard_map/ppermute | solution.py:235
  361.5 25.5 %copy-start.23 = (f32[320,1024]{1,0:T(8,128)S(1)}, f32[320,1024]{1,0:T(8,128)}, u32[]{:S(2)}) copy-start(f32[320,1024]{1,0:T(8,128)} %copy-done.21) | copy-start | bytes 3932164
  361.5 25.5 %copy-start.31 = (f32[320,1024]{1,0:T(8,128)S(1)}, f32[320,1024]{1,0:T(8,128)}, u32[]{:S(2)}) copy-start(f32[320,1024]{1,0:T(8,128)} %copy-done.30) | copy-start | bytes 3932164
  361.5 25.5 %copy-start.63 = (bf16[1152,1120]{1,0:T(8,128)(2,1)S(1)}, bf16[1152,1120]{1,0:T(8,128)(2,1)}, u32[]{:S(2)}) copy-start(bf16[1152,1120]{1,0:T(8,128)(2,1)} %fusion.pack_ref.refs_3_) | copy-start | bytes 7741444
  363.1 23.9 %copy-start.4 = (bf16[1792,512]{1,0:T(8,128)(2,1)S(1)}, bf16[1792,512]{1,0:T(8,128)(2,1)}, u32[]{:S(2)}) copy-start(bf16[1792,512]{1,0:T(8,128)(2,1)} %copy-done) | copy-start | bytes 5505028
  363.1 23.9 %copy-start.9 = (bf16[1792,512]{1,0:T(8,128)(2,1)S(1)}, bf16[1792,512]{1,0:T(8,128)(2,1)}, u32[]{:S(2)}) copy-start(bf16[1792,512]{1,0:T(8,128)(2,1)} %copy-done.5) | copy-start | bytes 5505028
  393.1 2.0 copy-start.68
  395.1 2.3 copy-start.47
  395.1 2.3 copy-start.50
  395.1 2.3 copy-start.53
  395.1 2.4 copy-start.56
  396.7 4.1 collective-permute-start.14
  397.5 1.6 copy-start.67
  400.7 5.7 %collective-permute-start.12 = (bf16[1792,512]{1,0:T(8,128)(2,1)S(1)}, bf16[1792,512]{1,0:T(8,128)(2,1)S(1)}, u32[]{:S(2)}, u32[]{:S(2)}) collective-permute-start(bf16[1792,512]{1,0:T(8,128)(2,1)S(1)} %convolution_convert_fusion.1), channel_id=1, source_target_pairs={{0,64},{64,0},{1,65},{65,1},{2,66},{66,2},{3,67},{67,3},{4,68},{68... | collective-permute-start | bytes 5505032 | tf_op jit(solution)/shard_map/ppermute | solution.py:235
  403.7 30.1 %collective-permute-start.15 = (bf16[512,1792]{1,0:T(8,128)(2,1)}, bf16[512,1792]{1,0:T(8,128)(2,1)}, u32[]{:S(2)}, u32[]{:S(2)}) collective-permute-start(bf16[512,1792]{1,0:T(8,128)(2,1)} %add_convert_fusion), channel_id=1, source_target_pairs={{1,64},{64,1},{3,66},{66,3},{5,68},{68,5},{7,70},{70,7},{9,72},{72... | collective-permute-start | bytes 5505032 | tf_op jit(solution)/shard_map/ppermute | solution.py:239
  409.3 51.2 %collective-permute-start.13 = (bf16[1792,512]{1,0:T(8,128)(2,1)}, bf16[1792,512]{1,0:T(8,128)(2,1)}, u32[]{:S(2)}, u32[]{:S(2)}) collective-permute-start(bf16[1792,512]{1,0:T(8,128)(2,1)} %add_convert_fusion.1), channel_id=1, source_target_pairs={{1,64},{64,1},{3,66},{66,3},{5,68},{68,5},{7,70},{70,7},{9,72},{72... | collective-permute-start | bytes 5505032 | tf_op jit(solution)/shard_map/ppermute | solution.py:239
  412.3 51.1 %all-to-all-start.6 = ((bf16[64,1,72,128]{3,2,1,0:T(8,128)(2,1)}), bf16[64,1,72,128]{3,2,1,0:T(8,128)(2,1)}, u32[]{:S(2)}, u32[]{:S(2)}) async-start(bf16[64,1,72,128]{3,2,1,0:T(8,128)(2,1)} %copy-done.34), calls=%async_computation.6 | async-start | bytes 2359296 | tf_op jit(solution)/shard_map/all_to_all | solution.py:244
  (26 other events, 27.4 us)
